TPU v7x, 32 devices: a whole 2x2x4 slice. The times are simulated.
32 devices in a mesh: dp: 4 (over y, core), expert: 8 (over z, x).
Axes of the slice: x: 2, y: 2, z: 4, core: 2. Of those that a mesh axis runs over, the one named last changes fastest.
Arguments:
- tokens: bfloat16 [4096, 2048], P(('dp', 'expert')), may hold values from -6 to 6
- attention_gain: bfloat16 [2048], replicated, may hold values from 0.5 to 1.5
- query_weight: bfloat16 [2048, 2048], P(None, 'expert'), may hold values from -0.125 to 0.125
- query_bias: bfloat16 [2048], P('expert'), may hold values from -3 to 3
- key_weight: bfloat16 [2048, 2048], P(None, 'expert'), may hold values from -0.125 to 0.125
- key_bias: bfloat16 [2048], P('expert'), may hold values from -3 to 3
- value_weight: bfloat16 [2048, 2048], P(None, 'expert'), may hold values from -0.125 to 0.125
- value_bias: bfloat16 [2048], P('expert'), may hold values from -3 to 3
- output_weight: bfloat16 [2048, 2048], P(None, 'expert'), may hold values from -0.5 to 0.5
- feedforward_gain: bfloat16 [2048], replicated, may hold values from 0.5 to 1.5
- shared_gate_weight: bfloat16 [2048, 5632], P(None, 'expert'), may hold values from -0.125 to 0.125
- shared_up_weight: bfloat16 [2048, 5632], P(None, 'expert'), may hold values from -0.125 to 0.125
- shared_down_weight: bfloat16 [2048, 5632], P(None, 'expert'), may hold values from -0.078125 to 0.078125
- shared_switch: bfloat16 [2048], replicated, may hold values from -0.125 to 0.125
- router_weight: bfloat16 [2048, 8], replicated, may hold values from -0.0625 to 0.0625
- expert_in: bfloat16 [8, 2048, 2816], P('expert'), may hold values from -0.125 to 0.125
- expert_out: bfloat16 [8, 2048, 1408], P('expert'), may hold values from -1.25 to 1.25
- routes: int32 [4096, 4], P(('dp', 'expert')), may hold values from 0 to 7, all different within a row; in each aligned block of 128 rows (0 to 127, 128 to 255, ...) at most 128 rows name the same one
- cotangent: bfloat16 [4096, 2048], P(('dp', 'expert')), may hold values from -6 to 6
Outputs:
- layer_out: bfloat16 [4096, 2048], P(('dp', 'expert'))
- grad_tokens: float32 [4096, 2048], P(('dp', 'expert'))
- grad_attention_gain: float32 [2048], replicated
- grad_query_weight: float32 [2048, 2048], P('dp', 'expert')
- grad_query_bias: float32 [2048], P('expert')
- grad_key_weight: float32 [2048, 2048], P('dp', 'expert')
- grad_key_bias: float32 [2048], P('expert')
- grad_value_weight: float32 [2048, 2048], P('dp', 'expert')
- grad_value_bias: float32 [2048], P('expert')
- grad_output_weight: float32 [2048, 2048], P('dp', 'expert')
- grad_feedforward_gain: float32 [2048], replicated
- grad_shared_gate_weight: float32 [2048, 5632], P('dp', 'expert')
- grad_shared_up_weight: float32 [2048, 5632], P('dp', 'expert')
- grad_shared_down_weight: float32 [2048, 5632], P('dp', 'expert')
- grad_shared_switch: float32 [2048], replicated
- grad_router_weight: float32 [2048, 8], replicated
- grad_expert_in: float32 [8, 2048, 2816], P('expert', 'dp')
- grad_expert_out: float32 [8, 2048, 1408], P('expert', 'dp')
Inputs may be any that keep to these rules, and one draw needn't show every extreme that they name: `routes`: each token names 4 different experts. Among the rows of one device (aligned blocks of 128 tokens) no expert is named more than 128 times, a bound that some block reaches.
All inputs are finite; a program needn't handle non-finite values.
Results may differ from a plain program's by a relative error of at most 0.03.
Values may be sent and summed in bfloat16 or wider, within the bound.
No kernel may reach another device: no remote copies, remote signals or barrier semaphores. Data moves between devices by JAX's collectives and lax.ppermute only.
A program may use at most 256 MiB of HBM per device.

v0:
```python
import jax
import jax.numpy as jnp
from jax import lax
from jax.sharding import PartitionSpec as P

H = 16
HD = 128
TOP = 4


EPSILON = 1e-06
THETA = 1000000.0
HIGHEST = lax.Precision.HIGHEST


def turn_half(values):
    middle = values.shape[-1] // 2
    return jnp.concatenate([-values[..., middle:], values[..., :middle]], -1)


def rope_tables(length, head_width):
    middle = head_width // 2
    inverse = THETA ** (-(jnp.arange(middle, dtype=jnp.float32) * 2.0 / head_width))
    angles = jnp.arange(length, dtype=jnp.float32)[:, None] * inverse[None, :]
    return (jnp.concatenate([jnp.cos(angles)] * 2, -1), jnp.concatenate([jnp.sin(angles)] * 2, -1))


def rotate(values, cosine_table, sine_table):
    return values * cosine_table[:, None, :] + turn_half(values) * sine_table[:, None, :]


def rotate_back(values, cosine_table, sine_table):
    return values * cosine_table[:, None, :] - turn_half(values) * sine_table[:, None, :]


def rms_scale(values):
    return lax.rsqrt(jnp.mean(values * values, -1, keepdims=True) + EPSILON)


def silu_back(gate_pre, up_pre, grad_hidden):
    sigmoid_gate = jax.nn.sigmoid(gate_pre)
    grad_gate = grad_hidden * up_pre * sigmoid_gate * (1.0 + gate_pre * (1.0 - sigmoid_gate))
    return (grad_gate, grad_hidden * gate_pre * sigmoid_gate)


def right_dot(left_side, right_side):
    return lax.dot_general(
        left_side, right_side, (((1,), (1,)), ((), ())), preferred_element_type=jnp.float32
    )


def left_dot(left_side, right_side):
    return lax.dot_general(
        left_side, right_side, (((0,), (0,)), ((), ())), preferred_element_type=jnp.float32
    )


def merge_lead(values, row_count):
    return values.reshape(-1, row_count, values.shape[-1])


def shards(
    tokens,
    attention_gain,
    query_weight,
    query_bias,
    key_weight,
    key_bias,
    value_weight,
    value_bias,
    output_weight,
    feedforward_gain,
    shared_gate_weight,
    shared_up_weight,
    shared_down_weight,
    shared_switch,
    router_weight,
    expert_in,
    expert_out,
    routes,
    cotangent,
):
    tok_rows, model_width = tokens.shape
    groups = lax.axis_size("expert")
    length = tok_rows * groups
    head_cols = query_weight.shape[1]
    heads_here = head_cols // HD
    shared_cols = shared_gate_weight.shape[1]
    experts = router_weight.shape[1]
    exp_here = expert_in.shape[0]
    ff_width = expert_out.shape[2]
    capacity = 2 * tok_rows * TOP // experts
    block_rows = min(512, length)
    block_count = length // block_rows
    score_scale = HD ** (-0.5)
    cosine_table, sine_table = rope_tables(length, HD)
    x_float = tokens.astype(jnp.float32)
    rms_attn = rms_scale(x_float)
    unit_attn = x_float * rms_attn
    gain_attn = attention_gain.astype(jnp.float32)
    h_attn = (unit_attn * gain_attn).astype(jnp.bfloat16)
    h_attn_all = lax.all_gather(h_attn, "expert", axis=0, tiled=True)

    def project(weight, bias_vec):
        result = jnp.dot(h_attn_all, weight, preferred_element_type=jnp.float32) + bias_vec.astype(
            jnp.float32
        )
        return result.reshape(length, heads_here, HD)

    q_rot = rotate(project(query_weight, query_bias), cosine_table, sine_table).astype(jnp.bfloat16)
    k_rot = rotate(project(key_weight, key_bias), cosine_table, sine_table).astype(jnp.bfloat16)
    v_low = project(value_weight, value_bias).astype(jnp.bfloat16)
    q_blocks = q_rot.reshape(block_count, block_rows, heads_here, HD)
    starts = jnp.arange(block_count, dtype=jnp.int32) * block_rows

    def block_scores(query_block, row_start):
        raw_scores = jnp.einsum(
            "qhd,khd->hqk", query_block, k_rot, preferred_element_type=jnp.float32
        )
        rows_at = row_start + jnp.arange(block_rows, dtype=jnp.int32)
        causal = jnp.arange(length, dtype=jnp.int32)[None, None, :] <= rows_at[None, :, None]
        return (causal, raw_scores * score_scale)

    def forward_block(packed):
        query_block, row_start = packed
        causal, scores = block_scores(query_block, row_start)
        scores = jnp.where(causal, scores, -jnp.inf)
        row_peak = jnp.max(scores, -1, keepdims=True)
        raised = jnp.exp(scores - row_peak)
        row_total = jnp.sum(raised, -1, keepdims=True)
        weights = (raised / row_total).astype(jnp.bfloat16)
        mixed_heads = jnp.einsum("hqk,khd->qhd", weights, v_low, preferred_element_type=jnp.float32)
        return (mixed_heads.astype(jnp.bfloat16), (row_peak + jnp.log(row_total))[..., 0])

    att_blocks, log_totals = lax.map(forward_block, (q_blocks, starts))
    att_low = att_blocks.reshape(length, head_cols)
    attention_own = lax.psum_scatter(
        right_dot(att_low, output_weight), "expert", scatter_dimension=0, tiled=True
    )
    residual = x_float + attention_own
    rms_ffn = rms_scale(residual)
    unit_ffn = residual * rms_ffn
    gain_ffn = feedforward_gain.astype(jnp.float32)
    h_ffn = (unit_ffn * gain_ffn).astype(jnp.bfloat16)
    h_ffn_all = lax.all_gather(h_ffn, "expert", axis=0, tiled=True)
    gate_pre = jnp.dot(h_ffn_all, shared_gate_weight, preferred_element_type=jnp.float32)
    up_pre = jnp.dot(h_ffn_all, shared_up_weight, preferred_element_type=jnp.float32)
    shared_hidden = (jax.nn.silu(gate_pre) * up_pre).astype(jnp.bfloat16)
    shared_own = lax.psum_scatter(
        right_dot(shared_hidden, shared_down_weight).astype(jnp.bfloat16),
        "expert",
        scatter_dimension=0,
        tiled=True,
    ).astype(jnp.float32)
    h_float = h_ffn.astype(jnp.float32)
    switch = jax.nn.sigmoid(jnp.dot(h_ffn, shared_switch, preferred_element_type=jnp.float32))
    logits = jnp.dot(h_ffn, router_weight, preferred_element_type=jnp.float32)
    row_peak = jnp.max(logits, -1, keepdims=True)
    raised = jnp.exp(logits - row_peak)
    router_probs = raised / jnp.sum(raised, -1, keepdims=True)
    picked = routes[:, :, None] == jnp.arange(experts, dtype=jnp.int32)[None, None, :]
    picked_float = picked.astype(jnp.float32)
    gate_probs = jnp.sum(picked_float * router_probs[:, None, :], -1)
    onehot_hits = picked.reshape(tok_rows * TOP, experts).astype(jnp.int32)
    before = jnp.cumsum(onehot_hits, 0) - onehot_hits
    slot_ids = jnp.sum(before * onehot_hits, 1)
    targets = routes.reshape(-1) * capacity + slot_ids
    send_rows = (
        jnp.zeros((experts * capacity, model_width), jnp.bfloat16)
        .at[targets]
        .set(jnp.repeat(h_ffn, TOP, axis=0))
    )
    send_rows = send_rows.reshape(experts, capacity, model_width)

    def expert_pass(arrived):
        row_count = arrived.shape[1]
        grouped = arrived.reshape(-1, exp_here, row_count, model_width)
        joined = jnp.einsum(
            "sjcd,jdf->sjcf", grouped, expert_in, preferred_element_type=jnp.float32
        )
        hidden = (jax.nn.silu(joined[..., :ff_width]) * joined[..., ff_width:]).astype(jnp.bfloat16)
        result = jnp.einsum(
            "sjcf,jdf->sjcd", hidden, expert_out, preferred_element_type=jnp.float32
        ).astype(jnp.bfloat16)
        return (
            arrived,
            merge_lead(joined, row_count),
            merge_lead(hidden, row_count),
            merge_lead(result, row_count),
        )

    def send_to_experts():
        return expert_pass(
            lax.all_to_all(send_rows, "expert", split_axis=0, concat_axis=0, tiled=True)
        )

    recv_rows, recv_joined, recv_hidden, recv_result = send_to_experts()
    returned = lax.all_to_all(
        recv_result, "expert", split_axis=0, concat_axis=0, tiled=True
    ).reshape(experts * capacity, model_width)
    expert_rows = returned[targets].reshape(tok_rows, TOP, model_width).astype(jnp.float32)
    routed = jnp.sum(gate_probs[:, :, None] * expert_rows, 1)
    layer_out = (residual + switch[:, None] * shared_own + routed).astype(jnp.bfloat16)
    grad_out = cotangent.astype(jnp.float32)
    grad_gates = jnp.sum(grad_out[:, None, :] * expert_rows, -1)
    grad_probs = jnp.sum(picked_float * grad_gates[:, :, None], 1)
    grad_logits = router_probs * (
        grad_probs - jnp.sum(router_probs * grad_probs, -1, keepdims=True)
    )
    grad_ffn = jnp.dot(grad_logits, router_weight.astype(jnp.float32).T, precision=HIGHEST)
    grad_router_part = jnp.dot(h_float.T, grad_logits, precision=HIGHEST)
    grad_switch = jnp.sum(grad_out * shared_own, -1) * switch * (1.0 - switch)
    grad_ffn = grad_ffn + grad_switch[:, None] * shared_switch.astype(jnp.float32)
    grad_switch_part = jnp.dot(grad_switch, h_float, precision=HIGHEST)
    grad_copies = (gate_probs[:, :, None] * grad_out[:, None, :]).astype(jnp.bfloat16)
    grad_send = (
        jnp.zeros((experts * capacity, model_width), jnp.bfloat16)
        .at[targets]
        .set(grad_copies.reshape(-1, model_width))
    )
    grad_send = grad_send.reshape(experts, capacity, model_width)
    recv_rows, recv_joined, recv_hidden, unused_rows = send_to_experts()
    grad_recv = lax.all_to_all(grad_send, "expert", split_axis=0, concat_axis=0, tiled=True)
    grad_grouped = grad_recv.reshape(-1, exp_here, capacity, model_width)
    joined_grouped = recv_joined.reshape(-1, exp_here, capacity, 2 * ff_width)
    grad_hidden = jnp.einsum(
        "sjcd,jdf->sjcf", grad_grouped, expert_out, preferred_element_type=jnp.float32
    )
    grad_gate_e, grad_up_e = silu_back(
        joined_grouped[..., :ff_width], joined_grouped[..., ff_width:], grad_hidden
    )
    grad_joined = jnp.concatenate([grad_gate_e, grad_up_e], -1).astype(jnp.bfloat16)
    grad_rows = jnp.einsum(
        "sjcf,jdf->sjcd", grad_joined, expert_in, preferred_element_type=jnp.float32
    ).astype(jnp.bfloat16)
    grad_rows = merge_lead(grad_rows, capacity)
    grad_back = lax.all_to_all(
        grad_rows, "expert", split_axis=0, concat_axis=0, tiled=True
    ).reshape(experts * capacity, model_width)
    grad_ffn = grad_ffn + jnp.sum(
        grad_back[targets].reshape(tok_rows, TOP, model_width).astype(jnp.float32), 1
    )
    shared_grad = (switch[:, None] * grad_out).astype(jnp.bfloat16)
    shared_grad_all = lax.all_gather(shared_grad, "expert", axis=0, tiled=True)
    grad_shared_hidden = jnp.dot(
        shared_grad_all, shared_down_weight, preferred_element_type=jnp.float32
    )
    grad_gate_s, grad_up_s = silu_back(gate_pre, up_pre, grad_shared_hidden)
    grad_gate_s = grad_gate_s.astype(jnp.bfloat16)
    grad_up_s = grad_up_s.astype(jnp.bfloat16)
    grad_ffn = grad_ffn + lax.psum_scatter(
        (
            right_dot(grad_gate_s, shared_gate_weight) + right_dot(grad_up_s, shared_up_weight)
        ).astype(jnp.bfloat16),
        "expert",
        scatter_dimension=0,
        tiled=True,
    ).astype(jnp.float32)
    grad_ffn_gain_part = jnp.sum(grad_ffn * unit_ffn, 0)
    grad_unit_ffn = grad_ffn * gain_ffn
    grad_residual = grad_out + rms_ffn * (
        grad_unit_ffn - unit_ffn * jnp.mean(grad_unit_ffn * unit_ffn, -1, keepdims=True)
    )
    attention_grad = grad_residual.astype(jnp.bfloat16)
    attention_grad_all = lax.all_gather(attention_grad, "expert", axis=0, tiled=True)
    grad_att = jnp.dot(
        attention_grad_all, output_weight, preferred_element_type=jnp.float32
    ).astype(jnp.bfloat16)
    grad_att_blocks = grad_att.reshape(block_count, block_rows, heads_here, HD)

    def backward_block(carry, packed):
        key_acc, value_acc = carry
        query_block, row_start, grad_block, log_block = packed
        causal, scores = block_scores(query_block, row_start)
        probs = jnp.where(causal, jnp.exp(scores - log_block[..., None]), 0.0)
        low_probs = probs.astype(jnp.bfloat16)
        value_acc = value_acc + jnp.einsum(
            "hqk,qhd->khd", low_probs, grad_block, preferred_element_type=jnp.float32
        )
        grad_weights = jnp.einsum(
            "qhd,khd->hqk", grad_block, v_low, preferred_element_type=jnp.float32
        )
        grad_scores = probs * (grad_weights - jnp.sum(probs * grad_weights, -1, keepdims=True))
        grad_raw = (grad_scores * score_scale).astype(jnp.bfloat16)
        query_grad = jnp.einsum("hqk,khd->qhd", grad_raw, k_rot, preferred_element_type=jnp.float32)
        key_acc = key_acc + jnp.einsum(
            "hqk,qhd->khd", grad_raw, query_block, preferred_element_type=jnp.float32
        )
        return ((key_acc, value_acc), query_grad)

    zeros_heads = jnp.zeros((length, heads_here, HD), jnp.float32)
    (key_acc, value_acc), query_grads = lax.scan(
        backward_block, (zeros_heads, zeros_heads), (q_blocks, starts, grad_att_blocks, log_totals)
    )
    grad_query = (
        rotate_back(query_grads.reshape(length, heads_here, HD), cosine_table, sine_table)
        .reshape(length, head_cols)
        .astype(jnp.bfloat16)
    )
    grad_key = (
        rotate_back(key_acc, cosine_table, sine_table)
        .reshape(length, head_cols)
        .astype(jnp.bfloat16)
    )
    grad_value = value_acc.reshape(length, head_cols).astype(jnp.bfloat16)
    grad_attn_in = lax.psum_scatter(
        (
            right_dot(grad_query, query_weight)
            + right_dot(grad_key, key_weight)
            + right_dot(grad_value, value_weight)
        ).astype(jnp.bfloat16),
        "expert",
        scatter_dimension=0,
        tiled=True,
    ).astype(jnp.float32)
    grad_attn_gain_part = jnp.sum(grad_attn_in * unit_attn, 0)
    grad_unit_attn = grad_attn_in * gain_attn
    grad_tokens = grad_residual + rms_attn * (
        grad_unit_attn - unit_attn * jnp.mean(grad_unit_attn * unit_attn, -1, keepdims=True)
    )
    rows_grouped = recv_rows.reshape(-1, exp_here, capacity, model_width)
    hidden_grouped = recv_hidden.reshape(-1, exp_here, capacity, ff_width)
    rows_here = model_width // lax.axis_size("dp")
    expert_in_part = jnp.einsum(
        "sjcd,sjcf->djf", rows_grouped, grad_joined, preferred_element_type=jnp.float32
    )
    expert_out_part = jnp.einsum(
        "sjcd,sjcf->djf", grad_grouped, hidden_grouped, preferred_element_type=jnp.float32
    )
    summed = lax.psum_scatter(
        jnp.concatenate(
            [
                left_dot(h_attn_all, grad_query),
                left_dot(h_attn_all, grad_key),
                left_dot(h_attn_all, grad_value),
                left_dot(attention_grad_all, att_low),
                left_dot(h_ffn_all, grad_gate_s),
                left_dot(h_ffn_all, grad_up_s),
                left_dot(shared_grad_all, shared_hidden),
                expert_in_part.reshape(rows_here * lax.axis_size("dp"), -1),
                expert_out_part.reshape(rows_here * lax.axis_size("dp"), -1),
            ],
            1,
        ).astype(jnp.bfloat16),
        "dp",
        scatter_dimension=0,
        tiled=True,
    ).astype(jnp.float32)
    offset = 0
    grad_query_weight = summed[:, offset : offset + head_cols]
    offset = offset + head_cols
    grad_key_weight = summed[:, offset : offset + head_cols]
    offset = offset + head_cols
    grad_value_weight = summed[:, offset : offset + head_cols]
    offset = offset + head_cols
    grad_output_weight = summed[:, offset : offset + head_cols]
    offset = offset + head_cols
    grad_shared_gate_weight = summed[:, offset : offset + shared_cols]
    offset = offset + shared_cols
    grad_shared_up_weight = summed[:, offset : offset + shared_cols]
    offset = offset + shared_cols
    grad_shared_down_weight = summed[:, offset : offset + shared_cols]
    offset = offset + shared_cols
    grad_expert_in = (
        summed[:, offset : offset + exp_here * 2 * ff_width]
        .reshape(rows_here, exp_here, 2 * ff_width)
        .transpose(1, 0, 2)
    )
    offset = offset + exp_here * 2 * ff_width
    grad_expert_out = (
        summed[:, offset : offset + exp_here * ff_width]
        .reshape(rows_here, exp_here, ff_width)
        .transpose(1, 0, 2)
    )
    bias_parts = jnp.stack(
        [
            jnp.sum(grad_query.astype(jnp.float32), 0),
            jnp.sum(grad_key.astype(jnp.float32), 0),
            jnp.sum(grad_value.astype(jnp.float32), 0),
        ]
    )
    position = lax.axis_index("expert") * head_cols
    bias_full = lax.dynamic_update_slice(
        jnp.zeros((3, H * HD), jnp.float32), bias_parts, (0, position)
    )
    (
        grad_attention_gain,
        grad_feedforward_gain,
        grad_shared_switch,
        grad_router_weight,
        bias_sums,
    ) = lax.psum(
        (grad_attn_gain_part, grad_ffn_gain_part, grad_switch_part, grad_router_part, bias_full),
        ("dp", "expert"),
    )
    bias_here = lax.dynamic_slice_in_dim(bias_sums, position, head_cols, 1)
    return (
        layer_out,
        grad_tokens,
        grad_attention_gain,
        grad_query_weight,
        bias_here[0],
        grad_key_weight,
        bias_here[1],
        grad_value_weight,
        bias_here[2],
        grad_output_weight,
        grad_feedforward_gain,
        grad_shared_gate_weight,
        grad_shared_up_weight,
        grad_shared_down_weight,
        grad_shared_switch,
        grad_router_weight,
        grad_expert_in,
        grad_expert_out,
    )


def solution(mesh):
    return jax.shard_map(
        shards,
        mesh=mesh,
        in_specs=(
            P(("dp", "expert"), None),
            P(),
            P(None, "expert"),
            P("expert"),
            P(None, "expert"),
            P("expert"),
            P(None, "expert"),
            P("expert"),
            P(None, "expert"),
            P(),
            P(None, "expert"),
            P(None, "expert"),
            P(None, "expert"),
            P(),
            P(),
            P("expert", None, None),
            P("expert", None, None),
            P(("dp", "expert"), None),
            P(("dp", "expert"), None),
        ),
        out_specs=(
            P(("dp", "expert"), None),
            P(("dp", "expert"), None),
            P(),
            P("dp", "expert"),
            P("expert"),
            P("dp", "expert"),
            P("expert"),
            P("dp", "expert"),
            P("expert"),
            P("dp", "expert"),
            P(),
            P("dp", "expert"),
            P("dp", "expert"),
            P("dp", "expert"),
            P(),
            P(),
            P("expert", "dp", None),
            P("expert", "dp", None),
        ),
        check_vma=False,
    )
```

profile of v0, /device:TPU:0, one launch (start us, length us, event | category | flops | bytes accessed | tf_op | source)
XLA Modules:
  0.0 1534.1 jit_solution(7515973256167623721)
XLA Ops:
  20.6 67.7 %all-gather.5.cloned.1.call-done = bf16[1024,2048]{1,0:T(8,128)(2,1)} async-done(((bf16[128,2048]{1,0:T(8,128)(2,1)}), bf16[1024,2048]{1,0:T(8,128)(2,1)}) %all-gather.5.cloned.1.call-update) | async-done | bytes 4194320 | tf_op jit(solution)/shard_map/all_gather | solution.py:102
  128.1 15.4 %while.27 = (s32[]{:T(128)}, bf16[2,512,2,128]{3,2,1,0:T(2,128)(2,1)}, f32[2,2,512]{2,1,0:T(2,128)S(1)}, s32[2]{0:T(128)S(1)}, bf16[2,512,2,128]{3,1,2,0:T(8,128...) while((s32[]{:T(128)}, bf16[2,512,2,128]{3,2,1,0:T(2,128)(2,1)}, ...), condition=%wide.region_4.5_spmd, body=%wide.region_1.4_spmd.sunk | while | flops 550108672 | bytes 21008560 | solution.py:135
  150.4 146.8 %reduce-scatter.6.cloned.1.call-done = f32[128,2048]{1,0:T(8,128)} async-done(((f32[1024,2048]{1,0:T(8,128)}), f32[128,2048]{1,0:T(8,128)}) %reduce-scatter.6.cloned.1.call-update) | async-done | bytes 1048592 | tf_op jit(solution)/shard_map/reduce_scatter | solution.py:137
  334.7 8.1 scatter_custom_fusion.1
  342.8 109.8 %all-to-all-done = bf16[8,128,2048]{2,1,0:T(8,128)(2,1)} async-done(((bf16[8,128,2048]{2,1,0:T(8,128)(2,1)}), bf16[8,128,2048]{2,1,0:T(8,128)(2,1)}, u32[]{:S(2)}, u32[]{:S(2)}) %all-to-all-start) | async-done | bytes 4194336 | tf_op jit(solution)/shard_map/all_to_all | solution.py:194
  470.0 123.8 %all-gather.9.cloned.1.call-done = bf16[1024,2048]{1,0:T(8,128)(2,1)} async-done(((bf16[128,2048]{1,0:T(8,128)(2,1)}), bf16[1024,2048]{1,0:T(8,128)(2,1)}) %all-gather.9.cloned.1.call-update) | async-done | bytes 4194320 | tf_op jit(solution)/shard_map/all_gather | solution.py:244
  593.8 8.9 multiply_convert_fusion.3
  608.9 18.8 %fusion.60 = f32[8,1,128,2816]{3,2,0,1:T(8,128)} fusion(bf16[8,128,2048]{2,1,0:T(8,128)(2,1)} %all-to-all-done, bf16[1,2048,2816]{2,1,0:T(8,128)(2,1)} %param.38), kind=kOutput, calls=%fused_computation.66 | convolution fusion | flops 11811160064 | bytes 27262976 | tf_op jit(solution)/shard_map/sjcd,jdf->sjcf/dot_general | solution.py:178
  627.7 15.0 fusion.84
  645.2 16.5 %fusion.75 = bf16[8,128,2048]{2,1,0:T(8,128)(2,1)} fusion(bf16[1,2048,2816]{2,1,0:T(8,128)(2,1)} %param.38, bf16[8,128,1408]{2,1,0:T(8,128)(2,1)S(1)} %get-tuple-element.448, bf16[8,128,1408]{2,1,0:T(8,128)(2,1)S(1)} %get-tuple-element.447), kind=kOutput, calls=%fused_computation.87 | convolution fusion | flops 11824791552 | bytes 21495808 | tf_op jit(solution)/shard_map/sjcf,jdf->sjcd/dot_general | solution.py:233
  673.9 11.0 fusion.72
  684.9 92.3 %all-to-all-done.3 = bf16[8,128,2048]{2,1,0:T(8,128)(2,1)} async-done(((bf16[8,128,2048]{2,1,0:T(8,128)(2,1)}), bf16[8,128,2048]{2,1,0:T(8,128)(2,1)}, u32[]{:S(2)}, u32[]{:S(2)}) %all-to-all-start.3) | async-done | bytes 4194336 | tf_op jit(solution)/shard_map/all_to_all | solution.py:237
  790.7 8.4 gather_fusion.1
  803.8 104.7 %all-to-all-done.1 = bf16[8,128,2048]{2,1,0:T(8,128)(2,1)} async-done(((bf16[8,128,2048]{2,1,0:T(8,128)(2,1)}), bf16[8,128,2048]{2,1,0:T(8,128)(2,1)}, u32[]{:S(2)}, u32[]{:S(2)}) %all-to-all-start.1) | async-done | bytes 4194336 | tf_op jit(solution)/shard_map/all_to_all | solution.py:198
  945.3 73.0 %all-gather.11.cloned.1.call-done = bf16[1024,2048]{1,0:T(8,128)(2,1)} async-done(((bf16[128,2048]{1,0:T(8,128)(2,1)}), bf16[1024,2048]{1,0:T(8,128)(2,1)}) %all-gather.11.cloned.1.call-update) | async-done | bytes 4194320 | tf_op jit(solution)/shard_map/all_gather | solution.py:265
  1024.8 52.5 %while.28 = (s32[]{:T(128)}, f32[1024,2,128]{0,2,1:T(8,128)}, f32[1024,2,128]{0,2,1:T(8,128)S(1)}, f32[2,512,2,128]{3,1,2,0:T(8,128)}, bf16[2,512,2,128]{3,1,2,0...) while((s32[]{:T(128)}, f32[1024,2,128]{0,2,1:T(8,128)}, ...), condition=%wide.region_26.27_spmd.clone, body=%wide.region_24.26_spmd.clone.sunk | while | flops 1358434816 | bytes 71844040 | solution.py:292
  1061.1 8.4 fusion.243
  1125.8 17.4 %bitcast_dynamic-update-slice_fusion.1 = bf16[2048,7360]{0,1:T(8,128)(2,1)} fusion(bf16[2048,7360]{0,1:T(8,128)(2,1)} %fusion.78, bf16[8,128,2048]{2,1,0:T(8,128)(2,1)} %all-to-all-done, bf16[8,128,1408]{2,1,0:T(8,128)(2,1)S(1)} %copy-done.71, bf16[8,128,1408]{2,1,0:T(8,128)(2,1)S(1)} %copy-done.69), kind=kOutput, calls=%fused_computation.56 | convolution fusion | flops 11828461568 | bytes 21495808 | tf_op jit(solution)/shard_map/sjcd,sjcf->djf/dot_general | solution.py:324
  1143.2 9.8 fusion.59
  1157.3 28.3 %reduce-scatter.12.cloned.1.call-done = bf16[128,2048]{1,0:T(8,128)(2,1)} async-done(((bf16[1024,2048]{1,0:T(8,128)(2,1)}), bf16[128,2048]{1,0:T(8,128)(2,1)}) %reduce-scatter.12.cloned.1.call-update) | async-done | bytes 524304 | tf_op jit(solution)/shard_map/reduce_scatter | solution.py:306
  1187.1 41.6 %all-reduce = (f32[2048]{0:T(1024)}, f32[3,2048]{1,0:T(4,128)S(1)}, f32[2048]{0:T(1024)}, f32[2048]{0:T(1024)}) all-reduce(f32[2048]{0:T(1024)S(1)} %get-tuple-element.397, f32[3,2048]{1,0:T(4,128)S(1)} %maximum_dynamic-update-slice_fusion, f32[2048]{0:T(1024)S(1)} %get-tuple-element.395, ...), channel_id=1, replica_groups=mesh['dp'=4,'expert'=8] {'dp','expert'}, use_global_device_ids=true, to_apply=%region_30.31 | all-reduce | flops 12288 | bytes 98304 | tf_op jit(solution)/shard_map/psum | solution.py:392
  1232.8 168.2 %reduce-scatter.14.cloned.1.call-done = bf16[512,7360]{0,1:T(8,128)(2,1)} async-done(((bf16[2048,7360]{0,1:T(8,128)(2,1)}), bf16[512,7360]{0,1:T(8,128)(2,1)}) %reduce-scatter.14.cloned.1.call-update) | async-done | bytes 7536656 | tf_op jit(solution)/shard_map/reduce_scatter | solution.py:330
  1401.0 10.6 convert_element_type.226
  1437.7 87.9 %all-reduce.3.cloned.1.call-done = f32[2048,8]{0,1:T(8,128)} async-done(((f32[2048,8]{0,1:T(8,128)}), f32[2048,8]{0,1:T(8,128)}) %all-reduce.3.cloned.1.call-update) | async-done | bytes 65552 | tf_op jit(solution)/shard_map/psum | solution.py:392
  (347 shorter events, 341.9 us)
Async XLA Ops:
  7.2 586.6 %copy-start = (bf16[2048,704]{0,1:T(8,128)(2,1)S(1)}, bf16[2048,704]{0,1:T(8,128)(2,1)}, u32[]{:S(2)}) copy-start(bf16[2048,704]{0,1:T(8,128)(2,1)} %param.35) | copy-start | bytes 8650756
  7.2 81.0 %all-gather.5.cloned.1.call-start = ((), (), s32[]{:S(2)}) async-start(), calls=%async_computation.9 | async-start | bytes 4718592 | tf_op jit(solution)/shard_map/all_gather | solution.py:102
  12.0 285.2 %reduce-scatter.6.cloned.1.call-start = ((), (), s32[]{:S(2)}) async-start(), calls=%async_computation.10 | async-start | bytes 9437184 | tf_op jit(solution)/shard_map/reduce_scatter | solution.py:137
  149.7 147.5 %copy-start.14 = (bf16[128,2048]{1,0:T(8,128)(2,1)S(1)}, bf16[128,2048]{1,0:T(8,128)(2,1)}, u32[]{:S(2)}) copy-start(bf16[128,2048]{1,0:T(8,128)(2,1)} %param.23) | copy-start | bytes 1572868
  149.7 150.8 %copy-start.43 = (s32[128,4]{0,1:T(4,128)S(1)}, s32[128,4]{0,1:T(4,128)}, u32[]{:S(2)}) copy-start(s32[128,4]{0,1:T(4,128)} %param.40) | copy-start | bytes 6148
  149.7 307.5 %all-gather.7.cloned.1.call-start = ((), (), s32[]{:S(2)}) async-start(), calls=%async_computation.11 | async-start | bytes 4718592 | tf_op jit(solution)/shard_map/all_gather | solution.py:145
  150.3 159.9 %copy-start.36 = (f32[2048]{0:T(1024)}, f32[2048]{0:T(1024)S(1)}, u32[]{:S(2)}) copy-start(f32[2048]{0:T(1024)S(1)} %convert_element_type.194) | copy-start | bytes 24580
  317.6 135.0 %all-to-all-start = ((bf16[8,128,2048]{2,1,0:T(8,128)(2,1)}), bf16[8,128,2048]{2,1,0:T(8,128)(2,1)}, u32[]{:S(2)}, u32[]{:S(2)}) async-start(bf16[8,128,2048]{2,1,0:T(8,128)(2,1)} %bitcast.288), calls=%async_computation.2 | async-start | bytes 8388608 | tf_op jit(solution)/shard_map/all_to_all | solution.py:194
  322.3 271.5 %all-gather.9.cloned.1.call-start = ((), (), s32[]{:S(2)}) async-start(), calls=%async_computation.13 | async-start | bytes 4718592 | tf_op jit(solution)/shard_map/all_gather | solution.py:244
  452.6 175.1 %all-to-all-start.2 = ((bf16[8,128,2048]{2,1,0:T(8,128)(2,1)}), bf16[8,128,2048]{2,1,0:T(8,128)(2,1)}, u32[]{:S(2)}, u32[]{:S(2)}) async-start(bf16[8,128,2048]{2,1,0:T(8,128)(2,1)} %bitcast.287), calls=%async_computation.4 | async-start | bytes 8388608 | tf_op jit(solution)/shard_map/all_to_all | solution.py:223
  457.2 477.0 %reduce-scatter.8.cloned.1.call-start = ((), (), s32[]{:S(2)}) async-start(), calls=%async_computation.12 | async-start | bytes 4718592 | tf_op jit(solution)/shard_map/reduce_scatter | solution.py:149
  661.7 115.5 %all-to-all-start.3 = ((bf16[8,128,2048]{2,1,0:T(8,128)(2,1)}), bf16[8,128,2048]{2,1,0:T(8,128)(2,1)}, u32[]{:S(2)}, u32[]{:S(2)}) async-start(bf16[8,128,2048]{2,1,0:T(8,128)(2,1)} %fusion.75), calls=%async_computation.5 | async-start | bytes 8388608 | tf_op jit(solution)/shard_map/all_to_all | solution.py:237
  684.9 96.9 %copy-start.59 = (bf16[2048,704]{0,1:T(8,128)(2,1)S(1)}, bf16[2048,704]{0,1:T(8,128)(2,1)}, u32[]{:S(2)}) copy-start(bf16[2048,704]{0,1:T(8,128)(2,1)} %param.34) | copy-start | bytes 8650756
  777.2 131.3 %all-to-all-start.1 = ((bf16[8,128,2048]{2,1,0:T(8,128)(2,1)}), bf16[8,128,2048]{2,1,0:T(8,128)(2,1)}, u32[]{:S(2)}, u32[]{:S(2)}) async-start(bf16[8,128,2048]{2,1,0:T(8,128)(2,1)} %fusion.72), calls=%async_computation.3 | async-start | bytes 8388608 | tf_op jit(solution)/shard_map/all_to_all | solution.py:198
  781.8 159.5 %reduce-scatter.10.cloned.1.call-start = ((), (), s32[]{:S(2)}) async-start(), calls=%async_computation.14 | async-start | bytes 4718592 | tf_op jit(solution)/shard_map/reduce_scatter | solution.py:251
  789.6 228.7 %all-gather.11.cloned.1.call-start = ((), (), s32[]{:S(2)}) async-start(), calls=%async_computation.15 | async-start | bytes 4718592 | tf_op jit(solution)/shard_map/all_gather | solution.py:265
  945.0 240.6 %reduce-scatter.12.cloned.1.call-start = ((), (), s32[]{:S(2)}) async-start(), calls=%async_computation.16 | async-start | bytes 4718592 | tf_op jit(solution)/shard_map/reduce_scatter | solution.py:306
  945.2 79.6 %copy-start.8 = (bf16[1024,2,128]{2,0,1:T(8,128)(2,1)S(1)}, bf16[1024,2,128]{2,0,1:T(8,128)(2,1)}, u32[]{:S(2)}) copy-start(bf16[1024,2,128]{2,0,1:T(8,128)(2,1)} %copy-done.7) | copy-start | bytes 1572868
  945.2 79.5 %copy-start.9 = (bf16[1024,2,128]{2,0,1:T(8,128)(2,1)S(1)}, bf16[1024,2,128]{2,0,1:T(8,128)(2,1)}, u32[]{:S(2)}) copy-start(bf16[1024,2,128]{2,0,1:T(8,128)(2,1)} %get-tuple-element.688) | copy-start | bytes 1572868
  945.2 79.5 %copy-start.42 = (f32[2,2,512]{2,1,0:T(2,128)S(1)}, f32[2,2,512]{2,1,0:T(2,128)}, u32[]{:S(2)}) copy-start(f32[2,2,512]{2,1,0:T(2,128)} %copy-done.41) | copy-start | bytes 24580
  945.3 79.5 %copy-start.61 = (s32[2]{0:T(128)S(1)}, s32[2]{0:T(128)}, u32[]{:S(2)}) copy-start(s32[2]{0:T(128)} %copy-done.60) | copy-start | bytes 28
  1099.2 301.8 %reduce-scatter.14.cloned.1.call-start = ((), (), s32[]{:S(2)}) async-start(), calls=%async_computation.17 | async-start | bytes 37683200 | tf_op jit(solution)/shard_map/reduce_scatter | solution.py:330
  1153.1 372.5 %all-reduce.3.cloned.1.call-start = ((), (), s32[]{:S(2)}) async-start(), calls=%async_computation.18 | async-start | bytes 131072 | tf_op jit(solution)/shard_map/psum | solution.py:392
  1427.9 99.2 %copy-start.1 = (bf16[2048,704]{0,1:T(8,128)(2,1)S(1)}, bf16[2048,704]{0,1:T(8,128)(2,1)}, u32[]{:S(2)}) copy-start(bf16[2048,704]{0,1:T(8,128)(2,1)} %param.35) | copy-start | bytes 8650756
  (67 other events, 500.9 us)
Sparse Core Ops, SparseCore 0:
  12.1 76.0 all-gather.4
  149.8 147.2 reduce-scatter.5
  300.7 144.5 all-gather.6
  448.0 145.7 all-gather.8
  609.1 107.0 reduce-scatter.7
  789.7 151.6 reduce-scatter.9
  945.1 73.1 all-gather.10
  1099.3 86.1 reduce-scatter.11
  1188.2 212.7 reduce-scatter.13
  1407.9 117.5 all-reduce.2
where the time goes:
time: 1550 us; the launch traced here: 1530 us
  waiting for transfers between devices  1010 us (65%)
  matrix products  242 us (16%)
  local copies, waits for them, and re-layouts  129 us (8%)
  other arithmetic  77.9 us (5%)
  blocking collectives  41.6 us (3%)
  starting transfers between devices  19.3 us (1%)
    reduce_scatter x1, waiting for transfers between devices, shards(): lax.psum_scatter(jnp.concatenate([left_dot(h_attn_all, grad_query), left_...  168 us
    reduce_scatter x1, waiting for transfers between devices, shards(): lax.psum_scatter(right_dot(att_low, output_weight), 'expert', scatter_dim...  147 us
    all_gather x1, waiting for transfers between devices, shards(): shared_grad_all = lax.all_gather(shared_grad, 'expert', axis=0, tiled=True)  124 us
    all_to_all x1, waiting for transfers between devices, send_to_experts(): lax.all_to_all(send_rows, 'expert', split_axis=0, concat_axis=0, tiled=True)  110 us
    all_to_all x1, waiting for transfers between devices, shards(): lax.all_to_all(recv_result, 'expert', split_axis=0, concat_axis=0, tiled=...  105 us
    all_to_all x1, waiting for transfers between devices, shards(): lax.all_to_all(grad_rows, 'expert', split_axis=0, concat_axis=0, tiled=True)  92.3 us
    psum x1, waiting for transfers between devices, shards(): lax.psum((grad_attn_gain_part, grad_ffn_gain_part, grad_switch_part, grad...  87.9 us
    all_gather x1, waiting for transfers between devices, shards(): lax.all_gather(attention_grad, 'expert', axis=0, tiled=True)  73 us
  transfers between devices with their start and end apart: 14, of which 11 were waited for; matrix products, arithmetic and copies ran while one was open for 19% of the time, Pallas kernels for 0%

commit v1 on v0

v1 whole, which is shorter than its diff:
```python
import functools

import jax
import jax.numpy as jnp
from jax import lax
from jax.experimental import pallas as pl
from jax.experimental.pallas import tpu as pltpu
from jax.sharding import PartitionSpec as P

HD = 128
EPSILON = 1e-06
THETA = 1000000.0
HIGHEST = lax.Precision.HIGHEST
BF = jnp.bfloat16
F32 = jnp.float32


def rope_tables(length):
    middle = HD // 2
    inverse = THETA ** (-(jnp.arange(middle, dtype=F32) * 2.0 / HD))
    angles = jnp.arange(length, dtype=F32)[:, None] * inverse[None, :]
    sine = jnp.sin(angles)
    return (jnp.concatenate([jnp.cos(angles)] * 2, -1), jnp.concatenate([-sine, sine], -1))


def rms_scale(values):
    return lax.rsqrt(jnp.mean(values * values, -1, keepdims=True) + EPSILON)


def plain_dot(left_side, right_side):
    return jnp.dot(left_side, right_side, preferred_element_type=F32)


def right_dot(left_side, right_side):
    return lax.dot_general(
        left_side, right_side, (((1,), (1,)), ((), ())), preferred_element_type=F32
    )


def left_dot(left_side, right_side):
    return lax.dot_general(
        left_side, right_side, (((0,), (0,)), ((), ())), preferred_element_type=F32
    )


def ring_order(count):
    wide = 2 if count <= 8 else 4
    tall = count // wide
    order = [z * wide for z in range(tall)]
    for z in range(tall - 1, -1, -1):
        row = list(range(1, wide))
        if (tall - 1 - z) % 2:
            row = row[::-1]
        order += [z * wide + x for x in row]
    return order


class Ring:
    def __init__(self, count):
        self.count = count
        self.half = count // 2
        order = ring_order(count)
        self.forward = [(order[i], order[(i + 1) % count]) for i in range(count)]
        self.backward = [(order[i], order[(i - 1) % count]) for i in range(count)]
        place = [0] * count
        for at, device in enumerate(order):
            place[device] = at
        distances = [0]
        for step in range(1, self.half):
            distances += [-step, step]
        distances.append(self.half)
        here = jnp.array(place, jnp.int32)[lax.axis_index("expert")]
        around = (here + jnp.array(distances, jnp.int32) + count) % count
        self.block_of_slot = jnp.array(order, jnp.int32)[around]
        hits = self.block_of_slot[None, :] == jnp.arange(count, dtype=jnp.int32)[:, None]
        self.slot_of_block = jnp.sum(hits * jnp.arange(count, dtype=jnp.int32)[None, :], 1)

    def slot(self, distance):
        if distance == self.half:
            return self.count - 1
        return 2 * abs(distance) - (distance < 0)

    def gather(self, block):
        middle = block.shape[0] // 2
        pieces = [block]
        ahead = behind = block
        for step in range(1, self.half):
            ahead = lax.ppermute(ahead, "expert", self.forward)
            behind = lax.ppermute(behind, "expert", self.backward)
            pieces += [ahead, behind]
        pieces.append(lax.ppermute(ahead[:middle], "expert", self.forward))
        pieces.append(lax.ppermute(behind[middle:], "expert", self.backward))
        return jnp.concatenate(pieces, 0)

    def scatter_sum(self, partial, held=BF):
        rows = partial.shape[0] // self.count
        middle = rows // 2

        def own(distance):
            start = self.slot(distance) * rows
            return partial[start : start + rows]

        far = own(self.half).astype(held)
        ahead = lax.ppermute(far[:middle], "expert", self.forward)
        behind = lax.ppermute(far[middle:], "expert", self.backward)
        for step in range(self.half - 1, 0, -1):
            up = own(step).astype(F32)
            down = own(-step).astype(F32)
            if step == self.half - 1:
                up = jnp.concatenate([up[:middle] + ahead.astype(F32), up[middle:]], 0)
                down = jnp.concatenate([down[:middle], down[middle:] + behind.astype(F32)], 0)
            else:
                up = up + ahead.astype(F32)
                down = down + behind.astype(F32)
            ahead = lax.ppermute(up.astype(held), "expert", self.forward)
            behind = lax.ppermute(down.astype(held), "expert", self.backward)
        return own(0).astype(F32) + ahead.astype(F32) + behind.astype(F32)


def cube_sum(values, axis):
    count = lax.axis_size(axis)
    step = 1
    while step < count:
        values = values + lax.ppermute(values, axis, [(i, i ^ step) for i in range(count)])
        step *= 2
    return values


def split_cores(values):
    count = lax.axis_size("dp")
    core = lax.axis_index("dp") % 2
    columns = values.shape[1] // count
    even = [values[:, i * columns : (i + 1) * columns] for i in range(0, count, 2)]
    odd = [values[:, i * columns : (i + 1) * columns] for i in range(1, count, 2)]
    even = jnp.concatenate(even, 1)
    odd = jnp.concatenate(odd, 1)
    return jnp.where(core == 0, odd, even), jnp.where(core == 0, even, odd)


def pair_sum(left_sides, right_side):
    count = lax.axis_size("dp")
    tall = count // 2
    far = lax.axis_index("dp") // 2
    other, own = left_sides
    rows = other.shape[1] // tall
    arrived = lax.ppermute(
        left_dot(other, right_side).astype(BF), "dp", [(i, i ^ 1) for i in range(count)]
    )
    both = left_dot(own, right_side) + arrived.astype(F32)

    def pick(which):
        return lax.dynamic_slice_in_dim(both, which * rows, rows, 0)

    total = pick(far)
    for step in range(1, tall):
        moves = [(i, (i // 2 + step) % tall * 2 + i % 2) for i in range(count)]
        out = pick((far + step) % tall).astype(BF)
        total = total + lax.ppermute(out, "dp", moves).astype(F32)
    return total


WHOLE = pl.BlockSpec(memory_space=pltpu.VMEM)


def params(mebibytes):
    return pltpu.CompilerParams(vmem_limit_bytes=mebibytes * 1024 * 1024)


def cost(flops, nbytes):
    return pl.CostEstimate(flops=int(flops), bytes_accessed=int(nbytes), transcendentals=0)


def turned(values, cosine, sine):
    return values * cosine + pltpu.roll(values, HD // 2, 1) * sine


def project_kernel(block_rows, places, h_ref, wq, wk, wv, bq, bk, bv, cos, sin, q_ref, k_ref, v_ref):
    step = pl.program_id(0)
    per_step = h_ref.shape[0] // block_rows
    h = h_ref[...]
    q = plain_dot(h, wq[...]) + bq[...].astype(F32)
    k = plain_dot(h, wk[...]) + bk[...].astype(F32)
    v = plain_dot(h, wv[...]) + bv[...].astype(F32)
    for part in range(per_step):
        start = places[step * per_step + part] * block_rows
        rows = pl.ds(pl.multiple_of(start, block_rows), block_rows)
        near = slice(part * block_rows, (part + 1) * block_rows)
        cosine, sine = cos[rows, :], sin[rows, :]
        for head in range(q.shape[1] // HD):
            cols = slice(head * HD, (head + 1) * HD)
            q_ref[rows, cols] = turned(q[near, cols], cosine, sine).astype(BF)
            k_ref[rows, cols] = turned(k[near, cols], cosine, sine).astype(BF)
        v_ref[rows, :] = v[near].astype(BF)


def project(ring, h_all, weights, biases, tables):
    length, width = h_all.shape
    cols = weights[0].shape[1]
    block_rows = length // ring.count
    step_rows = 2 * block_rows
    shape = jax.ShapeDtypeStruct((length, cols), BF)
    return pl.pallas_call(
        functools.partial(project_kernel, block_rows),
        out_shape=(shape,) * 3,
        grid_spec=pltpu.PrefetchScalarGridSpec(
            num_scalar_prefetch=1,
            grid=(length // step_rows,),
            in_specs=[pl.BlockSpec((step_rows, width), lambda i, places: (i, 0))]
            + [pl.BlockSpec((width, cols), lambda i, places: (0, 0))] * 3
            + [pl.BlockSpec((1, cols), lambda i, places: (0, 0))] * 3
            + [pl.BlockSpec((length, HD), lambda i, places: (0, 0))] * 2,
            out_specs=[pl.BlockSpec((length, cols), lambda i, places: (0, 0))] * 3,
        ),
        compiler_params=params(40),
        cost_estimate=cost(6 * length * width * cols, 2 * length * width + 6 * width * cols),
        name="project",
    )(ring.block_of_slot, h_all, *weights, *[b[None] for b in biases], *tables)


def attend_kernel(block_rows, wide, slots, q_ref, k_ref, v_ref, out_ref):
    length, cols = q_ref.shape
    scale = HD ** (-0.5)
    at_row = lax.broadcasted_iota(jnp.int32, (wide, wide), 0)
    at_col = lax.broadcasted_iota(jnp.int32, (wide, wide), 1)
    allowed = at_col <= at_row
    for head in range(cols // HD):
        hs = slice(head * HD, (head + 1) * HD)
        for i in range(length // wide):
            low, high = i * wide, (i + 1) * wide
            q = q_ref[low:high, hs]
            near = right_dot(q, k_ref[low:high, hs]) * scale
            near = jnp.where(allowed, near, -jnp.inf)
            peak = jnp.max(near, 1, keepdims=True)
            if i:
                past = right_dot(q, k_ref[:low, hs]) * scale
                peak = jnp.maximum(peak, jnp.max(past, 1, keepdims=True))
                past = jnp.exp(past - peak)
            near = jnp.exp(near - peak)
            total = jnp.sum(near, 1, keepdims=True)
            if i:
                total = total + jnp.sum(past, 1, keepdims=True)
            share = 1.0 / total
            out = plain_dot((near * share).astype(BF), v_ref[low:high, hs])
            if i:
                out = out + plain_dot((past * share).astype(BF), v_ref[:low, hs])
            out = out.astype(BF)
            for part in range(wide // block_rows):
                slot = slots[i * (wide // block_rows) + part]
                rows = pl.ds(pl.multiple_of(slot * block_rows, block_rows), block_rows)
                out_ref[rows, hs] = out[part * block_rows : (part + 1) * block_rows]


def attend(ring, q, k, v):
    length, cols = q.shape
    return pl.pallas_call(
        functools.partial(attend_kernel, length // ring.count, 2 * (length // ring.count)),
        out_shape=jax.ShapeDtypeStruct((length, cols), BF),
        in_specs=[pl.BlockSpec(memory_space=pltpu.SMEM)] + [WHOLE] * 3,
        out_specs=WHOLE,
        compiler_params=params(40),
        cost_estimate=cost(2 * length * length * cols, 8 * length * cols),
        name="attend",
    )(ring.slot_of_block, q, k, v)


def attend_back_kernel(
    block_rows, wide, slots, q_ref, k_ref, v_ref, g_ref, cos, sin, dq_ref, dk_ref, dv_ref, k_sum, v_sum
):
    length, cols = q_ref.shape
    scale = HD ** (-0.5)
    at_key = lax.broadcasted_iota(jnp.int32, (wide, wide), 0)
    at_query = lax.broadcasted_iota(jnp.int32, (wide, wide), 1)
    allowed = at_key <= at_query
    per = wide // block_rows

    def put(ref, low, hs, values):
        for part in range(per):
            slot = slots[low // block_rows + part]
            rows = pl.ds(pl.multiple_of(slot * block_rows, block_rows), block_rows)
            ref[rows, hs] = values[part * block_rows : (part + 1) * block_rows].astype(BF)

    def back(values, low, high):
        return values * cos[low:high] - pltpu.roll(values, HD // 2, 1) * sin[low:high]

    for head in range(cols // HD):
        hs = slice(head * HD, (head + 1) * HD)
        for i in range(length // wide):
            low, high = i * wide, (i + 1) * wide
            q = q_ref[low:high, hs]
            g = g_ref[low:high, hs]
            spans = [(low, high)] + ([(0, low)] if i else [])
            scores = [right_dot(k_ref[a:b, hs], q) * scale for a, b in spans]
            scores[0] = jnp.where(allowed, scores[0], -jnp.inf)
            peak = functools.reduce(jnp.maximum, [jnp.max(s, 0, keepdims=True) for s in scores])
            probs = [jnp.exp(s - peak) for s in scores]
            total = sum(jnp.sum(p, 0, keepdims=True) for p in probs)
            share = 1.0 / total
            probs = [p * share for p in probs]
            grads = [right_dot(v_ref[a:b, hs], g) for a, b in spans]
            mean = sum(jnp.sum(p * d, 0, keepdims=True) for p, d in zip(probs, grads))
            draws = [(p * (d - mean) * scale).astype(BF) for p, d in zip(probs, grads)]
            dq = sum(left_dot(d, k_ref[a:b, hs]) for d, (a, b) in zip(draws, spans))
            put(dq_ref, low, hs, back(dq, low, high))
            for at, (a, b) in enumerate(spans):
                dv = plain_dot(probs[at].astype(BF), g)
                dk = plain_dot(draws[at], q)
                if at == 0:
                    v_sum[a:b, hs] = dv
                    k_sum[a:b, hs] = dk
                else:
                    v_sum[a:b, hs] += dv
                    k_sum[a:b, hs] += dk
        for i in range(length // wide):
            low, high = i * wide, (i + 1) * wide
            put(dk_ref, low, hs, back(k_sum[low:high, hs], low, high))
            put(dv_ref, low, hs, v_sum[low:high, hs])


def attend_back(ring, q, k, v, grad, tables):
    length, cols = q.shape
    return pl.pallas_call(
        functools.partial(attend_back_kernel, length // ring.count, 2 * (length // ring.count)),
        out_shape=(jax.ShapeDtypeStruct((length, cols), BF),) * 3,
        in_specs=[pl.BlockSpec(memory_space=pltpu.SMEM)] + [WHOLE] * 6,
        out_specs=(WHOLE,) * 3,
        scratch_shapes=[pltpu.VMEM((length, cols), F32)] * 2,
        compiler_params=params(48),
        cost_estimate=cost(5 * length * length * cols, 16 * length * cols),
        name="attend_back",
    )(ring.slot_of_block, q, k, v, grad, *tables)


def reorder_dot_kernel(block_rows, places, h_ref, w_ref, out_ref):
    step = pl.program_id(0)
    per_step = h_ref.shape[0] // block_rows
    out = plain_dot(h_ref[...], w_ref[...]).astype(BF)
    for part in range(per_step):
        start = places[step * per_step + part] * block_rows
        rows = pl.ds(pl.multiple_of(start, block_rows), block_rows)
        out_ref[rows, :] = out[part * block_rows : (part + 1) * block_rows]


def reorder_dot(ring, h_all, weight):
    length, width = h_all.shape
    cols = weight.shape[1]
    block_rows = length // ring.count
    step_rows = 2 * block_rows
    return pl.pallas_call(
        functools.partial(reorder_dot_kernel, block_rows),
        out_shape=jax.ShapeDtypeStruct((length, cols), BF),
        grid_spec=pltpu.PrefetchScalarGridSpec(
            num_scalar_prefetch=1,
            grid=(length // step_rows,),
            in_specs=[
                pl.BlockSpec((step_rows, width), lambda i, places: (i, 0)),
                pl.BlockSpec((width, cols), lambda i, places: (0, 0)),
            ],
            out_specs=pl.BlockSpec((length, cols), lambda i, places: (0, 0)),
        ),
        compiler_params=params(40),
        cost_estimate=cost(2 * length * width * cols, 2 * length * width + 2 * width * cols),
        name="reorder_dot",
    )(ring.block_of_slot, h_all, weight)


def gated(gate_pre, up_pre, back, scale):
    sigmoid = 1.0 / (1.0 + jnp.exp(-gate_pre))
    silu = gate_pre * sigmoid
    hidden = silu * up_pre
    scaled = scale * back
    grad_gate = scaled * up_pre * sigmoid * (1.0 + gate_pre * (1.0 - sigmoid))
    return hidden, scale * hidden, grad_gate, scaled * silu


def expert_kernel(h_ref, wa_ref, wb_ref, back_ref, gate_ref, hid_ref, da_ref, db_ref, sum_ref):
    wide = wa_ref.shape[1]
    rows_at_once = 256
    weights = jnp.concatenate([wa_ref[...], wb_ref[...]], 1)

    @pl.when(pl.program_id(0) == 0)
    def _():
        sum_ref[...] = jnp.zeros_like(sum_ref)

    for start in range(0, h_ref.shape[0], rows_at_once):
        rows = slice(start, start + rows_at_once)
        both = plain_dot(h_ref[rows], weights)
        back = back_ref[rows].astype(F32)
        hidden, scaled, da, db = gated(both[:, :wide], both[:, wide:], back, gate_ref[rows])
        sum_ref[rows] += hidden * back
        hid_ref[rows] = scaled.astype(BF)
        da_ref[rows] = da.astype(BF)
        db_ref[rows] = db.astype(BF)


def expert_units(h_all, weight_in, back, gate):
    length, width = h_all.shape
    units = back.shape[1]
    wide = 128
    tiles = units // wide
    tile = pl.BlockSpec((length, wide), lambda j: (0, j))
    shape = jax.ShapeDtypeStruct((length, units), BF)
    return pl.pallas_call(
        expert_kernel,
        out_shape=(shape,) * 3 + (jax.ShapeDtypeStruct((length, wide), F32),),
        grid=(tiles,),
        in_specs=[
            pl.BlockSpec((length, width), lambda j: (0, 0)),
            pl.BlockSpec((width, wide), lambda j: (0, j)),
            pl.BlockSpec((width, wide), lambda j: (0, j + tiles)),
            tile,
            pl.BlockSpec((length, 1), lambda j: (0, 0)),
        ],
        out_specs=(tile,) * 3 + (pl.BlockSpec((length, wide), lambda j: (0, 0)),),
        compiler_params=params(48),
        cost_estimate=cost(
            4 * length * width * units, 2 * length * width + 4 * width * units + 8 * length * units
        ),
        name="expert_units",
    )(h_all, weight_in, weight_in, back, gate)


def shared_kernel(h_ref, wg_ref, wu_ref, back_ref, scale_ref, hid_ref, dg_ref, du_ref, sum_ref):
    h = h_ref[...]
    back = back_ref[...].astype(F32)
    hidden, scaled, dg, du = gated(
        plain_dot(h, wg_ref[...]), plain_dot(h, wu_ref[...]), back, scale_ref[...]
    )
    sum_ref[...] = jnp.sum(hidden * back, 1, keepdims=True)
    hid_ref[...] = scaled.astype(BF)
    dg_ref[...] = dg.astype(BF)
    du_ref[...] = du.astype(BF)


def shared_units(h_all, weight_gate, weight_up, back, scale):
    length, width = h_all.shape
    units = back.shape[1]
    rows = 256
    tile = pl.BlockSpec((rows, units), lambda i: (i, 0))
    column = pl.BlockSpec((rows, 1), lambda i: (i, 0))
    weight = pl.BlockSpec((width, units), lambda i: (0, 0))
    shape = jax.ShapeDtypeStruct((length, units), BF)
    return pl.pallas_call(
        shared_kernel,
        out_shape=(shape,) * 3 + (jax.ShapeDtypeStruct((length, 1), F32),),
        grid=(length // rows,),
        in_specs=[pl.BlockSpec((rows, width), lambda i: (i, 0)), weight, weight, tile, column],
        out_specs=(tile,) * 3 + (column,),
        compiler_params=params(48),
        cost_estimate=cost(
            4 * length * width * units, 2 * length * width + 4 * width * units + 8 * length * units
        ),
        name="shared_units",
    )(h_all, weight_gate, weight_up, back, scale)


def shards(
    tokens,
    attention_gain,
    query_weight,
    query_bias,
    key_weight,
    key_bias,
    value_weight,
    value_bias,
    output_weight,
    feedforward_gain,
    shared_gate_weight,
    shared_up_weight,
    shared_down_weight,
    shared_switch,
    router_weight,
    expert_in,
    expert_out,
    routes,
    cotangent,
):
    tok_rows, model_width = tokens.shape
    groups = lax.axis_size("expert")
    me = lax.axis_index("expert")
    ring = Ring(groups)
    length = tok_rows * groups
    experts = router_weight.shape[1]
    weight_in = expert_in[0]
    weight_out = expert_out[0]
    tables = rope_tables(length)
    x_float = tokens.astype(F32)
    rms_attn = rms_scale(x_float)
    unit_attn = x_float * rms_attn
    gain_attn = attention_gain.astype(F32)
    h_attn = (unit_attn * gain_attn).astype(BF)
    h_attn_all = ring.gather(h_attn)
    lanes = jnp.arange(128, dtype=jnp.int32)
    picked = jnp.sum((routes[:, :, None] == lanes[None, None, :]).astype(F32), 1)
    picked_all = ring.gather(picked.astype(BF))
    late_cotangent, h_attn_all = lax.optimization_barrier((cotangent, h_attn_all))
    cotangent_all = ring.gather(late_cotangent)

    q_rot, k_rot, v_low = project(
        ring,
        h_attn_all,
        (query_weight, key_weight, value_weight),
        (query_bias, key_bias, value_bias),
        tables,
    )
    att_low = attend(ring, q_rot, k_rot, v_low)
    attention_own = ring.scatter_sum(right_dot(att_low, output_weight).astype(BF))
    residual = x_float + attention_own
    rms_ffn = rms_scale(residual)
    unit_ffn = residual * rms_ffn
    gain_ffn = feedforward_gain.astype(F32)
    h_ffn = (unit_ffn * gain_ffn).astype(BF)
    h_ffn_all = ring.gather(h_ffn)

    back_shared = plain_dot(cotangent_all, shared_down_weight).astype(BF)
    back_expert = plain_dot(cotangent_all, weight_out).astype(BF)

    def route(rows):
        switch = jax.nn.sigmoid(plain_dot(rows, shared_switch))
        logits = plain_dot(rows, router_weight)
        raised = jnp.exp(logits - jnp.max(logits, -1, keepdims=True))
        return switch, raised / jnp.sum(raised, -1, keepdims=True)

    switch_all, probs_all = route(h_ffn_all)
    mine = (lanes == me).astype(F32)
    picked_here = jnp.sum(picked_all.astype(F32) * mine, 1, keepdims=True)
    gate_here = jnp.sum(probs_all * mine[:experts], 1, keepdims=True) * picked_here
    expert_hidden, grad_gate_e, grad_up_e, gate_sums = expert_units(
        h_ffn_all, weight_in, back_expert, gate_here
    )
    shared_hidden, grad_gate_s, grad_up_s, switch_sums = shared_units(
        h_ffn_all, shared_gate_weight, shared_up_weight, back_shared, switch_all[:, None]
    )
    gate_sums = jnp.sum(gate_sums, 1, keepdims=True) * picked_here
    small = gate_sums * mine + switch_sums * (lanes == experts).astype(F32)
    small = ring.scatter_sum(small, F32)

    grad_ffn_part = (
        right_dot(grad_gate_s, shared_gate_weight)
        + right_dot(grad_up_s, shared_up_weight)
        + right_dot(jnp.concatenate([grad_gate_e, grad_up_e], 1), weight_in)
    ).astype(BF)
    grad_ffn = ring.scatter_sum(grad_ffn_part)

    switch, router_probs = route(h_ffn)
    grad_probs = small[:, :experts]
    grad_logits = router_probs * (
        grad_probs - jnp.sum(router_probs * grad_probs, -1, keepdims=True)
    )
    grad_switch = small[:, experts] * switch * (1.0 - switch)
    h_float = h_ffn.astype(F32)
    grad_ffn = grad_ffn + jnp.dot(grad_logits, router_weight.astype(F32).T, precision=HIGHEST)
    grad_ffn = grad_ffn + grad_switch[:, None] * shared_switch.astype(F32)
    grad_router_part = jnp.dot(grad_logits.T, h_float, precision=HIGHEST)
    grad_switch_row = jnp.dot(grad_switch, h_float, precision=HIGHEST)
    grad_ffn_gain_part = jnp.sum(grad_ffn * unit_ffn, 0)
    early = jnp.concatenate(
        [grad_router_part, grad_switch_row[None], grad_ffn_gain_part[None]], 0
    )
    early = cube_sum(cube_sum(early, "expert"), "dp")

    grad_out = cotangent.astype(F32)
    grad_unit_ffn = grad_ffn * gain_ffn
    grad_residual = grad_out + rms_ffn * (
        grad_unit_ffn - unit_ffn * jnp.mean(grad_unit_ffn * unit_ffn, -1, keepdims=True)
    )
    attention_grad = grad_residual.astype(BF)
    attention_grad_all = ring.gather(attention_grad)

    layer_part = (
        right_dot(shared_hidden, shared_down_weight) + right_dot(expert_hidden, weight_out)
    ).astype(BF)
    layer_part, attention_grad_all = lax.optimization_barrier((layer_part, attention_grad_all))
    layer_out = (residual + ring.scatter_sum(layer_part)).astype(BF)

    grad_att = reorder_dot(ring, attention_grad_all, output_weight)
    grad_query, grad_key, grad_value = attend_back(ring, q_rot, k_rot, v_low, grad_att, tables)
    grad_attn_part = (
        right_dot(grad_query, query_weight)
        + right_dot(grad_key, key_weight)
        + right_dot(grad_value, value_weight)
    )
    grad_gain_part = jnp.sum(grad_attn_part * h_attn_all.astype(F32), 0) / gain_attn
    grad_attention_gain = cube_sum(
        cube_sum(grad_gain_part.reshape(-1, 128), "expert"), "dp"
    ).reshape(-1)
    grad_attn_in = ring.scatter_sum(grad_attn_part.astype(BF))
    grad_unit_attn = grad_attn_in * gain_attn
    grad_tokens = grad_residual + rms_attn * (
        grad_unit_attn - unit_attn * jnp.mean(grad_unit_attn * unit_attn, -1, keepdims=True)
    )
    biases = jnp.stack(
        [
            jnp.sum(grad_query.astype(F32), 0),
            jnp.sum(grad_key.astype(F32), 0),
            jnp.sum(grad_value.astype(F32), 0),
        ]
    )
    biases = cube_sum(biases, "dp")
    h_attn_split = split_cores(h_attn_all)
    h_ffn_split = split_cores(h_ffn_all)
    cotangent_split = split_cores(cotangent_all)
    return (
        layer_out,
        grad_tokens,
        grad_attention_gain,
        pair_sum(h_attn_split, grad_query),
        biases[0],
        pair_sum(h_attn_split, grad_key),
        biases[1],
        pair_sum(h_attn_split, grad_value),
        biases[2],
        pair_sum(split_cores(attention_grad_all), att_low),
        early[experts + 1],
        pair_sum(h_ffn_split, grad_gate_s),
        pair_sum(h_ffn_split, grad_up_s),
        pair_sum(cotangent_split, shared_hidden),
        early[experts],
        early[:experts].T,
        jnp.concatenate(
            [pair_sum(h_ffn_split, grad_gate_e), pair_sum(h_ffn_split, grad_up_e)], 1
        )[None],
        pair_sum(cotangent_split, expert_hidden)[None],
    )


def solution(mesh):
    return jax.shard_map(
        shards,
        mesh=mesh,
        in_specs=(
            P(("dp", "expert"), None),
            P(),
            P(None, "expert"),
            P("expert"),
            P(None, "expert"),
            P("expert"),
            P(None, "expert"),
            P("expert"),
            P(None, "expert"),
            P(),
            P(None, "expert"),
            P(None, "expert"),
            P(None, "expert"),
            P(),
            P(),
            P("expert", None, None),
            P("expert", None, None),
            P(("dp", "expert"), None),
            P(("dp", "expert"), None),
        ),
        out_specs=(
            P(("dp", "expert"), None),
            P(("dp", "expert"), None),
            P(),
            P("dp", "expert"),
            P("expert"),
            P("dp", "expert"),
            P("expert"),
            P("dp", "expert"),
            P("expert"),
            P("dp", "expert"),
            P(),
            P("dp", "expert"),
            P("dp", "expert"),
            P("dp", "expert"),
            P(),
            P(),
            P("expert", "dp", None),
            P("expert", "dp", None),
        ),
        check_vma=False,
    )
```

time: 1550 us -> 679 us (0.44)
  waiting for transfers between devices: 1010 us -> 256 us
  matrix products: 242 us -> 145 us
  starting transfers between devices: 19.3 us -> 104 us
  local copies, waits for them, and re-layouts: 129 us -> 58.3 us
  Pallas kernels: 0 us -> 53.8 us
  blocking collectives: 41.6 us -> 0 us
  other arithmetic: 77.9 us -> 48.3 us
    reduce_scatter x5 -> x0, waiting for transfers between devices: 349 us -> none  [the longest x1 168 us: shards(): lax.psum_scatter(jnp.concatenate([left_dot(h_attn_all, grad_query), left_...]
    all_to_all x4 -> x0, waiting for transfers between devices: 307 us -> none  [the longest x1 110 us: send_to_experts(): lax.all_to_all(send_rows, 'expert', split_axis=0, concat_axis=0, tiled=True)]
    all_gather x4 -> x0, waiting for transfers between devices: 264 us -> none  [the longest x1 124 us: shards(): shared_grad_all = lax.all_gather(shared_grad, 'expert', axis=0, tiled=True)]
    ppermute x0 -> x112, waiting for transfers between devices: none -> 256 us  [the longest x15 62.6 us: scatter_sum(): ahead = lax.ppermute(up.astype(held), 'expert', self.forward)]
    dot_general x32 -> x9, matrix products: 183 us -> 21.1 us  [the longest x6 17.2 us: plain_dot(): return jnp.dot(left_side, right_side, preferred_element_type=F32)]
    ppermute x0 -> x112, starting transfers between devices: none -> 104 us  [the longest x15 24.1 us: gather(): ahead = lax.ppermute(ahead, 'expert', self.forward)]
    psum x1 -> x0, waiting for transfers between devices: 87.9 us -> none  [shards(): lax.psum((grad_attn_gain_part, grad_ffn_gain_part, grad_switch_part, grad...]
    pallas_call x0 -> x6, Pallas kernels: none -> 53.8 us  [the longest x1 22.6 us: expert_units(): pl.pallas_call(expert_kernel, out_shape=(shape,) * 3 + (jax.ShapeDtypeStr...]
  transfers between devices with their start and end apart: 14 -> 112, of which waited for: 11 -> 54; matrix products, arithmetic and copies ran while one was open for 19% -> 29% of each run, Pallas kernels for 0% -> 3%
where the time goes in v1:
time: 679 us; the launch traced here: 669 us
  waiting for transfers between devices  256 us (38%)
  matrix products  145 us (21%)
  starting transfers between devices  104 us (15%)
  local copies, waits for them, and re-layouts  58.3 us (9%)
  Pallas kernels  53.8 us (8%)
  other arithmetic  48.3 us (7%)
    dot_general x9, matrix products, right_dot(): lax.dot_general(left_side, right_side, (((1,), (1,)), ((), ())), preferre...  65.5 us
    ppermute x15, waiting for transfers between devices, scatter_sum(): ahead = lax.ppermute(up.astype(held), 'expert', self.forward)  62.6 us
    dot_general x20, matrix products, left_dot(): lax.dot_general(left_side, right_side, (((0,), (0,)), ((), ())), preferre...  58.7 us
    ppermute x15, waiting for transfers between devices, gather(): ahead = lax.ppermute(ahead, 'expert', self.forward)  52.1 us
    ppermute x15, waiting for transfers between devices, scatter_sum(): behind = lax.ppermute(down.astype(held), 'expert', self.backward)  42.6 us
    ppermute x12, waiting for transfers between devices, cube_sum(): lax.ppermute(values, axis, [(i, i ^ step) for i in range(count)])  30.8 us
    unnamed x260, local copies, waits for them, and re-layouts  29.4 us
    ppermute x10, waiting for transfers between devices, pair_sum(): total = total + lax.ppermute(out, 'dp', moves).astype(F32)  24.2 us
  transfers between devices with their start and end apart: 112, of which 54 were waited for; matrix products, arithmetic and copies ran while one was open for 29% of the time, Pallas kernels for 3%

profile of v1, /device:TPU:0, one launch (start us, length us, event | category | flops | bytes accessed | tf_op | source)
XLA Modules:
  0.0 668.9 jit_solution(3462863402409832818)
XLA Ops:
  103.6 7.8 %collective-permute-done.9 = bf16[128,2048]{1,0:T(8,128)(2,1)S(1)} collective-permute-done((bf16[128,2048]{1,0:T(8,128)(2,1)S(1)}, bf16[128,2048]{1,0:T(8,128)(2,1)S(1)}, u32[]{:S(2)}, u32[]{:S(2)}) %collective-permute-start.9) | collective-permute-done | bytes 524320 | tf_op jit(solution)/shard_map/ppermute | solution.py:115
  113.3 9.4 %collective-permute-done.26 = bf16[128,2048]{1,0:T(8,128)(2,1)S(1)} collective-permute-done((bf16[128,2048]{1,0:T(8,128)(2,1)S(1)}, bf16[128,2048]{1,0:T(8,128)(2,1)S(1)}, u32[]{:S(2)}, u32[]{:S(2)}) %collective-permute-start.26) | collective-permute-done | bytes 524320 | tf_op jit(solution)/shard_map/ppermute | solution.py:88
  124.8 9.1 %collective-permute-done.10 = bf16[128,2048]{1,0:T(8,128)(2,1)S(1)} collective-permute-done((bf16[128,2048]{1,0:T(8,128)(2,1)S(1)}, bf16[128,2048]{1,0:T(8,128)(2,1)S(1)}, u32[]{:S(2)}, u32[]{:S(2)}) %collective-permute-start.10) | collective-permute-done | bytes 524320 | tf_op jit(solution)/shard_map/ppermute | solution.py:115
  136.5 7.2 %collective-permute-done.28 = bf16[128,2048]{1,0:T(8,128)(2,1)S(1)} collective-permute-done((bf16[128,2048]{1,0:T(8,128)(2,1)S(1)}, bf16[128,2048]{1,0:T(8,128)(2,1)S(1)}, u32[]{:S(2)}, u32[]{:S(2)}) %collective-permute-start.28) | collective-permute-done | bytes 524320 | tf_op jit(solution)/shard_map/ppermute | solution.py:88
  152.3 8.0 %fusion.8.back_ref = bf16[1024,1408]{1,0:T(8,128)(2,1)} fusion(bf16[1024,2048]{1,0:T(8,128)(2,1)S(1)} %constant_dynamic-update-slice_fusion.18, bf16[1,2048,1408]{2,1,0:T(8,128)(2,1)S(1)} %bitcast.153), kind=kOutput, calls=%fused_computation.17 | convolution fusion | flops 5907021824 | bytes 12845056 | tf_op jit(solution)/shard_map/dot_general | solution.py:31
  180.6 10.1 %collective-permute-done.18 = bf16[128,2048]{1,0:T(8,128)(2,1)S(1)} collective-permute-done((bf16[128,2048]{1,0:T(8,128)(2,1)}, bf16[128,2048]{1,0:T(8,128)(2,1)S(1)}, u32[]{:S(2)}, u32[]{:S(2)}) %collective-permute-start.18) | collective-permute-done | bytes 524320 | tf_op jit(solution)/shard_map/ppermute | solution.py:88
  194.0 8.3 %collective-permute-done.20 = bf16[128,2048]{1,0:T(8,128)(2,1)S(1)} collective-permute-done((bf16[128,2048]{1,0:T(8,128)(2,1)S(1)}, bf16[128,2048]{1,0:T(8,128)(2,1)S(1)}, u32[]{:S(2)}, u32[]{:S(2)}) %collective-permute-start.20) | collective-permute-done | bytes 524320 | tf_op jit(solution)/shard_map/ppermute | solution.py:88
  216.4 22.6 %expert_units.1 = (bf16[1024,1408]{1,0:T(8,128)(2,1)S(1)}, bf16[1024,1408]{1,0:T(8,128)(2,1)}, bf16[1024,1408]{1,0:T(8,128)(2,1)}, f32[1024,128]{1,0:T(8,128)S(1)}) custom-call(bf16[1024,2048]{1,0:T(8,128)(2,1)} %copy-done.40, bf16[2048,2816]{1,0:T(8,128)(2,1)} %bitcast.150, bf16[2048,2816]{1,0:T(8,128)(2,1)} %bitcast.151, ...), custom_call_target="tpu_custom_call" | custom-call | flops 11811160064 | bytes 27262976 | tf_op jit(solution)/shard_map/expert_units/pallas_call | solution.py:402
  255.0 12.1 %fusion.4 = f32[1024,2048]{1,0:T(8,128)} fusion(bf16[1024,1408]{1,0:T(8,128)(2,1)} %copy-done.35, bf16[1,2048,1408]{2,1,0:T(8,128)(2,1)} %param.38), kind=kOutput, calls=%fused_computation.10 | convolution fusion | flops 5905580032 | bytes 17039360 | tf_op jit(solution)/shard_map/dot_general | solution.py:35
  272.4 11.9 %shared_units.1 = (bf16[1024,704]{1,0:T(8,128)(2,1)S(1)}, bf16[1024,704]{1,0:T(8,128)(2,1)S(1)}, bf16[1024,704]{1,0:T(8,128)(2,1)S(1)}, f32[1024,1]{1,0:T(8,128)S(1)}) custom-call(bf16[1024,2048]{1,0:T(8,128)(2,1)} %copy-done.40, bf16[2048,704]{1,0:T(8,128)(2,1)} %copy.56.wg_ref, bf16[2048,704]{1,0:T(8,128)(2,1)} %copy.57.wu_ref, ...), custom_call_target="tpu_custom_call" | custom-call | flops 5905580032 | bytes 15728640 | tf_op jit(solution)/shard_map/shared_units/pallas_call | solution.py:442
  291.1 9.1 %fusion.75 = f32[1024,2048]{1,0:T(8,128)} fusion(bf16[1024,704]{1,0:T(8,128)(2,1)} %copy-done.27, bf16[2048,704]{0,1:T(8,128)(2,1)} %param.32), kind=kOutput, calls=%fused_computation.249 | convolution fusion | flops 2952790016 | bytes 12713984 | tf_op jit(solution)/shard_map/dot_general | solution.py:35
  310.8 20.4 %add_convert_fusion = bf16[1024,2048]{1,0:T(8,128)(2,1)} fusion(f32[1024,2048]{1,0:T(8,128)} %fusion.75, f32[1024,2048]{1,0:T(8,128)} %fusion.76, bf16[1024,1408]{1,0:T(8,128)(2,1)} %get-tuple-element.46, bf16[1024,1408]{1,0:T(8,128)(2,1)} %get-tuple-element.45, bf16[1,2048,2816]{2,1,0:T(8,128)(2,1)} %param.37), kind=kOutput, calls=%fused_computation.3 | convolution fusion | flops 11828985856 | bytes 38273024 | tf_op jit(solution)/shard_map/dot_general | solution.py:35
  372.2 6.9 %collective-permute-done.42 = bf16[128,2048]{1,0:T(8,128)(2,1)S(1)} collective-permute-done((bf16[128,2048]{1,0:T(8,128)(2,1)S(1)}, bf16[128,2048]{1,0:T(8,128)(2,1)S(1)}, u32[]{:S(2)}, u32[]{:S(2)}) %collective-permute-start.42) | collective-permute-done | bytes 524320 | tf_op jit(solution)/shard_map/ppermute | solution.py:115
  385.5 8.4 %collective-permute-done.46 = bf16[128,2048]{1,0:T(8,128)(2,1)S(1)} collective-permute-done((bf16[128,2048]{1,0:T(8,128)(2,1)S(1)}, bf16[128,2048]{1,0:T(8,128)(2,1)S(1)}, u32[]{:S(2)}, u32[]{:S(2)}) %collective-permute-start.46) | collective-permute-done | bytes 524320 | tf_op jit(solution)/shard_map/ppermute | solution.py:116
  399.6 9.4 %collective-permute-done.47 = bf16[128,2048]{1,0:T(8,128)(2,1)S(1)} collective-permute-done((bf16[128,2048]{1,0:T(8,128)(2,1)S(1)}, bf16[128,2048]{1,0:T(8,128)(2,1)S(1)}, u32[]{:S(2)}, u32[]{:S(2)}) %collective-permute-start.47) | collective-permute-done | bytes 524320 | tf_op jit(solution)/shard_map/ppermute | solution.py:116
  419.5 8.9 %collective-permute-done.103 = bf16[512,704]{0,1:T(8,128)(2,1)S(1)} collective-permute-done((bf16[512,704]{0,1:T(8,128)(2,1)S(1)}, bf16[512,704]{0,1:T(8,128)(2,1)S(1)}, u32[]{:S(2)}, u32[]{:S(2)}) %collective-permute-start.103) | collective-permute-done | bytes 720928 | tf_op jit(solution)/shard_map/ppermute | solution.py:158
  433.8 8.8 %collective-permute-done.101 = bf16[512,704]{0,1:T(8,128)(2,1)S(1)} collective-permute-done((bf16[512,704]{0,1:T(8,128)(2,1)S(1)}, bf16[512,704]{0,1:T(8,128)(2,1)S(1)}, u32[]{:S(2)}, u32[]{:S(2)}) %collective-permute-start.101) | collective-permute-done | bytes 720928 | tf_op jit(solution)/shard_map/ppermute | solution.py:158
  484.5 9.7 %collective-permute-done.60 = bf16[128,2048]{1,0:T(8,128)(2,1)S(1)} collective-permute-done((bf16[128,2048]{1,0:T(8,128)(2,1)S(1)}, bf16[128,2048]{1,0:T(8,128)(2,1)S(1)}, u32[]{:S(2)}, u32[]{:S(2)}) %collective-permute-start.60) | collective-permute-done | bytes 524320 | tf_op jit(solution)/shard_map/ppermute | solution.py:88
  507.4 7.3 %attend_back.1 = (bf16[1024,256]{1,0:T(8,128)(2,1)S(1)}, bf16[1024,256]{1,0:T(8,128)(2,1)S(1)}, bf16[1024,256]{1,0:T(8,128)(2,1)S(1)}) custom-call(s32[8]{0:T(128)S(1)} %select_reduce_fusion.slots, bf16[1024,256]{1,0:T(8,128)(2,1)S(1)} %copy-done.18, bf16[1024,256]{1,0:T(8,128)(2,1)S(1)} %copy-done.20, bf16[1024,256]{1,0:T(8,128)(2,1)S(1)} %copy-done.22, ...), custom_call_target="tpu_custom_call" | custom-call | flops 1342177280 | bytes 4194304 | tf_op jit(solution)/shard_map/attend_back/pallas_call | solution.py:321
  543.6 11.0 %collective-permute-done.88 = f32[3,256]{1,0:T(4,128)S(1)} collective-permute-done((f32[3,256]{1,0:T(4,128)S(1)}, f32[3,256]{1,0:T(4,128)S(1)}, u32[]{:S(2)}, u32[]{:S(2)}) %collective-permute-start.88) | collective-permute-done | bytes 3104 | tf_op jit(solution)/shard_map/ppermute | solution.py:124
  593.8 12.5 %collective-permute-done.73 = bf16[128,2048]{1,0:T(8,128)(2,1)S(1)} collective-permute-done((bf16[128,2048]{1,0:T(8,128)(2,1)S(1)}, bf16[128,2048]{1,0:T(8,128)(2,1)S(1)}, u32[]{:S(2)}, u32[]{:S(2)}) %collective-permute-start.73) | collective-permute-done | bytes 524320 | tf_op jit(solution)/shard_map/ppermute | solution.py:115
  636.2 9.2 %collective-permute-done.70 = bf16[128,2048]{1,0:T(8,128)(2,1)S(1)} collective-permute-done((bf16[128,2048]{1,0:T(8,128)(2,1)S(1)}, bf16[128,2048]{1,0:T(8,128)(2,1)S(1)}, u32[]{:S(2)}, u32[]{:S(2)}) %collective-permute-start.70) | collective-permute-done | bytes 524320 | tf_op jit(solution)/shard_map/ppermute | solution.py:116
  647.6 7.5 %collective-permute-done.75 = bf16[128,2048]{1,0:T(8,128)(2,1)S(1)} collective-permute-done((bf16[128,2048]{1,0:T(8,128)(2,1)S(1)}, bf16[128,2048]{1,0:T(8,128)(2,1)S(1)}, u32[]{:S(2)}, u32[]{:S(2)}) %collective-permute-start.75) | collective-permute-done | bytes 524320 | tf_op jit(solution)/shard_map/ppermute | solution.py:115
  657.2 9.1 %collective-permute-done.71 = bf16[128,2048]{1,0:T(8,128)(2,1)S(1)} collective-permute-done((bf16[128,2048]{1,0:T(8,128)(2,1)S(1)}, bf16[128,2048]{1,0:T(8,128)(2,1)S(1)}, u32[]{:S(2)}, u32[]{:S(2)}) %collective-permute-start.71) | collective-permute-done | bytes 524320 | tf_op jit(solution)/shard_map/ppermute | solution.py:116
  (651 shorter events, 420.8 us)
Async XLA Ops:
  5.1 23.6 %collective-permute-start = (bf16[128,2048]{1,0:T(8,128)(2,1)}, bf16[128,2048]{1,0:T(8,128)(2,1)}, u32[]{:S(2)}, u32[]{:S(2)}) collective-permute-start(bf16[128,2048]{1,0:T(8,128)(2,1)} %get-tuple-element.63), channel_id=1, source_target_pairs={{0,2},{2,4},{4,6},{6,7},{7,5},{5,3},{3,1},{1,0},{8,10},{10,12},{12... | collective-permute-start | bytes 1572872 | tf_op jit(solution)/shard_map/ppermute | solution.py:88
  71.2 30.4 %collective-permute-start.24 = (bf16[128,2048]{1,0:T(8,128)(2,1)S(1)}, bf16[128,2048]{1,0:T(8,128)(2,1)S(1)}, u32[]{:S(2)}, u32[]{:S(2)}) collective-permute-start(bf16[128,2048]{1,0:T(8,128)(2,1)S(1)} %copy-done.48), channel_id=1, source_target_pairs={{0,2},{2,4},{4,6},{6,7},{7,5},{5,3},{3,1},{1,0},{8,10},{10,12},{12... | collective-permute-start | bytes 1572872 | tf_op jit(solution)/shard_map/ppermute | solution.py:88
  72.9 30.3 %collective-permute-start.25 = (bf16[128,2048]{1,0:T(8,128)(2,1)S(1)}, bf16[128,2048]{1,0:T(8,128)(2,1)S(1)}, u32[]{:S(2)}, u32[]{:S(2)}) collective-permute-start(bf16[128,2048]{1,0:T(8,128)(2,1)S(1)} %copy-done.48), channel_id=1, source_target_pairs={{0,1},{2,0},{4,2},{6,4},{7,6},{5,7},{3,5},{1,3},{8,9},{10,8},{12,1... | collective-permute-start | bytes 1572872 | tf_op jit(solution)/shard_map/ppermute | solution.py:89
  100.9 23.9 %collective-permute-start.13 = (bf16[128,2048]{1,0:T(8,128)(2,1)S(1)}, bf16[128,2048]{1,0:T(8,128)(2,1)S(1)}, u32[]{:S(2)}, u32[]{:S(2)}) collective-permute-start(bf16[128,2048]{1,0:T(8,128)(2,1)S(1)} %pad_maximum_fusion.15), channel_id=1, source_target_pairs={{0,1},{2,0},{4,2},{6,4},{7,6},{5,7},{3,5},{1,3},{8,9},{10,8},{12,1... | collective-permute-start | bytes 1572872 | tf_op jit(solution)/shard_map/ppermute | solution.py:116
  135.2 25.0 %collective-permute-start.11 = (bf16[128,2048]{1,0:T(8,128)(2,1)S(1)}, bf16[128,2048]{1,0:T(8,128)(2,1)S(1)}, u32[]{:S(2)}, u32[]{:S(2)}) collective-permute-start(bf16[128,2048]{1,0:T(8,128)(2,1)S(1)} %get-tuple-element.110), channel_id=1, source_target_pairs={{0,2},{2,4},{4,6},{6,7},{7,5},{5,3},{3,1},{1,0},{8,10},{10,12},{12... | collective-permute-start | bytes 1572872 | tf_op jit(solution)/shard_map/ppermute | solution.py:115
  290.6 41.9 %collective-permute-start.48 = (f32[64,128]{0,1:T(8,128)}, f32[64,128]{0,1:T(8,128)}, u32[]{:S(2)}, u32[]{:S(2)}) collective-permute-start(f32[64,128]{0,1:T(8,128)} %slice.481), channel_id=1, source_target_pairs={{0,2},{2,4},{4,6},{6,7},{7,5},{5,3},{3,1},{1,0},{8,10},{10,12},{12... | collective-permute-start | bytes 98312 | tf_op jit(solution)/shard_map/ppermute | solution.py:104
  350.5 102.4 %collective-permute-start.110 = (bf16[1024,1408]{1,0:T(8,128)(2,1)S(1)}, bf16[1024,1408]{1,0:T(8,128)(2,1)}, u32[]{:S(2)}, u32[]{:S(2)}) collective-permute-start(bf16[1024,1408]{1,0:T(8,128)(2,1)S(1)} %copy-done.93), channel_id=1, source_target_pairs={{0,8},{8,0},{16,24},{24,16},{1,9},{9,1},{17,25},{25,17},{2,10},{10... | collective-permute-start | bytes 8650760 | tf_op jit(solution)/shard_map/ppermute | solution.py:146
  350.6 28.9 %collective-permute-start.104 = (bf16[1024,704]{0,1:T(8,128)(2,1)S(1)}, bf16[1024,704]{0,1:T(8,128)(2,1)S(1)}, u32[]{:S(2)}, u32[]{:S(2)}) collective-permute-start(bf16[1024,704]{0,1:T(8,128)(2,1)S(1)} %copy-done.94), channel_id=1, source_target_pairs={{0,8},{8,0},{16,24},{24,16},{1,9},{9,1},{17,25},{25,17},{2,10},{10... | collective-permute-start | bytes 4325384 | tf_op jit(solution)/shard_map/ppermute | solution.py:146
  357.8 23.9 %collective-permute-start.102 = (bf16[1024,704]{0,1:T(8,128)(2,1)S(1)}, bf16[1024,704]{0,1:T(8,128)(2,1)S(1)}, u32[]{:S(2)}, u32[]{:S(2)}) collective-permute-start(bf16[1024,704]{0,1:T(8,128)(2,1)S(1)} %convolution_convert_fusion.5), channel_id=1, source_target_pairs={{0,8},{8,0},{16,24},{24,16},{1,9},{9,1},{17,25},{25,17},{2,10},{10... | collective-permute-start | bytes 4325384 | tf_op jit(solution)/shard_map/ppermute | solution.py:146
  372.2 89.3 %collective-permute-start.106 = (bf16[1024,1408]{1,0:T(8,128)(2,1)S(1)}, bf16[1024,1408]{1,0:T(8,128)(2,1)}, u32[]{:S(2)}, u32[]{:S(2)}) collective-permute-start(bf16[1024,1408]{1,0:T(8,128)(2,1)S(1)} %copy-done.92), channel_id=1, source_target_pairs={{0,8},{8,0},{16,24},{24,16},{1,9},{9,1},{17,25},{25,17},{2,10},{10... | collective-permute-start | bytes 8650760 | tf_op jit(solution)/shard_map/ppermute | solution.py:146
  399.5 72.7 %collective-permute-start.108 = (bf16[1024,1408]{1,0:T(8,128)(2,1)S(1)}, bf16[1024,1408]{1,0:T(8,128)(2,1)}, u32[]{:S(2)}, u32[]{:S(2)}) collective-permute-start(bf16[1024,1408]{1,0:T(8,128)(2,1)S(1)} %copy-done.91), channel_id=1, source_target_pairs={{0,8},{8,0},{16,24},{24,16},{1,9},{9,1},{17,25},{25,17},{2,10},{10... | collective-permute-start | bytes 8650760 | tf_op jit(solution)/shard_map/ppermute | solution.py:146
  417.9 24.7 %collective-permute-start.101 = (bf16[512,704]{0,1:T(8,128)(2,1)S(1)}, bf16[512,704]{0,1:T(8,128)(2,1)S(1)}, u32[]{:S(2)}, u32[]{:S(2)}) collective-permute-start(bf16[512,704]{0,1:T(8,128)(2,1)S(1)} %dynamic-slice_convert_fusion.5), channel_id=1, source_target_pairs={{0,16},{8,24},{16,0},{24,8},{1,17},{9,25},{17,1},{25,9},{2,18},{10... | collective-permute-start | bytes 2162696 | tf_op jit(solution)/shard_map/ppermute | solution.py:158
  447.4 22.8 %collective-permute-start.56 = (bf16[128,2048]{1,0:T(8,128)(2,1)S(1)}, bf16[128,2048]{1,0:T(8,128)(2,1)S(1)}, u32[]{:S(2)}, u32[]{:S(2)}) collective-permute-start(bf16[128,2048]{1,0:T(8,128)(2,1)S(1)} %get-tuple-element.57), channel_id=1, source_target_pairs={{0,2},{2,4},{4,6},{6,7},{7,5},{5,3},{3,1},{1,0},{8,10},{10,12},{12... | collective-permute-start | bytes 1572872 | tf_op jit(solution)/shard_map/ppermute | solution.py:88
  459.9 100.1 %collective-permute-start.111 = (bf16[512,1408]{1,0:T(8,128)(2,1)}, bf16[512,1408]{1,0:T(8,128)(2,1)}, u32[]{:S(2)}, u32[]{:S(2)}) collective-permute-start(bf16[512,1408]{1,0:T(8,128)(2,1)} %dynamic-slice_convert_fusion), channel_id=1, source_target_pairs={{0,16},{8,24},{16,0},{24,8},{1,17},{9,25},{17,1},{25,9},{2,18},{10... | collective-permute-start | bytes 4325384 | tf_op jit(solution)/shard_map/ppermute | solution.py:158
  468.7 95.0 %collective-permute-start.107 = (bf16[512,1408]{1,0:T(8,128)(2,1)}, bf16[512,1408]{1,0:T(8,128)(2,1)}, u32[]{:S(2)}, u32[]{:S(2)}) collective-permute-start(bf16[512,1408]{1,0:T(8,128)(2,1)} %dynamic-slice_convert_fusion.2), channel_id=1, source_target_pairs={{0,16},{8,24},{16,0},{24,8},{1,17},{9,25},{17,1},{25,9},{2,18},{10... | collective-permute-start | bytes 4325384 | tf_op jit(solution)/shard_map/ppermute | solution.py:158
  479.1 87.9 %collective-permute-start.109 = (bf16[512,1408]{1,0:T(8,128)(2,1)}, bf16[512,1408]{1,0:T(8,128)(2,1)}, u32[]{:S(2)}, u32[]{:S(2)}) collective-permute-start(bf16[512,1408]{1,0:T(8,128)(2,1)} %dynamic-slice_convert_fusion.1), channel_id=1, source_target_pairs={{0,16},{8,24},{16,0},{24,8},{1,17},{9,25},{17,1},{25,9},{2,18},{10... | collective-permute-start | bytes 4325384 | tf_op jit(solution)/shard_map/ppermute | solution.py:158
  543.6 39.5 %collective-permute-start.93 = (bf16[1024,256]{1,0:T(8,128)(2,1)S(1)}, bf16[1024,256]{1,0:T(8,128)(2,1)S(1)}, u32[]{:S(2)}, u32[]{:S(2)}) collective-permute-start(bf16[1024,256]{1,0:T(8,128)(2,1)S(1)} %fusion.22), channel_id=1, source_target_pairs={{0,8},{8,0},{16,24},{24,16},{1,9},{9,1},{17,25},{25,17},{2,10},{10... | collective-permute-start | bytes 1572872 | tf_op jit(solution)/shard_map/ppermute | solution.py:146
  559.4 26.1 %collective-permute-start.91 = (bf16[1024,256]{1,0:T(8,128)(2,1)S(1)}, bf16[1024,256]{1,0:T(8,128)(2,1)}, u32[]{:S(2)}, u32[]{:S(2)}) collective-permute-start(bf16[1024,256]{1,0:T(8,128)(2,1)S(1)} %copy-done.95), channel_id=1, source_target_pairs={{0,8},{8,0},{16,24},{24,16},{1,9},{9,1},{17,25},{25,17},{2,10},{10... | collective-permute-start | bytes 1572872 | tf_op jit(solution)/shard_map/ppermute | solution.py:146
  560.0 27.9 %collective-permute-start.89 = (bf16[1024,256]{1,0:T(8,128)(2,1)S(1)}, bf16[1024,256]{1,0:T(8,128)(2,1)}, u32[]{:S(2)}, u32[]{:S(2)}) collective-permute-start(bf16[1024,256]{1,0:T(8,128)(2,1)S(1)} %convolution_convert_fusion.9), channel_id=1, source_target_pairs={{0,8},{8,0},{16,24},{24,16},{1,9},{9,1},{17,25},{25,17},{2,10},{10... | collective-permute-start | bytes 1572872 | tf_op jit(solution)/shard_map/ppermute | solution.py:146
  582.3 41.4 %collective-permute-start.69 = (bf16[128,2048]{1,0:T(8,128)(2,1)S(1)}, bf16[128,2048]{1,0:T(8,128)(2,1)S(1)}, u32[]{:S(2)}, u32[]{:S(2)}) collective-permute-start(bf16[128,2048]{1,0:T(8,128)(2,1)S(1)} %pad_maximum_fusion.19), channel_id=1, source_target_pairs={{0,1},{2,0},{4,2},{6,4},{7,6},{5,7},{3,5},{1,3},{8,9},{10,8},{12,1... | collective-permute-start | bytes 1572872 | tf_op jit(solution)/shard_map/ppermute | solution.py:116
  583.1 24.9 %collective-permute-start.65 = (bf16[128,2048]{1,0:T(8,128)(2,1)S(1)}, bf16[128,2048]{1,0:T(8,128)(2,1)S(1)}, u32[]{:S(2)}, u32[]{:S(2)}) collective-permute-start(bf16[128,2048]{1,0:T(8,128)(2,1)S(1)} %pad_maximum_fusion.18), channel_id=1, source_target_pairs={{0,2},{2,4},{4,6},{6,7},{7,5},{5,3},{3,1},{1,0},{8,10},{10,12},{12... | collective-permute-start | bytes 1572872 | tf_op jit(solution)/shard_map/ppermute | solution.py:115
  585.6 32.1 %collective-permute-start.77 = (bf16[128,2048]{1,0:T(8,128)(2,1)S(1)}, bf16[128,2048]{1,0:T(8,128)(2,1)S(1)}, u32[]{:S(2)}, u32[]{:S(2)}) collective-permute-start(bf16[128,2048]{1,0:T(8,128)(2,1)S(1)} %pad_maximum_fusion.21), channel_id=1, source_target_pairs={{0,1},{2,0},{4,2},{6,4},{7,6},{5,7},{3,5},{1,3},{8,9},{10,8},{12,1... | collective-permute-start | bytes 1572872 | tf_op jit(solution)/shard_map/ppermute | solution.py:116
  617.6 29.1 %collective-permute-start.86 = (bf16[512,256]{1,0:T(8,128)(2,1)S(1)}, bf16[512,256]{1,0:T(8,128)(2,1)S(1)}, u32[]{:S(2)}, u32[]{:S(2)}) collective-permute-start(bf16[512,256]{1,0:T(8,128)(2,1)S(1)} %dynamic-slice_convert_fusion.9), channel_id=1, source_target_pairs={{0,16},{8,24},{16,0},{24,8},{1,17},{9,25},{17,1},{25,9},{2,18},{10... | collective-permute-start | bytes 786440 | tf_op jit(solution)/shard_map/ppermute | solution.py:158
  632.6 24.6 %collective-permute-start.67 = (bf16[128,2048]{1,0:T(8,128)(2,1)S(1)}, bf16[128,2048]{1,0:T(8,128)(2,1)S(1)}, u32[]{:S(2)}, u32[]{:S(2)}) collective-permute-start(bf16[128,2048]{1,0:T(8,128)(2,1)S(1)} %get-tuple-element.94), channel_id=1, source_target_pairs={{0,2},{2,4},{4,6},{6,7},{7,5},{5,3},{3,1},{1,0},{8,10},{10,12},{12... | collective-permute-start | bytes 1572872 | tf_op jit(solution)/shard_map/ppermute | solution.py:115
  (202 other events, 2673.5 us)

commit v2 on v1

v2 whole, which is shorter than its diff:
```python
import functools

import jax
import jax.numpy as jnp
from jax import lax
from jax.experimental import pallas as pl
from jax.experimental.pallas import tpu as pltpu
from jax.sharding import PartitionSpec as P

HD = 128
EPSILON = 1e-06
THETA = 1000000.0
HIGHEST = lax.Precision.HIGHEST
BF = jnp.bfloat16
F32 = jnp.float32


def rope_tables(length):
    middle = HD // 2
    inverse = THETA ** (-(jnp.arange(middle, dtype=F32) * 2.0 / HD))
    angles = jnp.arange(length, dtype=F32)[:, None] * inverse[None, :]
    sine = jnp.sin(angles)
    return (jnp.concatenate([jnp.cos(angles)] * 2, -1), jnp.concatenate([-sine, sine], -1))


def rms_scale(values):
    return lax.rsqrt(jnp.mean(values * values, -1, keepdims=True) + EPSILON)


def plain_dot(left_side, right_side):
    return jnp.dot(left_side, right_side, preferred_element_type=F32)


def right_dot(left_side, right_side):
    return lax.dot_general(
        left_side, right_side, (((1,), (1,)), ((), ())), preferred_element_type=F32
    )


def left_dot(left_side, right_side):
    return lax.dot_general(
        left_side, right_side, (((0,), (0,)), ((), ())), preferred_element_type=F32
    )


def ring_order(count):
    wide = 2 if count <= 8 else 4
    tall = count // wide
    order = [z * wide for z in range(tall)]
    for z in range(tall - 1, -1, -1):
        row = list(range(1, wide))
        if (tall - 1 - z) % 2:
            row = row[::-1]
        order += [z * wide + x for x in row]
    return order


class Ring:
    def __init__(self, count):
        self.count = count
        self.half = count // 2
        place = lax.axis_index("dp").astype(jnp.int32)
        self.core = jnp.stack([place % 2, place // 2])
        order = ring_order(count)
        self.forward = [(order[i], order[(i + 1) % count]) for i in range(count)]
        self.backward = [(order[i], order[(i - 1) % count]) for i in range(count)]
        place = [0] * count
        for at, device in enumerate(order):
            place[device] = at
        distances = []
        for step in range(1, self.half):
            distances += [-step, step]
        distances += [0, self.half]
        here = jnp.array(place, jnp.int32)[lax.axis_index("expert")]
        around = (here + jnp.array(distances, jnp.int32) + count) % count
        self.block_of_slot = jnp.array(order, jnp.int32)[around]
        hits = self.block_of_slot[None, :] == jnp.arange(count, dtype=jnp.int32)[:, None]
        self.slot_of_block = jnp.sum(hits * jnp.arange(count, dtype=jnp.int32)[None, :], 1)

    def slot(self, distance):
        if distance in (0, self.half):
            return self.count - 2 + (distance > 0)
        return 2 * abs(distance) - 2 + (distance > 0)


def after(values, *others):
    return lax.optimization_barrier((values, others))[0]


def move(ring, rounds, *others):
    up, down = zip(*[each.outgoing() for each in rounds])
    rows = [piece.shape[0] for piece in up]
    if len(rounds) > 1:
        up, down = jnp.concatenate(up, 0), jnp.concatenate(down, 0)
    else:
        up, down = up[0], down[0]
    up, down = after((up, down), *others)
    ahead = lax.ppermute(up, "expert", ring.forward)
    behind = lax.ppermute(down, "expert", ring.backward)
    at = 0
    for each, count in zip(rounds, rows):
        if len(rounds) > 1:
            each.arrive(ahead[at : at + count], behind[at : at + count])
        else:
            each.arrive(ahead, behind)
        at += count
    return (ahead, behind)


class Gather:
    def __init__(self, ring, block):
        self.ring = ring
        self.pieces = [block]
        self.ahead = self.behind = block
        self.at = 0

    def outgoing(self):
        self.at += 1
        if self.at < self.ring.half:
            return self.ahead, self.behind
        middle = self.pieces[0].shape[0] // 2
        return self.ahead[:middle], self.behind[middle:]

    def arrive(self, ahead, behind):
        self.ahead, self.behind = ahead, behind
        self.pieces += [ahead, behind]

    def step(self, *others):
        return move(self.ring, [self], *others)

    def chunk(self, which):
        if which < self.ring.half - 1:
            return self.pieces[2 * which + 1 : 2 * which + 3]
        return [self.pieces[0]] + self.pieces[-2:]

    def rest(self):
        while self.at < self.ring.half:
            self.step()
        return self.pieces[1:-2] + [self.pieces[0]] + self.pieces[-2:]


class Scatter:
    def __init__(self, ring, chunks, rows):
        self.ring = ring
        self.chunks = chunks
        self.rows = rows
        self.at = ring.half

    def own(self, distance):
        slot = self.ring.slot(distance)
        slots = self.ring.count // len(self.chunks)
        start = slot % slots * self.rows
        return self.chunks[slot // slots][start : start + self.rows]

    def outgoing(self):
        middle = self.rows // 2
        at = self.at
        self.at -= 1
        if at == self.ring.half:
            far = self.own(at)
            return far[:middle], far[middle:]
        up = self.own(at).astype(F32)
        down = self.own(-at).astype(F32)
        if at == self.ring.half - 1:
            up = jnp.concatenate([up[:middle] + self.ahead.astype(F32), up[middle:]], 0)
            down = jnp.concatenate([down[:middle], down[middle:] + self.behind.astype(F32)], 0)
        else:
            up = up + self.ahead.astype(F32)
            down = down + self.behind.astype(F32)
        return up.astype(BF), down.astype(BF)

    def arrive(self, ahead, behind):
        self.ahead, self.behind = ahead, behind

    def step(self, *others):
        return move(self.ring, [self], *others)

    def rest(self, *others):
        while self.at:
            self.step()
        return after(self.own(0), *others).astype(F32) + self.ahead.astype(F32) + self.behind.astype(F32)


def cube_steps(axis):
    count = lax.axis_size(axis)
    step, moves = 1, []
    while step < count:
        moves.append((axis, [(i, i ^ step) for i in range(count)]))
        step *= 2
    return moves


class PairSum:
    def __init__(self, splits, rights):
        self.splits = splits
        self.rights = rights
        self.tall = len(splits[0]) - 1

    def lefts(self, which, *others):
        return after([split[which] for split in self.splits], *others)

    def cores(self, *others, time=0):
        count = lax.axis_size("dp")
        (sent,) = pair_dot(self.lefts(0, *others), self.rights, [], BF, 1, time)
        self.arrived = lax.ppermute(sent, "dp", [(i, i ^ 1) for i in range(count)])
        return sent

    def chips(self, *others, time=0):
        count = lax.axis_size("dp")
        size = self.splits[0][1].shape[1]
        self.parts = []
        out = others
        for step in range(1, self.tall):
            adds = [(self.arrived, step * size)]
            (out,) = pair_dot(self.lefts(1 + step, *others), self.rights, adds, BF, 1, time)
            moves = [(i, (i // 2 + step) % self.tall * 2 + i % 2) for i in range(count)]
            self.parts.append(lax.ppermute(out, "dp", moves))
        return out

    def total(self, *others, time=0, outs=1, turned_rows=0):
        adds = [(self.arrived, 0)] + [(part, 0) for part in self.parts]
        lefts = self.lefts(1, *others)
        return pair_dot(lefts, self.rights, adds, F32, outs, time, turned_rows)


WHOLE = pl.BlockSpec(memory_space=pltpu.VMEM)
ANY = pl.BlockSpec(memory_space=pl.ANY)
SCALARS = pl.BlockSpec(memory_space=pltpu.SMEM)


class Copies:
    def __init__(self, sems):
        self.sems = sems
        self.count = 0

    def start(self, source, target):
        copy = pltpu.make_async_copy(source, target, self.sems.at[self.count])
        self.count += 1
        copy.start()
        return copy


def tiles_of(columns, wide):
    return [(low, min(low + wide, columns)) for low in range(0, columns, wide)]


def bring(copies, pieces, rows_ref):
    at, started = 0, []
    for piece in pieces:
        rows = slice(at, at + piece.shape[0])
        started.append(copies.start(piece, rows_ref.at[rows]))
        at += piece.shape[0]
    return started


def chunks_of(pieces, brought, wide):
    at, left = 0, list(zip(pieces, brought))
    for low in range(0, sum(piece.shape[0] for piece in pieces), wide):
        waits = []
        while left and at < low + wide:
            piece, copy = left.pop(0)
            at += piece.shape[0]
            waits.append(copy)
        yield slice(low, low + wide), waits


def params(mebibytes):
    return pltpu.CompilerParams(vmem_limit_bytes=mebibytes * 1024 * 1024)


def cost(time):
    return pl.CostEstimate(flops=int(1e9 * time) + 1, bytes_accessed=1, transcendentals=0)


def split_shapes(rows, width):
    count = lax.axis_size("dp")
    widths = [width // 2] + [width // count] * (count // 2)
    return tuple(jax.ShapeDtypeStruct((rows, w), BF) for w in widths)


def put_split(place, row_ref, refs, rows=slice(None)):
    core, far = place[0], place[1]
    other_ref, own_refs = refs[0], refs[1:]
    columns, tall = own_refs[0].shape[1], len(own_refs)
    for part in range(tall):
        chip = lax.rem(far + part, tall)
        at = pl.multiple_of((2 * chip + 1 - core) * columns, columns)
        there = slice(part * columns, (part + 1) * columns)
        other_ref[rows, there] = row_ref[rows, pl.ds(at, columns)]
        at = pl.multiple_of((2 * chip + core) * columns, columns)
        own_refs[part][rows, :] = row_ref[rows, pl.ds(at, columns)]


def turned(values, cosine, sine):
    return values * cosine + pltpu.roll(values, HD // 2, 1) * sine


def project_kernel(pieces, splits, places, place, *refs):
    parts, refs = refs[:pieces], refs[pieces:]
    hbm, refs = refs[:8], refs[8:]
    outs, refs = refs[:3], refs[3:]
    split_hbm, refs = refs[: splits + 1], refs[splits + 1 :]
    q_ref, k_ref, v_ref = outs
    h_ref, refs = refs[0], refs[1:]
    split_ref, refs = refs[:splits], refs[splits:]
    w_ref, bq, bk, bv, cos, sin, sems = refs
    cols = bq.shape[1]
    copies = Copies(sems)
    targets = [w_ref.at[:, at * cols : (at + 1) * cols] for at in range(3)]
    of_weights = [copies.start(a, b) for a, b in zip(hbm, targets + [bq, bk, bv, cos, sin])]
    brought = bring(copies, parts, h_ref)
    block_rows = h_ref.shape[0] // places.shape[0]
    for copy in of_weights:
        copy.wait()
    kept = []
    sources = [h_ref] + list(split_ref)
    targets = [split_hbm[-1]] + list(split_hbm[:-1])
    for chunk, waits in chunks_of(parts, brought, 2 * block_rows):
        for copy in waits:
            copy.wait()
        put_split(place, h_ref, split_ref, chunk)
        kept += [copies.start(a.at[chunk], b.at[chunk]) for a, b in zip(sources, targets)]
        qkv = plain_dot(h_ref[chunk], w_ref[...])
        q = qkv[:, :cols] + bq[...].astype(F32)
        k = qkv[:, cols : 2 * cols] + bk[...].astype(F32)
        v = qkv[:, 2 * cols :] + bv[...].astype(F32)
        for part in range(2):
            start = places[chunk.start // block_rows + part] * block_rows
            rows = pl.ds(pl.multiple_of(start, block_rows), block_rows)
            near = slice(part * block_rows, (part + 1) * block_rows)
            cosine, sine = cos[rows, :], sin[rows, :]
            for head in range(cols // HD):
                hs = slice(head * HD, (head + 1) * HD)
                q_ref[rows, hs] = turned(q[near, hs], cosine, sine).astype(BF)
                k_ref[rows, hs] = turned(k[near, hs], cosine, sine).astype(BF)
            v_ref[rows, :] = v[near].astype(BF)
    for copy in kept:
        copy.wait()


def project(ring, parts, weights, biases, tables, time=3):
    width, cols = weights[0].shape
    length = sum(part.shape[0] for part in parts)
    shape = jax.ShapeDtypeStruct((length, cols), BF)
    split = split_shapes(length, width)
    pieces = len(parts)
    return pl.pallas_call(
        functools.partial(project_kernel, pieces, len(split)),
        out_shape=(shape,) * 3 + split + (jax.ShapeDtypeStruct((length, width), BF),),
        in_specs=[SCALARS] * 2 + [ANY] * (pieces + 8),
        out_specs=(WHOLE,) * 3 + (ANY,) * (len(split) + 1),
        scratch_shapes=[pltpu.VMEM((length, width), BF)]
        + [pltpu.VMEM(part.shape, BF) for part in split]
        + [pltpu.VMEM((width, 3 * cols), BF)]
        + [pltpu.VMEM((1, cols), BF)] * 3
        + [pltpu.VMEM((length, HD), F32)] * 2
        + [pltpu.SemaphoreType.DMA((pieces + 8 + ring.half * (len(split) + 1),))],
        compiler_params=params(52),
        cost_estimate=cost(time),
        name="project",
    )(ring.block_of_slot, ring.core, *parts, *weights, *[b[None] for b in biases], *tables)


def bring_all(sources, targets, sems):
    copies = Copies(sems)
    for copy in [copies.start(source, target) for source, target in zip(sources, targets)]:
        copy.wait()


def attend_kernel(
    block_rows, wide, slots, q_hbm, k_hbm, v_hbm, out_ref, q_ref, k_ref, v_ref, sems
):
    bring_all((q_hbm, k_hbm, v_hbm), (q_ref, k_ref, v_ref), sems)
    length, cols = q_ref.shape
    scale = HD ** (-0.5)
    at_row = lax.broadcasted_iota(jnp.int32, (wide, wide), 0)
    at_col = lax.broadcasted_iota(jnp.int32, (wide, wide), 1)
    allowed = at_col <= at_row
    for head in range(cols // HD):
        hs = slice(head * HD, (head + 1) * HD)
        for i in range(length // wide):
            low, high = i * wide, (i + 1) * wide
            q = q_ref[low:high, hs]
            near = right_dot(q, k_ref[low:high, hs]) * scale
            near = jnp.where(allowed, near, -jnp.inf)
            peak = jnp.max(near, 1, keepdims=True)
            if i:
                past = right_dot(q, k_ref[:low, hs]) * scale
                peak = jnp.maximum(peak, jnp.max(past, 1, keepdims=True))
                past = jnp.exp(past - peak)
            near = jnp.exp(near - peak)
            total = jnp.sum(near, 1, keepdims=True)
            if i:
                total = total + jnp.sum(past, 1, keepdims=True)
            share = 1.0 / total
            out = plain_dot((near * share).astype(BF), v_ref[low:high, hs])
            if i:
                out = out + plain_dot((past * share).astype(BF), v_ref[:low, hs])
            out = out.astype(BF)
            for part in range(wide // block_rows):
                slot = slots[i * (wide // block_rows) + part]
                rows = pl.ds(pl.multiple_of(slot * block_rows, block_rows), block_rows)
                out_ref[rows, hs] = out[part * block_rows : (part + 1) * block_rows]


def attend(ring, q, k, v, time=3):
    length, cols = q.shape
    return pl.pallas_call(
        functools.partial(attend_kernel, length // ring.count, 2 * (length // ring.count)),
        out_shape=jax.ShapeDtypeStruct((length, cols), BF),
        in_specs=[SCALARS] + [ANY] * 3,
        out_specs=WHOLE,
        scratch_shapes=[pltpu.VMEM((length, cols), BF)] * 3 + [pltpu.SemaphoreType.DMA((3,))],
        compiler_params=params(40),
        cost_estimate=cost(time),
        name="attend",
    )(ring.slot_of_block, q, k, v)


def attend_back_kernel(
    block_rows, wide, slots, q_hbm, k_hbm, v_hbm, g_hbm, cos_hbm, sin_hbm, out_ref, bias_ref,
    q_ref, k_ref, v_ref, g_ref, cos, sin, k_sum, v_sum, sems,
):
    sources = (q_hbm, k_hbm, v_hbm, g_hbm, cos_hbm, sin_hbm)
    bring_all(sources, (q_ref, k_ref, v_ref, g_ref, cos, sin), sems)
    length, cols = q_ref.shape
    scale = HD ** (-0.5)
    at_key = lax.broadcasted_iota(jnp.int32, (wide, wide), 0)
    at_query = lax.broadcasted_iota(jnp.int32, (wide, wide), 1)
    allowed = at_key <= at_query
    per = wide // block_rows
    bias_ref[...] = jnp.zeros_like(bias_ref)

    def put(which, low, head, values):
        hs = slice(which * cols + head * HD, which * cols + (head + 1) * HD)
        values = values.astype(BF)
        bias_ref[:, hs] += jnp.sum(values.astype(F32), 0, keepdims=True)
        for part in range(per):
            slot = slots[low // block_rows + part]
            rows = pl.ds(pl.multiple_of(slot * block_rows, block_rows), block_rows)
            out_ref[rows, hs] = values[part * block_rows : (part + 1) * block_rows]

    def back(values, low, high):
        return values * cos[low:high] - pltpu.roll(values, HD // 2, 1) * sin[low:high]

    for head in range(cols // HD):
        hs = slice(head * HD, (head + 1) * HD)
        for i in range(length // wide):
            low, high = i * wide, (i + 1) * wide
            q = q_ref[low:high, hs]
            g = g_ref[low:high, hs]
            spans = [(low, high)] + ([(0, low)] if i else [])
            scores = [right_dot(k_ref[a:b, hs], q) * scale for a, b in spans]
            scores[0] = jnp.where(allowed, scores[0], -jnp.inf)
            peak = functools.reduce(jnp.maximum, [jnp.max(s, 0, keepdims=True) for s in scores])
            probs = [jnp.exp(s - peak) for s in scores]
            total = sum(jnp.sum(p, 0, keepdims=True) for p in probs)
            share = 1.0 / total
            probs = [p * share for p in probs]
            grads = [right_dot(v_ref[a:b, hs], g) for a, b in spans]
            mean = sum(jnp.sum(p * d, 0, keepdims=True) for p, d in zip(probs, grads))
            draws = [(p * (d - mean) * scale).astype(BF) for p, d in zip(probs, grads)]
            dq = sum(left_dot(d, k_ref[a:b, hs]) for d, (a, b) in zip(draws, spans))
            put(0, low, head, back(dq, low, high))
            for at, (a, b) in enumerate(spans):
                dv = plain_dot(probs[at].astype(BF), g)
                dk = plain_dot(draws[at], q)
                if at == 0:
                    v_sum[a:b, hs] = dv
                    k_sum[a:b, hs] = dk
                else:
                    v_sum[a:b, hs] += dv
                    k_sum[a:b, hs] += dk
        for i in range(length // wide):
            low, high = i * wide, (i + 1) * wide
            put(1, low, head, back(k_sum[low:high, hs], low, high))
            put(2, low, head, v_sum[low:high, hs])


def attend_back(ring, q, k, v, grad, tables, time=20):
    length, cols = q.shape
    return pl.pallas_call(
        functools.partial(attend_back_kernel, length // ring.count, 2 * (length // ring.count)),
        out_shape=(
            jax.ShapeDtypeStruct((length, 3 * cols), BF),
            jax.ShapeDtypeStruct((1, 3 * cols), F32),
        ),
        in_specs=[SCALARS] + [ANY] * 6,
        out_specs=(WHOLE,) * 2,
        scratch_shapes=[pltpu.VMEM((length, cols), BF)] * 4
        + [pltpu.VMEM((length, HD), F32)] * 2
        + [pltpu.VMEM((length, cols), F32)] * 2
        + [pltpu.SemaphoreType.DMA((6,))],
        compiler_params=params(48),
        cost_estimate=cost(time),
        name="attend_back",
    )(ring.slot_of_block, q, k, v, grad, *tables)


def attend_in_kernel(
    d_hbm, wq_hbm, wk_hbm, wv_hbm, h_hbm, gain_ref, out_hbm, gain_out,
    d_ref, wq_ref, wk_ref, wv_ref, h_ref, out_ref, sems,
):
    cols = wq_ref.shape[1]
    copies = Copies(sems)
    of_d = copies.start(d_hbm, d_ref)
    tiles = tiles_of(h_ref.shape[1], 512)
    weights = ((wq_hbm, wq_ref), (wk_hbm, wk_ref), (wv_hbm, wv_ref))
    of_tiles = [
        [copies.start(a.at[low:high], b.at[low:high]) for a, b in weights]
        + [copies.start(h_hbm.at[:, low:high], h_ref.at[:, low:high])]
        for low, high in tiles
    ]
    of_d.wait()
    kept = []
    for started, (low, high) in zip(of_tiles, tiles):
        for copy in started[:-1]:
            copy.wait()
        out = right_dot(d_ref[:, :cols], wq_ref[low:high])
        out = out + right_dot(d_ref[:, cols : 2 * cols], wk_ref[low:high])
        out = out + right_dot(d_ref[:, 2 * cols :], wv_ref[low:high])
        out_ref[:, low:high] = out.astype(BF)
        kept.append(copies.start(out_ref.at[:, low:high], out_hbm.at[:, low:high]))
        started[-1].wait()
        products = out * h_ref[:, low:high].astype(F32)
        gain_out[:, low:high] = jnp.sum(products, 0, keepdims=True) / gain_ref[:, low:high]
    for copy in kept:
        copy.wait()


def attend_in(grads, weights, h_all, gain, time=1):
    length, cols = grads.shape
    width = h_all.shape[1]
    return pl.pallas_call(
        attend_in_kernel,
        out_shape=(
            jax.ShapeDtypeStruct((length, width), BF),
            jax.ShapeDtypeStruct((1, width), F32),
        ),
        in_specs=[ANY] * 5 + [WHOLE],
        out_specs=(ANY, WHOLE),
        scratch_shapes=[pltpu.VMEM((length, cols), BF)]
        + [pltpu.VMEM((width, cols // 3), BF)] * 3
        + [
            pltpu.VMEM((length, width), BF),
            pltpu.VMEM((length, width), BF),
            pltpu.SemaphoreType.DMA((1 + 5 * len(tiles_of(width, 512)),)),
        ],
        compiler_params=params(48),
        cost_estimate=cost(time),
        name="attend_in",
    )(grads, *weights, h_all, gain)


def reorder_dot_kernel(pieces, splits, places, place, *refs):
    parts, refs = refs[:pieces], refs[pieces:]
    w_hbm, out_ref, refs = refs[0], refs[1], refs[2:]
    split_hbm, refs = refs[:splits], refs[splits:]
    h_ref, split_ref, w_ref = refs[0], refs[1 : 1 + splits], refs[1 + splits]
    copies = Copies(refs[-1])
    of_weight = copies.start(w_hbm, w_ref)
    brought = bring(copies, parts, h_ref)
    block_rows = h_ref.shape[0] // places.shape[0]
    of_weight.wait()
    kept = []
    for chunk, waits in chunks_of(parts, brought, 2 * block_rows):
        for copy in waits:
            copy.wait()
        put_split(place, h_ref, split_ref, chunk)
        kept += [copies.start(a.at[chunk], b.at[chunk]) for a, b in zip(split_ref, split_hbm)]
        out = plain_dot(h_ref[chunk], w_ref[...]).astype(BF)
        for part in range(2):
            start = places[chunk.start // block_rows + part] * block_rows
            rows = pl.ds(pl.multiple_of(start, block_rows), block_rows)
            out_ref[rows, :] = out[part * block_rows : (part + 1) * block_rows]
    for copy in kept:
        copy.wait()


def reorder_dot(ring, parts, weight, time=10):
    width, cols = weight.shape
    length = sum(part.shape[0] for part in parts)
    split = split_shapes(length, width)
    pieces = len(parts)
    return pl.pallas_call(
        functools.partial(reorder_dot_kernel, pieces, len(split)),
        out_shape=(jax.ShapeDtypeStruct((length, cols), BF),) + split,
        in_specs=[SCALARS] * 2 + [ANY] * (pieces + 1),
        out_specs=(WHOLE,) + (ANY,) * len(split),
        scratch_shapes=[pltpu.VMEM((length, width), BF)]
        + [pltpu.VMEM(part.shape, BF) for part in split]
        + [
            pltpu.VMEM((width, cols), BF),
            pltpu.SemaphoreType.DMA((pieces + 1 + ring.half * len(split),)),
        ],
        compiler_params=params(52),
        cost_estimate=cost(time),
        name="reorder_dot",
    )(ring.block_of_slot, ring.core, *parts, weight)


def gated(gate_pre, up_pre, back, scale):
    sigmoid = 0.5 + 0.5 * jnp.tanh(0.5 * gate_pre)
    silu = gate_pre * sigmoid
    hidden = silu * up_pre
    scaled = scale * back
    grad_gate = scaled * up_pre * (sigmoid + silu * (1.0 - sigmoid))
    return hidden, scale * hidden, grad_gate, scaled * silu


def back_kernel(pieces, which, split, place, *refs):
    parts, refs = refs[:pieces], refs[pieces:]
    wo_hbm, wd_hbm = refs[:2]
    refs = refs[-(2 * split + 6) :]
    back_e_ref, back_s_ref = refs[:2]
    kept_hbm, kept_ref = refs[2 : 2 + split], refs[2 + split : 2 + 2 * split]
    rows_ref, wo_ref, wd_ref, sems = refs[-4:]
    rows, width = rows_ref.shape
    copies = Copies(sems)
    brought = bring(copies, parts, rows_ref)
    tiles = tiles_of(wo_ref.shape[1], 512)
    of_e = [copies.start(wo_hbm.at[:, a:b], wo_ref.at[:, a:b]) for a, b in tiles]
    of_s = copies.start(wd_hbm, wd_ref)
    for copy in brought:
        copy.wait()
    put_split(place, rows_ref, kept_ref)
    chunk = slice(which * rows, (which + 1) * rows)
    kept = [copies.start(ref, hbm.at[chunk]) for ref, hbm in zip(kept_ref, kept_hbm)]
    for copy, (a, b) in zip(of_e, tiles):
        copy.wait()
        back_e_ref[:, a:b] = plain_dot(rows_ref[...], wo_ref[:, a:b]).astype(BF)
    of_s.wait()
    back_s_ref[...] = right_dot(rows_ref[...], wd_ref[...]).astype(BF)
    for copy in kept:
        copy.wait()


def back_units(ring, which, parts, weight_out, weight_down, kept, time=6):
    width, units = weight_out.shape
    shared = weight_down.shape[0]
    rows = sum(part.shape[0] for part in parts)
    pieces = len(parts)
    first = pieces + 3
    split = split_shapes(rows * ring.half, width)
    return pl.pallas_call(
        functools.partial(back_kernel, pieces, which, len(split)),
        out_shape=(
            jax.ShapeDtypeStruct((rows, units), BF),
            jax.ShapeDtypeStruct((rows, shared), BF),
        )
        + split,
        in_specs=[SCALARS] + [ANY] * (pieces + 2 + len(kept)),
        out_specs=(WHOLE, WHOLE) + (ANY,) * len(split),
        scratch_shapes=[pltpu.VMEM((rows, part.shape[1]), BF) for part in split]
        + [
            pltpu.VMEM((rows, width), BF),
            pltpu.VMEM((width, units), BF),
            pltpu.VMEM((shared, width), BF),
            pltpu.SemaphoreType.DMA((pieces + len(tiles_of(units, 512)) + 1 + len(split),)),
        ],
        input_output_aliases={first + at: 2 + at for at in range(len(kept))},
        compiler_params=params(48),
        cost_estimate=cost(time),
        name="back_units",
    )(ring.core, *parts, weight_out, weight_down, *kept)


UNIT_TILE = 512


def units_kernel(pieces, which, experts, count, me_ref, place, *refs):
    parts, refs = refs[:pieces], refs[pieces:]
    wi_hbm, wg_hbm, wu_hbm, back_e_hbm, back_s_hbm = refs[:5]
    refs = refs[-(2 * count + 9) :]
    small_ref = refs[0]
    kept_hbm, kept_ref = refs[1 : 1 + count], refs[1 + count : 1 + 2 * count]
    hid_e_ref, hid_s_ref, both_ref, both_s_ref = kept_ref[:4]
    h_ref, wi_ref, wg_ref, wu_ref, back_e_ref, back_s_ref, sum_ref, sems = refs[-8:]
    rows = h_ref.shape[0]
    width, units = wi_ref.shape[0], wi_ref.shape[1] // 2
    me = me_ref[0]
    copies = Copies(sems)
    brought = bring(copies, parts, h_ref)
    tiles = tiles_of(units, UNIT_TILE)
    of_e = []
    for a, b in tiles:
        of_e.append(
            (
                copies.start(wi_hbm.at[:, a:b], wi_ref.at[:, 2 * a : a + b]),
                copies.start(wi_hbm.at[:, units + a : units + b], wi_ref.at[:, a + b : 2 * b]),
            )
        )
        if a == 0:
            of_back_e = copies.start(back_e_hbm, back_e_ref)
    of_s = [
        copies.start(wg_hbm, wg_ref),
        copies.start(wu_hbm, wu_ref),
        copies.start(back_s_hbm, back_s_ref),
    ]
    chunk = slice(which * rows, (which + 1) * rows)
    started = []

    def keep(*places):
        for at in places:
            started.append(copies.start(kept_ref[at], kept_hbm[at].at[chunk]))

    def scale_of(low, high):
        aux = h_ref[:, width:].astype(F32)
        lane = lax.broadcasted_iota(jnp.int32, aux.shape, 1)
        return jnp.sum(jnp.where((lane == low) | (lane == high), aux, 0.0), 1, keepdims=True)

    for copy in brought:
        copy.wait()
    put_split(place, h_ref, kept_ref[4:])
    keep(*range(4, count))
    gate = scale_of(me, experts + me)
    h = h_ref[:, :width]
    sum_ref[...] = jnp.zeros_like(sum_ref)
    for which_tile, (a, b) in enumerate(tiles):
        for copy in of_e[which_tile]:
            copy.wait()
        if a == 0:
            of_back_e.wait()
        both = plain_dot(h, wi_ref[:, 2 * a : 2 * b])
        back = back_e_ref[:, a:b].astype(F32)
        hidden, scaled, da, db = gated(both[:, : b - a], both[:, b - a :], back, gate)
        products = hidden * back
        for low in range(0, b - a, 128):
            sum_ref[...] += products[:, low : low + 128]
        hid_e_ref[:, a:b] = scaled.astype(BF)
        both_ref[:, a:b] = da.astype(BF)
        both_ref[:, units + a : units + b] = db.astype(BF)
    keep(0, 2)
    for copy in of_s:
        copy.wait()
    switch = scale_of(2 * experts, 3 * experts)
    back = back_s_ref[...].astype(F32)
    hidden, scaled, dg, du = gated(
        right_dot(h, wg_ref[...]), right_dot(h, wu_ref[...]), back, switch
    )
    hid_s_ref[...] = jnp.zeros_like(hid_s_ref)
    hid_s_ref[:, : scaled.shape[1]] = scaled.astype(BF)
    shared = dg.shape[1]
    both_s_ref[:, :shared] = dg.astype(BF)
    both_s_ref[:, shared:] = du.astype(BF)
    keep(1, 3)
    of_switch = jnp.sum(hidden * back, 1, keepdims=True)
    of_gate = jnp.sum(sum_ref[...], 1, keepdims=True)
    lane = lax.broadcasted_iota(jnp.int32, small_ref.shape, 1)
    small = jnp.zeros(small_ref.shape, F32)
    for value, first in ((of_gate, 0), (of_switch, 2 * experts)):
        high = value.astype(BF).astype(F32)
        small = small + jnp.where(lane == first + me, high, 0.0)
        small = small + jnp.where(lane == first + experts + me, value - high, 0.0)
    small_ref[...] = small.astype(BF)
    for copy in started:
        copy.wait()


def hidden_units(
    ring, which, me, experts, parts, weight_in, weight_gate, weight_up, back_e, back_s, kept,
    time=6,
):
    rows, units = back_e.shape
    shared = back_s.shape[1]
    width = weight_in.shape[0]
    pieces = len(parts)
    first = pieces + 7
    columns = [units, -(-shared // 128) * 128, 2 * units, 2 * shared]
    columns += [part.shape[1] for part in split_shapes(rows, width)]
    copies = pieces + 2 * len(tiles_of(units, UNIT_TILE)) + 4 + len(columns)
    return pl.pallas_call(
        functools.partial(units_kernel, pieces, which, experts, len(columns)),
        out_shape=(jax.ShapeDtypeStruct((rows, 128), BF),)
        + tuple(jax.ShapeDtypeStruct((rows * ring.half, c), BF) for c in columns),
        in_specs=[SCALARS] * 2 + [ANY] * (pieces + 5 + len(kept)),
        out_specs=(WHOLE,) + (ANY,) * len(columns),
        scratch_shapes=[pltpu.VMEM((rows, c), BF) for c in columns]
        + [
            pltpu.VMEM((rows, width + 128), BF),
            pltpu.VMEM((width, 2 * units), BF),
            pltpu.VMEM((shared, width), BF),
            pltpu.VMEM((shared, width), BF),
            pltpu.VMEM((rows, units), BF),
            pltpu.VMEM((rows, shared), BF),
            pltpu.VMEM((rows, 128), F32),
            pltpu.SemaphoreType.DMA((copies,)),
        ],
        input_output_aliases={first + at: 1 + at for at in range(len(kept))},
        compiler_params=params(52),
        cost_estimate=cost(time),
        name="hidden_units",
    )(
        me,
        ring.core,
        *parts,
        weight_in,
        weight_gate,
        weight_up,
        back_e,
        back_s,
        *kept,
    )


IN_TILE = 512


def units_in_kernel(
    which, both_hbm, both_s_hbm, small_ref, wi_hbm, wg_hbm, wu_hbm, out_ref,
    both_ref, both_s_ref, wi_ref, ws_ref, sems,
):
    rows = both_ref.shape[0]
    width, shared = wi_ref.shape[0], ws_ref.shape[0] // 2
    copies = Copies(sems)
    chunk = slice(which * rows, (which + 1) * rows)
    brought = [
        copies.start(both_hbm.at[chunk], both_ref),
        copies.start(both_s_hbm.at[chunk], both_s_ref),
    ]
    tiles = tiles_of(width, IN_TILE)
    weights = [
        [
            copies.start(wi_hbm.at[a:b], wi_ref.at[a:b]),
            copies.start(wg_hbm.at[:, a:b], ws_ref.at[:shared, a:b]),
            copies.start(wu_hbm.at[:, a:b], ws_ref.at[shared:, a:b]),
        ]
        for a, b in tiles
    ]
    out_ref[:, width:] = small_ref[...]
    for copy in brought:
        copy.wait()
    for started, (a, b) in zip(weights, tiles):
        for copy in started:
            copy.wait()
        out = right_dot(both_ref[...], wi_ref[a:b])
        out = out + plain_dot(both_s_ref[...], ws_ref[:, a:b])
        out_ref[:, a:b] = out.astype(BF)


def units_in(which, both, both_s, small, weight_in, weight_gate, weight_up, time):
    joined, joined_s = both.shape[1], both_s.shape[1]
    rows = small.shape[0]
    width = weight_in.shape[0]
    return pl.pallas_call(
        functools.partial(units_in_kernel, which),
        out_shape=jax.ShapeDtypeStruct((rows, width + 128), BF),
        in_specs=[ANY] * 2 + [WHOLE] + [ANY] * 3,
        out_specs=WHOLE,
        scratch_shapes=[
            pltpu.VMEM((rows, joined), BF),
            pltpu.VMEM((rows, joined_s), BF),
            pltpu.VMEM((width, joined), BF),
            pltpu.VMEM((joined_s, width), BF),
            pltpu.SemaphoreType.DMA((2 + 3 * len(tiles_of(width, IN_TILE)),)),
        ],
        compiler_params=params(48),
        cost_estimate=cost(time),
        name="units_in",
    )(both, both_s, small, weight_in, weight_gate, weight_up)


def pair_kernel(pairs, first_rows, outs, turned_rows, *refs):
    adds = len(first_rows)
    lefts_hbm, rights_hbm = refs[:pairs], refs[pairs : 2 * pairs]
    refs = refs[2 * pairs :]
    adds_hbm, outs_hbm = refs[:adds], refs[adds : adds + outs]
    refs = refs[adds + outs :]
    lefts_ref, rights_ref = refs[:pairs], refs[pairs : 2 * pairs]
    refs = refs[2 * pairs :]
    adds_ref, outs_ref = refs[:adds], refs[adds : adds + outs]
    copies = Copies(refs[-1])
    rows = lefts_ref[0].shape[1]
    tiles = pair_tiles([ref.shape[1] for ref in rights_ref], 1 if turned_rows else outs)
    of_lefts = [None] * pairs
    of_tiles = []
    for pair, low, a, b in tiles:
        if of_lefts[pair] is None:
            of_lefts[pair] = copies.start(lefts_hbm[pair], lefts_ref[pair])
        near = slice(a - low, b - low)
        started = [copies.start(rights_hbm[pair].at[:, near], rights_ref[pair].at[:, near])]
        for first, hbm, ref in zip(first_rows, adds_hbm, adds_ref):
            started.append(copies.start(hbm.at[first : first + rows, a:b], ref.at[:, a:b]))
        of_tiles.append(started)
    started = []
    for at, (pair, low, a, b) in enumerate(tiles):
        if of_lefts[pair] is not None:
            of_lefts[pair].wait()
            of_lefts[pair] = None
        for copy in of_tiles[at]:
            copy.wait()
        out = left_dot(lefts_ref[pair][...], rights_ref[pair][:, a - low : b - low])
        for ref in adds_ref:
            out = out + ref[:, a:b].astype(F32)
        if turned_rows:
            out = out.T
            for which, target in enumerate(outs_ref):
                low = which * turned_rows
                first, last = max(a, low), min(b, low + turned_rows)
                if first < last:
                    target[first - low : last - low] = out[first - a : last - a]
            continue
        wide = outs_ref[0].shape[1]
        target, hbm = outs_ref[a // wide], outs_hbm[a // wide]
        near = slice(a % wide, a % wide + b - a)
        target[:, near] = out.astype(target.dtype)
        started.append(copies.start(target.at[:, near], hbm.at[:, near]))
    if turned_rows:
        started = [copies.start(target, hbm) for target, hbm in zip(outs_ref, outs_hbm)]
    for copy in started:
        copy.wait()


def pair_tiles(widths, outs):
    wide = sum(widths) // outs
    tiles, low = [], 0
    for pair, width in enumerate(widths):
        a = low
        while a < low + width:
            b = min(a + 512, low + width, (a // wide + 1) * wide)
            tiles.append((pair, low, a, b))
            a = b
        low += width
    return tiles


def pair_dot(lefts, rights, adds, held, outs=1, time=0, turned_rows=0):
    length, rows = lefts[0].shape
    widths = [right.shape[1] for right in rights]
    columns = sum(widths)
    tiles = len(pair_tiles(widths, 1 if turned_rows else outs))
    pairs = len(lefts)
    shape = (turned_rows, rows) if turned_rows else (rows, columns // outs)
    return pl.pallas_call(
        functools.partial(
            pair_kernel, pairs, [first for _, first in adds], outs, turned_rows
        ),
        out_shape=(jax.ShapeDtypeStruct(shape, held),) * outs,
        in_specs=[ANY] * (2 * pairs + len(adds)),
        out_specs=(ANY,) * outs,
        scratch_shapes=[pltpu.VMEM((length, rows), BF)] * pairs
        + [pltpu.VMEM((length, width), BF) for width in widths]
        + [pltpu.VMEM((rows, columns), BF)] * len(adds)
        + [pltpu.VMEM(shape, held)] * outs
        + [pltpu.SemaphoreType.DMA((pairs + outs + tiles * (2 + len(adds)),))],
        compiler_params=params(52),
        cost_estimate=cost(time),
        name="pair_dot",
    )(*lefts, *rights, *[values for values, _ in adds])


def layer_kernel(low, he_hbm, hs_hbm, wo_hbm, wd_hbm, out_ref, he_ref, hs_ref, wo_ref, wd_ref, sems):
    rows = slice(low, low + he_ref.shape[0])
    copies = Copies(sems)
    brought = [
        copies.start(he_hbm.at[rows], he_ref),
        copies.start(hs_hbm.at[rows], hs_ref),
    ]
    tiles = tiles_of(wo_ref.shape[0], IN_TILE)
    weights = [
        (
            copies.start(wo_hbm.at[a:b], wo_ref.at[a:b]),
            copies.start(wd_hbm.at[:, a:b], wd_ref.at[:, a:b]),
        )
        for a, b in tiles
    ]
    for copy in brought:
        copy.wait()
    for started, (a, b) in zip(weights, tiles):
        for copy in started:
            copy.wait()
        out = right_dot(he_ref[...], wo_ref[a:b]) + plain_dot(hs_ref[:, : wd_ref.shape[0]], wd_ref[:, a:b])
        out_ref[:, a:b] = out.astype(BF)


def layer_part(low, high, hid_e, hid_s, weight_out, weight_down, time):
    width, units = weight_out.shape
    shared = weight_down.shape[0]
    rows = high - low
    return pl.pallas_call(
        functools.partial(layer_kernel, low),
        out_shape=jax.ShapeDtypeStruct((rows, width), BF),
        in_specs=[ANY] * 4,
        out_specs=WHOLE,
        scratch_shapes=[
            pltpu.VMEM((rows, units), BF),
            pltpu.VMEM((rows, hid_s.shape[1]), BF),
            pltpu.VMEM((width, units), BF),
            pltpu.VMEM((shared, width), BF),
            pltpu.SemaphoreType.DMA((2 + 2 * len(tiles_of(width, IN_TILE)),)),
        ],
        compiler_params=params(48),
        cost_estimate=cost(time),
        name="layer_part",
    )(hid_e, hid_s, weight_out, weight_down)


def routing_kernel(
    experts, x_ref, own_ref, ahead_ref, behind_ref, gain_ref, head_ref, picked_ref,
    residual_ref, sent_ref, routing_ref,
):
    width = x_ref.shape[1]
    residual = x_ref[...].astype(F32) + own_ref[...].astype(F32)
    residual = residual + ahead_ref[...].astype(F32) + behind_ref[...].astype(F32)
    h = (residual * rms_scale(residual) * gain_ref[...].astype(F32)).astype(BF)
    scores = right_dot(h, head_ref[...])
    lane = lax.broadcasted_iota(jnp.int32, scores.shape, 1)
    is_expert = lane < experts
    raised = jnp.where(is_expert, scores, -jnp.inf)
    raised = jnp.exp(raised - jnp.max(raised, 1, keepdims=True))
    probs = raised / jnp.sum(raised, 1, keepdims=True)
    switch = jnp.where(lane == 2 * experts, 1.0 / (1.0 + jnp.exp(-scores)), 0.0)
    values = probs * picked_ref[...] + switch
    high = values.astype(BF).astype(F32)
    rest = pltpu.roll(values - high, experts, 1)
    residual_ref[...] = residual
    routing_ref[...] = probs + switch
    sent_ref[:, :width] = h
    sent_ref[:, width:] = (high + rest).astype(BF)


def routing(experts, x, own, ahead, behind, gain, head, picked, time=0):
    rows, width = x.shape
    return pl.pallas_call(
        functools.partial(routing_kernel, experts),
        out_shape=(
            jax.ShapeDtypeStruct((rows, width), F32),
            jax.ShapeDtypeStruct((rows, width + 128), BF),
            jax.ShapeDtypeStruct((rows, 128), F32),
        ),
        in_specs=[WHOLE] * 7,
        out_specs=(WHOLE,) * 3,
        compiler_params=params(40),
        cost_estimate=cost(time),
        name="routing",
    )(x, own, ahead, behind, gain, head, picked)


def shards(
    tokens,
    attention_gain,
    query_weight,
    query_bias,
    key_weight,
    key_bias,
    value_weight,
    value_bias,
    output_weight,
    feedforward_gain,
    shared_gate_weight,
    shared_up_weight,
    shared_down_weight,
    shared_switch,
    router_weight,
    expert_in,
    expert_out,
    routes,
    cotangent,
):
    tok_rows, model_width = tokens.shape
    groups = lax.axis_size("expert")
    me = lax.axis_index("expert").astype(jnp.int32)[None]
    ring = Ring(groups)
    length = tok_rows * groups
    experts = router_weight.shape[1]
    weight_in = expert_in[0]
    weight_out = expert_out[0]
    weight_gate = shared_gate_weight.T
    weight_up = shared_up_weight.T
    weight_down = shared_down_weight.T
    x_float = tokens.astype(F32)
    rms_attn = rms_scale(x_float)
    unit_attn = x_float * rms_attn
    gain_attn = attention_gain.astype(F32)
    h_attn = (unit_attn * gain_attn).astype(BF)

    lanes = jnp.arange(128, dtype=jnp.int32)
    picked = jnp.sum((routes[:, :, None] == lanes).astype(F32), 1)
    head = jnp.concatenate(
        [
            router_weight.T,
            jnp.zeros((experts, model_width), BF),
            shared_switch[None],
            jnp.zeros((127 - 2 * experts, model_width), BF),
        ],
        0,
    )

    gather_attn = Gather(ring, h_attn)
    last = gather_attn.step()
    tables = rope_tables(length)
    last = gather_attn.step(tables, head, picked)
    h_attn_parts = gather_attn.rest()
    gather_cot = Gather(ring, after(cotangent, *gather_attn.pieces[-2:]))
    of_cot = gather_cot.step()

    q_rot, k_rot, v_low, *h_attn_split, h_attn_all = project(
        ring,
        h_attn_parts,
        (query_weight, key_weight, value_weight),
        (query_bias, key_bias, value_bias),
        tables,
    )
    att_low = attend(ring, q_rot, k_rot, v_low)
    sum_att = Scatter(
        ring, [right_dot(after(att_low, of_cot), output_weight).astype(BF)], tok_rows
    )
    backs = []
    cotangent_split = []

    def next_back(*others):
        which = len(backs)
        parts = after(gather_cot.chunk(which), *others)
        new = back_units(ring, which, parts, weight_out, weight_down, cotangent_split)
        cotangent_split[:] = new[2:]
        backs.append(new[:2])
        return new[:2]

    befores = [sum_att.chunks, move(ring, [sum_att, gather_cot])]
    while sum_att.at:
        busy = next_back(befores[-2])
        rounds = [sum_att] + [gather_cot] * (gather_cot.at < ring.half)
        befores.append(move(ring, rounds, busy))
    busy = next_back(befores[-2])

    residual, h_sent, routed = routing(
        experts,
        tokens,
        sum_att.own(0),
        sum_att.ahead,
        after(sum_att.behind, busy),
        feedforward_gain[None],
        head,
        picked,
    )
    gain_ffn = feedforward_gain.astype(F32)

    gather_ffn = Gather(ring, h_sent)
    last = gather_ffn.step()
    busy = ()
    smalls = []
    kept = []

    def next_units(*others):
        which = len(smalls)
        parts = after(gather_ffn.chunk(which), *others)
        small, *new = hidden_units(
            ring,
            which,
            me,
            experts,
            parts,
            weight_in,
            weight_gate,
            weight_up,
            *backs[which],
            kept,
        )
        kept[:] = new
        smalls.append(small)
        return small

    while gather_ffn.at < ring.half:
        last = gather_ffn.step(busy)
        busy = next_units()
    next_units()
    hid_e, hid_s, grad_joined, grad_shared, *h_ffn_split = kept

    def chunk_in(which, time, *others):
        return units_in(
            which,
            *after((grad_joined, grad_shared), *others),
            smalls[which],
            weight_in,
            weight_gate,
            weight_up,
            time,
        )

    out_e = PairSum([cotangent_split], [hid_e])
    out_s = PairSum([cotangent_split], [hid_s])
    in_e = PairSum([h_ffn_split], [grad_joined])
    in_s = PairSum([h_ffn_split], [grad_shared])
    half_rows = length // 2

    def layer_rows(low, time, *others):
        return layer_part(
            low, low + half_rows, *after((hid_e, hid_s), *others), weight_out, weight_down, time
        )

    chunks = [None] * ring.half
    layer_parts = [None, None]
    busy = in_e.cores()
    chunks[-1] = chunk_in(ring.half - 1, 70, busy)
    sum_ffn = Scatter(ring, chunks, tok_rows)
    befores = [chunks[-1], sum_ffn.step()]
    busy = chunks[-1]
    works = [(6, in_e.chips), (6, out_e.cores), (12, out_s.cores)]
    for at, which in enumerate(range(ring.half - 2, -1, -1)):
        time, work = works[at] if at < len(works) else (6, None)
        chunks[which] = chunk_in(which, time, busy, befores[-2])
        busy = chunks[which]
        if work is not None:
            busy = (busy, work(busy))
        befores.append(sum_ffn.step(busy))
    layer_parts[1] = layer_rows(half_rows, 12, befores[-2], busy)
    grad_sum = sum_ffn.rest(layer_parts[1])

    rms_ffn = rms_scale(residual)
    unit_ffn = residual * rms_ffn
    small = grad_sum[:, model_width:]
    router_probs = routed[:, :experts]
    switch = routed[:, 2 * experts]
    grad_probs = picked[:, :experts] * (small[:, :experts] + small[:, experts : 2 * experts])
    grad_logits = router_probs * (
        grad_probs - jnp.sum(router_probs * grad_probs, -1, keepdims=True)
    )
    grad_switch = jnp.sum(small[:, 2 * experts : 4 * experts], 1) * switch * (1.0 - switch)
    h_float = h_sent[:, :model_width].astype(F32)
    grad_ffn = grad_sum[:, :model_width]
    grad_ffn = grad_ffn + jnp.dot(grad_logits, router_weight.astype(F32).T, precision=HIGHEST)
    grad_ffn = grad_ffn + grad_switch[:, None] * shared_switch.astype(F32)
    grad_out = cotangent.astype(F32)
    grad_unit_ffn = grad_ffn * gain_ffn
    grad_residual = grad_out + rms_ffn * (
        grad_unit_ffn - unit_ffn * jnp.mean(grad_unit_ffn * unit_ffn, -1, keepdims=True)
    )
    attention_grad = grad_residual.astype(BF)

    gather_grad = Gather(ring, attention_grad)
    first = gather_grad.step()
    layer_parts[0] = layer_rows(0, 12, attention_grad)
    busy = out_e.chips(layer_parts[0])
    second = gather_grad.step(busy)
    totals = in_e.total(first, busy, time=7.5)
    busy = out_s.chips(totals)
    third = gather_grad.step(busy)
    busy = in_s.cores(second, busy, time=7.5)
    last = gather_grad.step(busy)
    while gather_grad.at < ring.half:
        last = gather_grad.step()
    attention_grad_parts = gather_grad.rest()
    sum_layer = Scatter(ring, layer_parts, tok_rows)
    of_layer = sum_layer.step(last)
    grad_att, *grad_split = reorder_dot(
        ring, after(attention_grad_parts, totals), output_weight
    )
    grads, biases = attend_back(ring, q_rot, k_rot, v_low, grad_att, tables)
    attn_part, gain_part = attend_in(
        after(grads, of_layer),
        (query_weight, key_weight, value_weight),
        h_attn_all,
        gain_attn[None],
    )
    sum_attn = Scatter(ring, [attn_part], tok_rows)
    first = move(ring, [sum_attn, sum_layer])

    grad_router_part = jnp.dot(grad_logits.T, h_float, precision=HIGHEST)
    grad_switch_row = jnp.dot(grad_switch, h_float, precision=HIGHEST)
    grad_ffn_gain_part = jnp.sum(grad_ffn * unit_ffn, 0)
    sums = jnp.concatenate(
        [gain_part, grad_switch_row[None], grad_ffn_gain_part[None], grad_router_part], 0
    )
    in_qkvo = PairSum([h_attn_split, grad_split], [grads, att_low])
    packed = jnp.concatenate([sums.reshape(-1), biases[0]]).reshape(-1, 128)
    for axis, moves in cube_steps("dp"):
        packed = packed + lax.ppermute(packed, axis, moves)
    totals += out_e.total(attn_part, time=6)
    busy = in_qkvo.cores(totals)
    sums = packed.reshape(-1)[: sums.size].reshape(sums.shape)
    rounds = [sum_attn, sum_layer]
    befores = [attn_part, first]
    shared_cols = shared_gate_weight.shape[1]
    while sum_layer.at:
        befores.append(move(ring, rounds, busy))
        if len(befores) == 3:
            busy = in_s.chips(befores[-2], busy, time=6)
            totals += out_s.total(busy, turned_rows=shared_cols)
            busy = totals
        elif len(befores) == 4:
            busy = in_qkvo.chips(befores[-2], totals, time=6)
    last = sum_attn.step()
    totals += in_s.total(befores[-1], busy, time=3, outs=2, turned_rows=shared_cols)
    while sum_attn.at:
        last = sum_attn.step()
    for axis, moves in cube_steps("expert"):
        sums = sums + lax.ppermute(after(sums, last), axis, moves)
    biases = packed.reshape(-1)[sums.size :].reshape(3, -1)

    layer_out = (residual + sum_layer.rest()).astype(BF)
    grad_attn_in = sum_attn.rest()
    grad_unit_attn = grad_attn_in * gain_attn
    grad_tokens = grad_residual + rms_attn * (
        grad_unit_attn - unit_attn * jnp.mean(grad_unit_attn * unit_attn, -1, keepdims=True)
    )
    qkv = in_qkvo.total(last, outs=4)
    return (
        layer_out,
        grad_tokens,
        sums[0],
        qkv[0],
        biases[0],
        qkv[1],
        biases[1],
        qkv[2],
        biases[2],
        qkv[3],
        sums[2],
        totals[3].T,
        totals[4].T,
        totals[2].T,
        sums[1],
        sums[3:].T,
        totals[0][None],
        totals[1][None],
    )


def solution(mesh):
    return jax.shard_map(
        shards,
        mesh=mesh,
        in_specs=(
            P(("dp", "expert"), None),
            P(),
            P(None, "expert"),
            P("expert"),
            P(None, "expert"),
            P("expert"),
            P(None, "expert"),
            P("expert"),
            P(None, "expert"),
            P(),
            P(None, "expert"),
            P(None, "expert"),
            P(None, "expert"),
            P(),
            P(),
            P("expert", None, None),
            P("expert", None, None),
            P(("dp", "expert"), None),
            P(("dp", "expert"), None),
        ),
        out_specs=(
            P(("dp", "expert"), None),
            P(("dp", "expert"), None),
            P(),
            P("dp", "expert"),
            P("expert"),
            P("dp", "expert"),
            P("expert"),
            P("dp", "expert"),
            P("expert"),
            P("dp", "expert"),
            P(),
            P("dp", "expert"),
            P("dp", "expert"),
            P("dp", "expert"),
            P(),
            P(),
            P("expert", "dp", None),
            P("expert", "dp", None),
        ),
        check_vma=False,
    )
```

time: 679 us -> 517 us (0.76)
  Pallas kernels: 53.8 us -> 243 us
  matrix products: 145 us -> 4.3 us
  waiting for transfers between devices: 256 us -> 137 us
  starting transfers between devices: 104 us -> 68.6 us
  local copies, waits for them, and re-layouts: 58.3 us -> 23.9 us
  other arithmetic: 48.3 us -> 33 us
    pallas_call x4 -> x33, Pallas kernels: 41.8 us -> 230 us  [the longest x15 89.4 us: pair_dot(): pl.pallas_call(functools.partial(pair_kernel, pairs, [first for _, first...]
    ppermute x112 -> x67, waiting for transfers between devices: 256 us -> 137 us  [the longest x26 73.1 us: move(): ahead = lax.ppermute(up, 'expert', ring.forward)]
    dot_general x26 -> x0, matrix products: 75.9 us -> none  [the longest x20 58.7 us: left_dot(): lax.dot_general(left_side, right_side, (((0,), (0,)), ((), ())), preferre...]
    dot_general x9 -> x1, matrix products: 65.5 us -> 1.29 us  [right_dot(): lax.dot_general(left_side, right_side, (((1,), (1,)), ((), ())), preferre...]
    ppermute x112 -> x67, starting transfers between devices: 104 us -> 68.6 us  [the longest x26 28.4 us: move(): ahead = lax.ppermute(up, 'expert', ring.forward)]
    unnamed x260 -> x186, local copies, waits for them, and re-layouts: 29.4 us -> 14.8 us
    add x27 -> x6, other arithmetic: 12.1 us -> 0.27 us  [the longest x1 0.18 us: rest(): after(self.own(0), *others).astype(F32) + self.ahead.astype(F32)]
    slice x20 -> x27, local copies, waits for them, and re-layouts: 14.5 us -> 6.38 us  [the longest x4 2.35 us: outgoing(): down[:middle]]
  transfers between devices with their start and end apart: 112 -> 67, of which waited for: 54 -> 31; matrix products, arithmetic and copies ran while one was open for 29% -> 7% of each run, Pallas kernels for 3% -> 42%
where the time goes in v2:
time: 517 us; the launch traced here: 512 us
  Pallas kernels  243 us (47%)
  waiting for transfers between devices  137 us (26%)
  starting transfers between devices  68.6 us (13%)
  other arithmetic  33 us (6%)
  local copies, waits for them, and re-layouts  23.9 us (5%)
    pallas_call x15, Pallas kernels, pair_dot(): pl.pallas_call(functools.partial(pair_kernel, pairs, [first for _, first...  89.4 us
    ppermute x26, waiting for transfers between devices, move(): ahead = lax.ppermute(up, 'expert', ring.forward)  73.1 us
    pallas_call x4, Pallas kernels, hidden_units(): pl.pallas_call(functools.partial(units_kernel, pieces, which, experts, le...  44.4 us
    ppermute x26, waiting for transfers between devices, move(): behind = lax.ppermute(down, 'expert', ring.backward)  35.3 us
    pallas_call x4, Pallas kernels, units_in(): pl.pallas_call(functools.partial(units_in_kernel, which), out_shape=jax.S...  32.8 us
    ppermute x26, starting transfers between devices, move(): ahead = lax.ppermute(up, 'expert', ring.forward)  28.4 us
    ppermute x26, starting transfers between devices, move(): behind = lax.ppermute(down, 'expert', ring.backward)  27.4 us
    pallas_call x4, Pallas kernels, back_units(): pl.pallas_call(functools.partial(back_kernel, pieces, which, len(split)),...  24.6 us
  transfers between devices with their start and end apart: 67, of which 31 were waited for; matrix products, arithmetic and copies ran while one was open for 7% of the time, Pallas kernels for 42%

profile of v2, /device:TPU:0, one launch (start us, length us, event | category | flops | bytes accessed | tf_op | source)
XLA Modules:
  0.0 512.0 jit_solution(4562652631881203866)
XLA Ops:
  10.8 7.9 %collective-permute-done.refs_0_ = bf16[128,2048]{1,0:T(8,128)(2,1)S(1)} collective-permute-done((bf16[128,2048]{1,0:T(8,128)(2,1)S(1)}, bf16[128,2048]{1,0:T(8,128)(2,1)S(1)}, u32[]{:S(2)}, u32[]{:S(2)}) %collective-permute-start) | collective-permute-done | bytes 524320 | tf_op jit(solution)/shard_map/ppermute | solution.py:98
  22.4 10.4 %collective-permute-done.2.refs_2_ = bf16[128,2048]{1,0:T(8,128)(2,1)S(1)} collective-permute-done((bf16[128,2048]{1,0:T(8,128)(2,1)S(1)}, bf16[128,2048]{1,0:T(8,128)(2,1)S(1)}, u32[]{:S(2)}, u32[]{:S(2)}) %collective-permute-start.2) | collective-permute-done | bytes 524320 | tf_op jit(solution)/shard_map/ppermute | solution.py:98
  37.5 8.0 %collective-permute-done.4.refs_4_ = bf16[128,2048]{1,0:T(8,128)(2,1)S(1)} collective-permute-done((bf16[128,2048]{1,0:T(8,128)(2,1)S(1)}, bf16[128,2048]{1,0:T(8,128)(2,1)S(1)}, u32[]{:S(2)}, u32[]{:S(2)}) %collective-permute-start.4) | collective-permute-done | bytes 524320 | tf_op jit(solution)/shard_map/ppermute | solution.py:98
  58.9 10.0 %project.1 = (bf16[1024,256]{1,0:T(8,128)(2,1)S(1)}, bf16[1024,256]{1,0:T(8,128)(2,1)S(1)}, bf16[1024,256]{1,0:T(8,128)(2,1)}, bf16[1024,1024]{1,0:T(8,128)(2,1)...) custom-call(s32[8]{0:T(128)S(1)} %gather_fusion, s32[2]{0:T(128)S(1)} %pad_add_fusion.place, ...), custom_call_target="tpu_custom_call" | custom-call | flops 3000000000 | bytes 1 | tf_op jit(solution)/shard_map/project/pallas_call | solution.py:347
  102.7 13.0 %collective-permute-done.13 = bf16[256,2048]{1,0:T(8,128)(2,1)S(1)} collective-permute-done((bf16[256,2048]{1,0:T(8,128)(2,1)S(1)}, bf16[256,2048]{1,0:T(8,128)(2,1)S(1)}, u32[]{:S(2)}, u32[]{:S(2)}) %collective-permute-start.13) | collective-permute-done | bytes 1048608 | tf_op jit(solution)/shard_map/ppermute | solution.py:99
  126.4 7.5 %collective-permute-done.14 = bf16[192,2048]{1,0:T(8,128)(2,1)} collective-permute-done((bf16[192,2048]{1,0:T(8,128)(2,1)S(1)}, bf16[192,2048]{1,0:T(8,128)(2,1)}, u32[]{:S(2)}, u32[]{:S(2)}) %collective-permute-start.14) | collective-permute-done | bytes 786464 | tf_op jit(solution)/shard_map/ppermute | solution.py:98
  159.2 8.9 %collective-permute-done.18.refs_0_ = bf16[128,2176]{1,0:T(8,128)(2,1)S(1)} collective-permute-done((bf16[128,2176]{1,0:T(8,128)(2,1)S(1)}, bf16[128,2176]{1,0:T(8,128)(2,1)S(1)}, u32[]{:S(2)}, u32[]{:S(2)}) %collective-permute-start.18) | collective-permute-done | bytes 557088 | tf_op jit(solution)/shard_map/ppermute | solution.py:98
  170.5 11.1 %hidden_units.4 = (bf16[256,128]{1,0:T(8,128)(2,1)S(1)}, bf16[1024,1408]{1,0:T(8,128)(2,1)}, bf16[1024,768]{1,0:T(8,128)(2,1)}, bf16[1024,2816]{1,0:T(8,128)(2,1...) custom-call(s32[1]{0:T(128)} %bitcast.6.me_ref, ...), custom_call_target="tpu_custom_call" | custom-call | flops 6000000000 | bytes 1 | tf_op jit(solution)/shard_map/hidden_units/pallas_call | solution.py:772
  183.7 11.1 %hidden_units.5 = (bf16[256,128]{1,0:T(8,128)(2,1)S(1)}, bf16[1024,1408]{1,0:T(8,128)(2,1)}, bf16[1024,768]{1,0:T(8,128)(2,1)}, bf16[1024,2816]{1,0:T(8,128)(2,1...) custom-call(s32[1]{0:T(128)} %bitcast.6.me_ref, ...), custom_call_target="tpu_custom_call", output_to_operand_aliasing={{1}: (9, {}), {2}: (10, {}), {3}: (11, {}), {4}: (12, {}), ... | custom-call | flops 6000000000 | bytes 1 | tf_op jit(solution)/shard_map/hidden_units/pallas_call | solution.py:772
  196.9 11.1 %hidden_units.6 = (bf16[256,128]{1,0:T(8,128)(2,1)S(1)}, bf16[1024,1408]{1,0:T(8,128)(2,1)}, bf16[1024,768]{1,0:T(8,128)(2,1)}, bf16[1024,2816]{1,0:T(8,128)(2,1...) custom-call(s32[1]{0:T(128)} %bitcast.6.me_ref, ...), custom_call_target="tpu_custom_call", output_to_operand_aliasing={{1}: (9, {}), {2}: (10, {}), {3}: (11, {}), {4}: (12, {}), ... | custom-call | flops 6000000000 | bytes 1 | tf_op jit(solution)/shard_map/hidden_units/pallas_call | solution.py:772
  208.0 11.2 %hidden_units.7 = (bf16[256,128]{1,0:T(8,128)(2,1)S(1)}, bf16[1024,1408]{1,0:T(8,128)(2,1)}, bf16[1024,768]{1,0:T(8,128)(2,1)}, bf16[1024,2816]{1,0:T(8,128)(2,1...) custom-call(s32[1]{0:T(128)} %bitcast.6.me_ref, ...), custom_call_target="tpu_custom_call", output_to_operand_aliasing={{1}: (10, {}), {2}: (11, {}), {3}: (12, {}), {4}: (13, {}),... | custom-call | flops 6000000000 | bytes 1 | tf_op jit(solution)/shard_map/hidden_units/pallas_call | solution.py:772
  219.2 11.1 %pair_dot.15 = bf16[1024,2816]{1,0:T(8,128)(2,1)} custom-call(bf16[1024,1024]{1,0:T(8,128)(2,1)} %get-tuple-element.343.refs_0_, bf16[1024,2816]{1,0:T(8,128)(2,1)} %get-tuple-element.321.refs_1_.both_hbm), custom_call_target="tpu_custom_call" | custom-call | flops 1 | bytes 1 | tf_op jit(solution)/shard_map/pair_dot/pallas_call | solution.py:934
  230.4 8.2 %units_in.4 = bf16[256,2176]{1,0:T(8,128)(2,1)S(1)} custom-call(bf16[1024,2816]{1,0:T(8,128)(2,1)} %get-tuple-element.321.refs_1_.both_hbm, bf16[1024,1408]{1,0:T(8,128)(2,1)S(1)} %copy-done, bf16[256,128]{1,0:T(8,128)(2,1)S(1)} %get-tuple-element.305.small_ref, bf16[2048,2816]{1,0:T(8,128)(2,1)} %bitcast.47, bf16[704,2048]{1,0:T(8,128)(2,1)} %bitcast.55, ...), custom_call_target="tpu_custom_call" | custom-call | flops 70000001024 | bytes 1 | tf_op jit(solution)/shard_map/units_in/pallas_call | solution.py:845
  240.8 8.1 %units_in.5 = bf16[256,2176]{1,0:T(8,128)(2,1)S(1)} custom-call(bf16[1024,2816]{1,0:T(8,128)(2,1)} %get-tuple-element.321.refs_1_.both_hbm, bf16[1024,1408]{1,0:T(8,128)(2,1)S(1)} %copy-done, bf16[256,128]{1,0:T(8,128)(2,1)S(1)} %get-tuple-element.308.small_ref, bf16[2048,2816]{1,0:T(8,128)(2,1)} %bitcast.48, bf16[704,2048]{1,0:T(8,128)(2,1)} %bitcast.56, ...), custom_call_target="tpu_custom_call" | custom-call | flops 6000000000 | bytes 1 | tf_op jit(solution)/shard_map/units_in/pallas_call | solution.py:845
  252.5 7.0 %pair_dot.16 = bf16[512,2816]{1,0:T(8,128)(2,1)} custom-call(bf16[1024,512]{1,0:T(8,128)(2,1)S(1)} %copy-done.4, bf16[1024,2816]{1,0:T(8,128)(2,1)} %get-tuple-element.321.refs_1_.both_hbm, bf16[1024,2816]{1,0:T(8,128)(2,1)} %copy-done.58), custom_call_target="tpu_custom_call" | custom-call | flops 1 | bytes 1 | tf_op jit(solution)/shard_map/pair_dot/pallas_call | solution.py:934
  263.0 8.2 %units_in.6 = bf16[256,2176]{1,0:T(8,128)(2,1)S(1)} custom-call(bf16[1024,2816]{1,0:T(8,128)(2,1)} %get-tuple-element.321.refs_1_.both_hbm, bf16[1024,1408]{1,0:T(8,128)(2,1)S(1)} %copy-done, bf16[256,128]{1,0:T(8,128)(2,1)S(1)} %get-tuple-element.276.small_ref, bf16[2048,2816]{1,0:T(8,128)(2,1)} %bitcast.49, bf16[704,2048]{1,0:T(8,128)(2,1)} %bitcast.57, ...), custom_call_target="tpu_custom_call" | custom-call | flops 6000000000 | bytes 1 | tf_op jit(solution)/shard_map/units_in/pallas_call | solution.py:845
  280.3 8.4 %units_in.7 = bf16[256,2176]{1,0:T(8,128)(2,1)S(1)} custom-call(bf16[1024,2816]{1,0:T(8,128)(2,1)} %get-tuple-element.321.refs_1_.both_hbm, bf16[1024,1408]{1,0:T(8,128)(2,1)S(1)} %copy-done, bf16[256,128]{1,0:T(8,128)(2,1)S(1)} %get-tuple-element.264.small_ref, bf16[2048,2816]{1,0:T(8,128)(2,1)} %bitcast.50, bf16[704,2048]{1,0:T(8,128)(2,1)} %bitcast.58, ...), custom_call_target="tpu_custom_call" | custom-call | flops 12000000000 | bytes 1 | tf_op jit(solution)/shard_map/units_in/pallas_call | solution.py:845
  297.0 7.6 %layer_part.2 = bf16[512,2048]{1,0:T(8,128)(2,1)S(1)} custom-call(bf16[1024,1408]{1,0:T(8,128)(2,1)} %get-tuple-element.333.refs_1_.he_hbm, bf16[1024,768]{1,0:T(8,128)(2,1)S(1)} %copy-done.1, bf16[2048,1408]{1,0:T(8,128)(2,1)} %bitcast.78, bf16[704,2048]{1,0:T(8,128)(2,1)} %bitcast.84), custom_call_target="tpu_custom_call" | custom-call | flops 12000000000 | bytes 1 | tf_op jit(solution)/shard_map/layer_part/pallas_call | solution.py:980
  318.5 7.6 %layer_part.3 = bf16[512,2048]{1,0:T(8,128)(2,1)S(1)} custom-call(bf16[1024,1408]{1,0:T(8,128)(2,1)} %get-tuple-element.333.refs_1_.he_hbm, bf16[1024,768]{1,0:T(8,128)(2,1)S(1)} %copy-done.1, bf16[2048,1408]{1,0:T(8,128)(2,1)} %bitcast.79, bf16[704,2048]{1,0:T(8,128)(2,1)} %bitcast.85), custom_call_target="tpu_custom_call" | custom-call | flops 12000000000 | bytes 1 | tf_op jit(solution)/shard_map/layer_part/pallas_call | solution.py:980
  333.6 7.3 %pair_dot.20 = f32[512,2816]{1,0:T(8,128)} custom-call(bf16[1024,512]{1,0:T(8,128)(2,1)S(1)} %copy-done.9, bf16[1024,2816]{1,0:T(8,128)(2,1)} %get-tuple-element.321.refs_1_.both_hbm, bf16[1024,2816]{1,0:T(8,128)(2,1)} %copy-done.58, bf16[512,2816]{1,0:T(8,128)(2,1)} %collective-permute-done.40.refs_3_), custom_call_target="tpu_custom_call" | custom-call | flops 7500000256 | bytes 1 | tf_op jit(solution)/shard_map/pair_dot/pallas_call | solution.py:934
  377.3 7.7 %attend_back.1 = (bf16[1024,768]{1,0:T(8,128)(2,1)S(1)}, f32[1,768]{1,0:T(1,128)S(1)}) custom-call(s32[8]{0:T(128)S(1)} %copy-done.45, bf16[1024,256]{1,0:T(8,128)(2,1)S(1)} %copy-done.48, bf16[1024,256]{1,0:T(8,128)(2,1)S(1)} %copy-done.50, bf16[1024,256]{1,0:T(8,128)(2,1)S(1)} %copy-done.52, bf16[1024,256]{1,0:T(8,128)(2,1)S(1)} %copy-done.54, ...), custom_call_target="tpu_custom_call" | custom-call | flops 20000000000 | bytes 1 | tf_op jit(solution)/shard_map/attend_back/pallas_call | solution.py:482
  424.0 8.3 %collective-permute-done.54.refs_3_ = bf16[512,768]{1,0:T(8,128)(2,1)} collective-permute-done((bf16[512,768]{1,0:T(8,128)(2,1)}, bf16[512,768]{1,0:T(8,128)(2,1)}, u32[]{:S(2)}, u32[]{:S(2)}) %collective-permute-start.54) | collective-permute-done | bytes 786464 | tf_op jit(solution)/shard_map/ppermute | solution.py:217
  450.8 11.4 %collective-permute-done.55 = bf16[256,2048]{1,0:T(8,128)(2,1)} collective-permute-done((bf16[256,2048]{1,0:T(8,128)(2,1)}, bf16[256,2048]{1,0:T(8,128)(2,1)}, u32[]{:S(2)}, u32[]{:S(2)}) %collective-permute-start.55) | collective-permute-done | bytes 1048608 | tf_op jit(solution)/shard_map/ppermute | solution.py:98
  473.7 9.3 %collective-permute-done.66.refs_3_ = bf16[512,1408]{1,0:T(8,128)(2,1)} collective-permute-done((bf16[512,1408]{1,0:T(8,128)(2,1)}, bf16[512,1408]{1,0:T(8,128)(2,1)}, u32[]{:S(2)}, u32[]{:S(2)}) %collective-permute-start.66) | collective-permute-done | bytes 1441824 | tf_op jit(solution)/shard_map/ppermute | solution.py:217
  (437 shorter events, 288.7 us)
Async XLA Ops:
  56.7 18.5 %collective-permute-start.8 = (bf16[128,2048]{1,0:T(8,128)(2,1)S(1)}, bf16[128,2048]{1,0:T(8,128)(2,1)S(1)}, u32[]{:S(2)}, u32[]{:S(2)}) collective-permute-start(bf16[128,2048]{1,0:T(8,128)(2,1)S(1)} %copy-done.21), channel_id=1, source_target_pairs={{0,2},{2,4},{4,6},{6,7},{7,5},{5,3},{3,1},{1,0},{8,10},{10,12},{12... | collective-permute-start | bytes 1572872 | tf_op jit(solution)/shard_map/ppermute | solution.py:98
  57.7 17.6 %collective-permute-start.9 = (bf16[128,2048]{1,0:T(8,128)(2,1)S(1)}, bf16[128,2048]{1,0:T(8,128)(2,1)S(1)}, u32[]{:S(2)}, u32[]{:S(2)}) collective-permute-start(bf16[128,2048]{1,0:T(8,128)(2,1)S(1)} %copy-done.21), channel_id=1, source_target_pairs={{0,1},{2,0},{4,2},{6,4},{7,6},{5,7},{3,5},{1,3},{8,9},{10,8},{12,1... | collective-permute-start | bytes 1572872 | tf_op jit(solution)/shard_map/ppermute | solution.py:99
  94.0 21.7 %collective-permute-start.13 = (bf16[256,2048]{1,0:T(8,128)(2,1)S(1)}, bf16[256,2048]{1,0:T(8,128)(2,1)S(1)}, u32[]{:S(2)}, u32[]{:S(2)}) collective-permute-start(bf16[256,2048]{1,0:T(8,128)(2,1)S(1)} %pad_maximum_fusion.1), channel_id=1, source_target_pairs={{0,1},{2,0},{4,2},{6,4},{7,6},{5,7},{3,5},{1,3},{8,9},{10,8},{12,1... | collective-permute-start | bytes 3145736 | tf_op jit(solution)/shard_map/ppermute | solution.py:99
  94.6 22.9 %collective-permute-start.12 = (bf16[256,2048]{1,0:T(8,128)(2,1)}, bf16[256,2048]{1,0:T(8,128)(2,1)S(1)}, u32[]{:S(2)}, u32[]{:S(2)}) collective-permute-start(bf16[256,2048]{1,0:T(8,128)(2,1)} %pad_maximum_fusion), channel_id=1, source_target_pairs={{0,2},{2,4},{4,6},{6,7},{7,5},{5,3},{3,1},{1,0},{8,10},{10,12},{12... | collective-permute-start | bytes 3145736 | tf_op jit(solution)/shard_map/ppermute | solution.py:98
  120.0 17.7 %collective-permute-start.15 = (bf16[192,2048]{1,0:T(8,128)(2,1)S(1)}, bf16[192,2048]{1,0:T(8,128)(2,1)}, u32[]{:S(2)}, u32[]{:S(2)}) collective-permute-start(bf16[192,2048]{1,0:T(8,128)(2,1)S(1)} %pad_maximum_fusion.9), channel_id=1, source_target_pairs={{0,1},{2,0},{4,2},{6,4},{7,6},{5,7},{3,5},{1,3},{8,9},{10,8},{12,1... | collective-permute-start | bytes 2359304 | tf_op jit(solution)/shard_map/ppermute | solution.py:99
  230.3 19.7 %collective-permute-start.26 = (bf16[1024,2816]{1,0:T(8,128)(2,1)}, bf16[1024,2816]{1,0:T(8,128)(2,1)S(1)}, u32[]{:S(2)}, u32[]{:S(2)}) collective-permute-start(bf16[1024,2816]{1,0:T(8,128)(2,1)} %pair_dot.15), channel_id=1, source_target_pairs={{0,8},{8,0},{16,24},{24,16},{1,9},{9,1},{17,25},{25,17},{2,10},{10... | collective-permute-start | bytes 17301512 | tf_op jit(solution)/shard_map/ppermute | solution.py:205
  259.5 74.2 %collective-permute-start.40 = (bf16[512,2816]{1,0:T(8,128)(2,1)}, bf16[512,2816]{1,0:T(8,128)(2,1)}, u32[]{:S(2)}, u32[]{:S(2)}) collective-permute-start(bf16[512,2816]{1,0:T(8,128)(2,1)} %pair_dot.16), channel_id=1, source_target_pairs={{0,16},{8,24},{16,0},{24,8},{1,17},{9,25},{17,1},{25,9},{2,18},{10... | collective-permute-start | bytes 8650760 | tf_op jit(solution)/shard_map/ppermute | solution.py:217
  261.0 17.0 %collective-permute-start.29 = (bf16[128,2176]{1,0:T(8,128)(2,1)}, bf16[128,2176]{1,0:T(8,128)(2,1)S(1)}, u32[]{:S(2)}, u32[]{:S(2)}) collective-permute-start(bf16[128,2176]{1,0:T(8,128)(2,1)} %pad_maximum_fusion.12), channel_id=1, source_target_pairs={{0,2},{2,4},{4,6},{6,7},{7,5},{5,3},{3,1},{1,0},{8,10},{10,12},{12... | collective-permute-start | bytes 1671176 | tf_op jit(solution)/shard_map/ppermute | solution.py:98
  261.1 16.9 %collective-permute-start.30 = (bf16[128,2176]{1,0:T(8,128)(2,1)S(1)}, bf16[128,2176]{1,0:T(8,128)(2,1)S(1)}, u32[]{:S(2)}, u32[]{:S(2)}) collective-permute-start(bf16[128,2176]{1,0:T(8,128)(2,1)S(1)} %pad_maximum_fusion.13), channel_id=1, source_target_pairs={{0,1},{2,0},{4,2},{6,4},{7,6},{5,7},{3,5},{1,3},{8,9},{10,8},{12,1... | collective-permute-start | bytes 1671176 | tf_op jit(solution)/shard_map/ppermute | solution.py:99
  277.9 48.3 %collective-permute-start.37 = (bf16[1024,1408]{1,0:T(8,128)(2,1)}, bf16[1024,1408]{1,0:T(8,128)(2,1)}, u32[]{:S(2)}, u32[]{:S(2)}) collective-permute-start(bf16[1024,1408]{1,0:T(8,128)(2,1)} %pair_dot.17), channel_id=1, source_target_pairs={{0,8},{8,0},{16,24},{24,16},{1,9},{9,1},{17,25},{25,17},{2,10},{10... | collective-permute-start | bytes 8650760 | tf_op jit(solution)/shard_map/ppermute | solution.py:205
  294.6 46.4 %collective-permute-start.41 = (bf16[1024,768]{1,0:T(8,128)(2,1)}, bf16[1024,768]{1,0:T(8,128)(2,1)}, u32[]{:S(2)}, u32[]{:S(2)}) collective-permute-start(bf16[1024,768]{1,0:T(8,128)(2,1)} %pair_dot.18), channel_id=1, source_target_pairs={{0,8},{8,0},{16,24},{24,16},{1,9},{9,1},{17,25},{25,17},{2,10},{10... | collective-permute-start | bytes 4718600 | tf_op jit(solution)/shard_map/ppermute | solution.py:205
  361.1 35.8 %collective-permute-start.50 = (bf16[512,1408]{1,0:T(8,128)(2,1)}, bf16[512,1408]{1,0:T(8,128)(2,1)}, u32[]{:S(2)}, u32[]{:S(2)}) collective-permute-start(bf16[512,1408]{1,0:T(8,128)(2,1)} %pair_dot.19), channel_id=1, source_target_pairs={{0,16},{8,24},{16,0},{24,8},{1,17},{9,25},{17,1},{25,9},{2,18},{10... | collective-permute-start | bytes 4325384 | tf_op jit(solution)/shard_map/ppermute | solution.py:217
  361.6 57.7 %collective-permute-start.53 = (bf16[1024,1408]{1,0:T(8,128)(2,1)}, bf16[1024,1408]{1,0:T(8,128)(2,1)}, u32[]{:S(2)}, u32[]{:S(2)}) collective-permute-start(bf16[1024,1408]{1,0:T(8,128)(2,1)} %pair_dot.22), channel_id=1, source_target_pairs={{0,8},{8,0},{16,24},{24,16},{1,9},{9,1},{17,25},{25,17},{2,10},{10... | collective-permute-start | bytes 8650760 | tf_op jit(solution)/shard_map/ppermute | solution.py:205
  365.5 19.6 %collective-permute-start.46 = (bf16[64,2048]{1,0:T(8,128)(2,1)}, bf16[64,2048]{1,0:T(8,128)(2,1)}, u32[]{:S(2)}, u32[]{:S(2)}) collective-permute-start(bf16[64,2048]{1,0:T(8,128)(2,1)} %get-tuple-element.357), channel_id=1, source_target_pairs={{0,2},{2,4},{4,6},{6,7},{7,5},{5,3},{3,1},{1,0},{8,10},{10,12},{12... | collective-permute-start | bytes 786440 | tf_op jit(solution)/shard_map/ppermute | solution.py:98
  367.0 18.0 %collective-permute-start.47 = (bf16[64,2048]{1,0:T(8,128)(2,1)}, bf16[64,2048]{1,0:T(8,128)(2,1)}, u32[]{:S(2)}, u32[]{:S(2)}) collective-permute-start(bf16[64,2048]{1,0:T(8,128)(2,1)} %get-tuple-element.358), channel_id=1, source_target_pairs={{0,1},{2,0},{4,2},{6,4},{7,6},{5,7},{3,5},{1,3},{8,9},{10,8},{12,1... | collective-permute-start | bytes 786440 | tf_op jit(solution)/shard_map/ppermute | solution.py:99
  414.9 22.1 %collective-permute-start.51 = (bf16[256,2048]{1,0:T(8,128)(2,1)}, bf16[256,2048]{1,0:T(8,128)(2,1)}, u32[]{:S(2)}, u32[]{:S(2)}) collective-permute-start(bf16[256,2048]{1,0:T(8,128)(2,1)} %pad_maximum_fusion.2), channel_id=1, source_target_pairs={{0,2},{2,4},{4,6},{6,7},{7,5},{5,3},{3,1},{1,0},{8,10},{10,12},{12... | collective-permute-start | bytes 3145736 | tf_op jit(solution)/shard_map/ppermute | solution.py:98
  416.3 20.6 %collective-permute-start.52 = (bf16[256,2048]{1,0:T(8,128)(2,1)}, bf16[256,2048]{1,0:T(8,128)(2,1)}, u32[]{:S(2)}, u32[]{:S(2)}) collective-permute-start(bf16[256,2048]{1,0:T(8,128)(2,1)} %pad_maximum_fusion.3), channel_id=1, source_target_pairs={{0,1},{2,0},{4,2},{6,4},{7,6},{5,7},{3,5},{1,3},{8,9},{10,8},{12,1... | collective-permute-start | bytes 3145736 | tf_op jit(solution)/shard_map/ppermute | solution.py:99
  419.2 48.3 %collective-permute-start.64 = (bf16[1024,1024]{1,0:T(8,128)(2,1)}, bf16[1024,1024]{1,0:T(8,128)(2,1)}, u32[]{:S(2)}, u32[]{:S(2)}) collective-permute-start(bf16[1024,1024]{1,0:T(8,128)(2,1)} %pair_dot.24), channel_id=1, source_target_pairs={{0,8},{8,0},{16,24},{24,16},{1,9},{9,1},{17,25},{25,17},{2,10},{10... | collective-permute-start | bytes 6291464 | tf_op jit(solution)/shard_map/ppermute | solution.py:205
  441.8 20.4 %collective-permute-start.55 = (bf16[256,2048]{1,0:T(8,128)(2,1)}, bf16[256,2048]{1,0:T(8,128)(2,1)}, u32[]{:S(2)}, u32[]{:S(2)}) collective-permute-start(bf16[256,2048]{1,0:T(8,128)(2,1)} %pad_maximum_fusion.4), channel_id=1, source_target_pairs={{0,2},{2,4},{4,6},{6,7},{7,5},{5,3},{3,1},{1,0},{8,10},{10,12},{12... | collective-permute-start | bytes 3145736 | tf_op jit(solution)/shard_map/ppermute | solution.py:98
  442.9 19.3 %collective-permute-start.56 = (bf16[256,2048]{1,0:T(8,128)(2,1)}, bf16[256,2048]{1,0:T(8,128)(2,1)}, u32[]{:S(2)}, u32[]{:S(2)}) collective-permute-start(bf16[256,2048]{1,0:T(8,128)(2,1)} %pad_maximum_fusion.5), channel_id=1, source_target_pairs={{0,1},{2,0},{4,2},{6,4},{7,6},{5,7},{3,5},{1,3},{8,9},{10,8},{12,1... | collective-permute-start | bytes 3145736 | tf_op jit(solution)/shard_map/ppermute | solution.py:99
  448.2 34.8 %collective-permute-start.66 = (bf16[512,1408]{1,0:T(8,128)(2,1)}, bf16[512,1408]{1,0:T(8,128)(2,1)}, u32[]{:S(2)}, u32[]{:S(2)}) collective-permute-start(bf16[512,1408]{1,0:T(8,128)(2,1)} %pair_dot.25), channel_id=1, source_target_pairs={{0,16},{8,24},{16,0},{24,8},{1,17},{9,25},{17,1},{25,9},{2,18},{10... | collective-permute-start | bytes 4325384 | tf_op jit(solution)/shard_map/ppermute | solution.py:217
  465.5 23.2 %collective-permute-start.57 = (bf16[128,2048]{1,0:T(8,128)(2,1)S(1)}, bf16[128,2048]{1,0:T(8,128)(2,1)S(1)}, u32[]{:S(2)}, u32[]{:S(2)}) collective-permute-start(bf16[128,2048]{1,0:T(8,128)(2,1)S(1)} %get-tuple-element.376), channel_id=1, source_target_pairs={{0,2},{2,4},{4,6},{6,7},{7,5},{5,3},{3,1},{1,0},{8,10},{10,12},{12... | collective-permute-start | bytes 1572872 | tf_op jit(solution)/shard_map/ppermute | solution.py:98
  466.4 22.3 %collective-permute-start.58 = (bf16[128,2048]{1,0:T(8,128)(2,1)S(1)}, bf16[128,2048]{1,0:T(8,128)(2,1)S(1)}, u32[]{:S(2)}, u32[]{:S(2)}) collective-permute-start(bf16[128,2048]{1,0:T(8,128)(2,1)S(1)} %get-tuple-element.377), channel_id=1, source_target_pairs={{0,1},{2,0},{4,2},{6,4},{7,6},{5,7},{3,5},{1,3},{8,9},{10,8},{12,1... | collective-permute-start | bytes 1572872 | tf_op jit(solution)/shard_map/ppermute | solution.py:99
  471.6 32.7 %collective-permute-start.65 = (bf16[512,1024]{1,0:T(8,128)(2,1)S(1)}, bf16[512,1024]{1,0:T(8,128)(2,1)S(1)}, u32[]{:S(2)}, u32[]{:S(2)}) collective-permute-start(bf16[512,1024]{1,0:T(8,128)(2,1)S(1)} %pair_dot.27), channel_id=1, source_target_pairs={{0,16},{8,24},{16,0},{24,8},{1,17},{9,25},{17,1},{25,9},{2,18},{10... | collective-permute-start | bytes 3145736 | tf_op jit(solution)/shard_map/ppermute | solution.py:217
  (138 other events, 1942.1 us)

commit v3 on v2

--- a/solution.py
+++ b/solution.py
@@ -10,7 +10,6 @@
 HD = 128
 EPSILON = 1e-06
 THETA = 1000000.0
-HIGHEST = lax.Precision.HIGHEST
 BF = jnp.bfloat16
 F32 = jnp.float32
 
@@ -995,6 +994,57 @@
     )(hid_e, hid_s, weight_out, weight_down)
 
 
+def past_units_kernel(
+    experts, residual_ref, own_ref, ahead_ref, behind_ref, grad_ref, gain_ref, head_ref,
+    routed_ref, picked_ref, sent_ref, out_ref, low_ref, rows_ref, gain_out,
+):
+    width = residual_ref.shape[1]
+    total = own_ref[...].astype(F32) + ahead_ref[...].astype(F32) + behind_ref[...].astype(F32)
+    small = total[:, width:]
+    routed = routed_ref[...]
+    lane = lax.broadcasted_iota(jnp.int32, small.shape, 1)
+    probs = jnp.where(lane < experts, routed, 0.0)
+    grads = picked_ref[...] * (small + pltpu.roll(small, 128 - experts, 1))
+    grads = jnp.where(lane < experts, grads, 0.0)
+    logits = probs * (grads - jnp.sum(probs * grads, 1, keepdims=True))
+    switch = jnp.where(lane == 2 * experts, routed, 0.0)
+    of_switch = jnp.where((lane >= 2 * experts) & (lane < 4 * experts), small, 0.0)
+    of_switch = jnp.sum(of_switch, 1, keepdims=True) * switch * (1.0 - switch)
+    scores = logits + of_switch
+    high = scores.astype(BF)
+    rest = (scores - high.astype(F32)).astype(BF)
+    grad = total[:, :width] + plain_dot(high, head_ref[...]) + plain_dot(rest, head_ref[...])
+    h = sent_ref[:, :width]
+    rows_ref[...] = left_dot(high, h) + left_dot(rest, h)
+    residual = residual_ref[...]
+    scale = rms_scale(residual)
+    unit = residual * scale
+    gain_out[...] = jnp.sum(grad * unit, 0, keepdims=True)
+    grad = grad * gain_ref[...].astype(F32)
+    mean = jnp.mean(grad * unit, -1, keepdims=True)
+    out = grad_ref[...].astype(F32) + scale * (grad - unit * mean)
+    out_ref[...] = out
+    low_ref[...] = out.astype(BF)
+
+
+def past_units(experts, residual, own, ahead, behind, grad, gain, head, routed, picked, sent):
+    rows, width = residual.shape
+    return pl.pallas_call(
+        functools.partial(past_units_kernel, experts),
+        out_shape=(
+            jax.ShapeDtypeStruct((rows, width), F32),
+            jax.ShapeDtypeStruct((rows, width), BF),
+            jax.ShapeDtypeStruct((128, width), F32),
+            jax.ShapeDtypeStruct((1, width), F32),
+        ),
+        in_specs=[WHOLE] * 10,
+        out_specs=(WHOLE,) * 4,
+        compiler_params=params(40),
+        cost_estimate=cost(0),
+        name="past_units",
+    )(residual, own, ahead, behind, grad, gain, head, routed, picked, sent)
+
+
 def routing_kernel(
     experts, x_ref, own_ref, ahead_ref, behind_ref, gain_ref, head_ref, picked_ref,
     residual_ref, sent_ref, routing_ref,
@@ -1133,7 +1183,6 @@
         head,
         picked,
     )
-    gain_ffn = feedforward_gain.astype(F32)
 
     gather_ffn = Gather(ring, h_sent)
     last = gather_ffn.step()
@@ -1204,28 +1253,20 @@
             busy = (busy, work(busy))
         befores.append(sum_ffn.step(busy))
     layer_parts[1] = layer_rows(half_rows, 12, befores[-2], busy)
-    grad_sum = sum_ffn.rest(layer_parts[1])
-
-    rms_ffn = rms_scale(residual)
-    unit_ffn = residual * rms_ffn
-    small = grad_sum[:, model_width:]
-    router_probs = routed[:, :experts]
-    switch = routed[:, 2 * experts]
-    grad_probs = picked[:, :experts] * (small[:, :experts] + small[:, experts : 2 * experts])
-    grad_logits = router_probs * (
-        grad_probs - jnp.sum(router_probs * grad_probs, -1, keepdims=True)
+
+    grad_residual, attention_grad, score_rows, grad_ffn_gain_part = past_units(
+        experts,
+        residual,
+        after(sum_ffn.own(0), layer_parts[1]),
+        sum_ffn.ahead,
+        sum_ffn.behind,
+        cotangent,
+        feedforward_gain[None],
+        head,
+        routed,
+        picked,
+        h_sent,
     )
-    grad_switch = jnp.sum(small[:, 2 * experts : 4 * experts], 1) * switch * (1.0 - switch)
-    h_float = h_sent[:, :model_width].astype(F32)
-    grad_ffn = grad_sum[:, :model_width]
-    grad_ffn = grad_ffn + jnp.dot(grad_logits, router_weight.astype(F32).T, precision=HIGHEST)
-    grad_ffn = grad_ffn + grad_switch[:, None] * shared_switch.astype(F32)
-    grad_out = cotangent.astype(F32)
-    grad_unit_ffn = grad_ffn * gain_ffn
-    grad_residual = grad_out + rms_ffn * (
-        grad_unit_ffn - unit_ffn * jnp.mean(grad_unit_ffn * unit_ffn, -1, keepdims=True)
-    )
-    attention_grad = grad_residual.astype(BF)
 
     gather_grad = Gather(ring, attention_grad)
     first = gather_grad.step()
@@ -1255,11 +1296,14 @@
     sum_attn = Scatter(ring, [attn_part], tok_rows)
     first = move(ring, [sum_attn, sum_layer])
 
-    grad_router_part = jnp.dot(grad_logits.T, h_float, precision=HIGHEST)
-    grad_switch_row = jnp.dot(grad_switch, h_float, precision=HIGHEST)
-    grad_ffn_gain_part = jnp.sum(grad_ffn * unit_ffn, 0)
     sums = jnp.concatenate(
-        [gain_part, grad_switch_row[None], grad_ffn_gain_part[None], grad_router_part], 0
+        [
+            gain_part,
+            score_rows[2 * experts : 2 * experts + 1],
+            grad_ffn_gain_part,
+            score_rows[:experts],
+        ],
+        0,
     )
     in_qkvo = PairSum([h_attn_split, grad_split], [grads, att_low])
     packed = jnp.concatenate([sums.reshape(-1), biases[0]]).reshape(-1, 128)

time: 517 us -> 508 us (0.983)
  other arithmetic: 33 us -> 27.2 us
    ppermute x26, starting transfers between devices: 28.4 us -> 33.5 us  [move(): ahead = lax.ppermute(up, 'expert', ring.forward)]
    unnamed x186 -> x170, local copies, waits for them, and re-layouts: 14.8 us -> 10.3 us
  transfers between devices with their start and end apart: 67 -> 67, of which waited for: 31 -> 34; matrix products, arithmetic and copies ran while one was open for 7% -> 6% of each run, Pallas kernels for 42% -> 42%
where the time goes in v3:
time: 508 us; the launch traced here: 504 us
  Pallas kernels  243 us (48%)
  waiting for transfers between devices  141 us (28%)
  starting transfers between devices  67 us (13%)
  other arithmetic  27.2 us (5%)
  local copies, waits for them, and re-layouts  21.1 us (4%)
    pallas_call x15, Pallas kernels, pair_dot(): pl.pallas_call(functools.partial(pair_kernel, pairs, [first for _, first...  88.8 us
    ppermute x26, waiting for transfers between devices, move(): ahead = lax.ppermute(up, 'expert', ring.forward)  75 us
    pallas_call x4, Pallas kernels, hidden_units(): pl.pallas_call(functools.partial(units_kernel, pieces, which, experts, le...  44.4 us
    ppermute x26, waiting for transfers between devices, move(): behind = lax.ppermute(down, 'expert', ring.backward)  35.7 us
    ppermute x26, starting transfers between devices, move(): ahead = lax.ppermute(up, 'expert', ring.forward)  33.5 us
    pallas_call x4, Pallas kernels, units_in(): pl.pallas_call(functools.partial(units_in_kernel, which), out_shape=jax.S...  32.7 us
    pallas_call x4, Pallas kernels, back_units(): pl.pallas_call(functools.partial(back_kernel, pieces, which, len(split)),...  24.6 us
    ppermute x26, starting transfers between devices, move(): behind = lax.ppermute(down, 'expert', ring.backward)  22.3 us
  transfers between devices with their start and end apart: 67, of which 34 were waited for; matrix products, arithmetic and copies ran while one was open for 6% of the time, Pallas kernels for 42%

profile of v3, /device:TPU:0, one launch (start us, length us, event | category | flops | bytes accessed | tf_op | source)
XLA Modules:
  0.0 503.5 jit_solution(14545720883417584669)
XLA Ops:
  10.8 8.0 %collective-permute-done.refs_0_ = bf16[128,2048]{1,0:T(8,128)(2,1)S(1)} collective-permute-done((bf16[128,2048]{1,0:T(8,128)(2,1)S(1)}, bf16[128,2048]{1,0:T(8,128)(2,1)S(1)}, u32[]{:S(2)}, u32[]{:S(2)}) %collective-permute-start) | collective-permute-done | bytes 524320 | tf_op jit(solution)/shard_map/ppermute | solution.py:97
  22.4 10.4 %collective-permute-done.2.refs_2_ = bf16[128,2048]{1,0:T(8,128)(2,1)S(1)} collective-permute-done((bf16[128,2048]{1,0:T(8,128)(2,1)S(1)}, bf16[128,2048]{1,0:T(8,128)(2,1)S(1)}, u32[]{:S(2)}, u32[]{:S(2)}) %collective-permute-start.2) | collective-permute-done | bytes 524320 | tf_op jit(solution)/shard_map/ppermute | solution.py:97
  37.5 8.0 %collective-permute-done.4.refs_4_ = bf16[128,2048]{1,0:T(8,128)(2,1)S(1)} collective-permute-done((bf16[128,2048]{1,0:T(8,128)(2,1)S(1)}, bf16[128,2048]{1,0:T(8,128)(2,1)S(1)}, u32[]{:S(2)}, u32[]{:S(2)}) %collective-permute-start.4) | collective-permute-done | bytes 524320 | tf_op jit(solution)/shard_map/ppermute | solution.py:97
  58.9 10.0 %project.1 = (bf16[1024,256]{1,0:T(8,128)(2,1)S(1)}, bf16[1024,256]{1,0:T(8,128)(2,1)S(1)}, bf16[1024,256]{1,0:T(8,128)(2,1)}, bf16[1024,1024]{1,0:T(8,128)(2,1)...) custom-call(s32[8]{0:T(128)S(1)} %gather_fusion, s32[2]{0:T(128)S(1)} %pad_add_fusion.place, ...), custom_call_target="tpu_custom_call" | custom-call | flops 3000000000 | bytes 1 | tf_op jit(solution)/shard_map/project/pallas_call | solution.py:346
  85.9 7.4 %collective-permute-done.11 = bf16[192,2048]{1,0:T(8,128)(2,1)S(1)} collective-permute-done((bf16[192,2048]{1,0:T(8,128)(2,1)S(1)}, bf16[192,2048]{1,0:T(8,128)(2,1)S(1)}, u32[]{:S(2)}, u32[]{:S(2)}) %collective-permute-start.11) | collective-permute-done | bytes 786464 | tf_op jit(solution)/shard_map/ppermute | solution.py:98
  102.8 11.6 %collective-permute-done.13 = bf16[256,2048]{1,0:T(8,128)(2,1)S(1)} collective-permute-done((bf16[256,2048]{1,0:T(8,128)(2,1)S(1)}, bf16[256,2048]{1,0:T(8,128)(2,1)S(1)}, u32[]{:S(2)}, u32[]{:S(2)}) %collective-permute-start.13) | collective-permute-done | bytes 1048608 | tf_op jit(solution)/shard_map/ppermute | solution.py:98
  127.3 8.1 %collective-permute-done.14 = bf16[192,2048]{1,0:T(8,128)(2,1)S(1)} collective-permute-done((bf16[192,2048]{1,0:T(8,128)(2,1)S(1)}, bf16[192,2048]{1,0:T(8,128)(2,1)S(1)}, u32[]{:S(2)}, u32[]{:S(2)}) %collective-permute-start.14) | collective-permute-done | bytes 786464 | tf_op jit(solution)/shard_map/ppermute | solution.py:97
  155.3 9.8 %collective-permute-done.18.refs_0_ = bf16[128,2176]{1,0:T(8,128)(2,1)S(1)} collective-permute-done((bf16[128,2176]{1,0:T(8,128)(2,1)S(1)}, bf16[128,2176]{1,0:T(8,128)(2,1)S(1)}, u32[]{:S(2)}, u32[]{:S(2)}) %collective-permute-start.18) | collective-permute-done | bytes 557088 | tf_op jit(solution)/shard_map/ppermute | solution.py:97
  168.8 11.1 %hidden_units.4 = (bf16[256,128]{1,0:T(8,128)(2,1)S(1)}, bf16[1024,1408]{1,0:T(8,128)(2,1)}, bf16[1024,768]{1,0:T(8,128)(2,1)}, bf16[1024,2816]{1,0:T(8,128)(2,1...) custom-call(s32[1]{0:T(128)} %bitcast.6.me_ref, ...), custom_call_target="tpu_custom_call" | custom-call | flops 6000000000 | bytes 1 | tf_op jit(solution)/shard_map/hidden_units/pallas_call | solution.py:771
  181.9 11.1 %hidden_units.5 = (bf16[256,128]{1,0:T(8,128)(2,1)S(1)}, bf16[1024,1408]{1,0:T(8,128)(2,1)}, bf16[1024,768]{1,0:T(8,128)(2,1)}, bf16[1024,2816]{1,0:T(8,128)(2,1...) custom-call(s32[1]{0:T(128)} %bitcast.6.me_ref, ...), custom_call_target="tpu_custom_call", output_to_operand_aliasing={{1}: (9, {}), {2}: (10, {}), {3}: (11, {}), {4}: (12, {}), ... | custom-call | flops 6000000000 | bytes 1 | tf_op jit(solution)/shard_map/hidden_units/pallas_call | solution.py:771
  195.2 11.1 %hidden_units.6 = (bf16[256,128]{1,0:T(8,128)(2,1)S(1)}, bf16[1024,1408]{1,0:T(8,128)(2,1)}, bf16[1024,768]{1,0:T(8,128)(2,1)}, bf16[1024,2816]{1,0:T(8,128)(2,1...) custom-call(s32[1]{0:T(128)} %bitcast.6.me_ref, ...), custom_call_target="tpu_custom_call", output_to_operand_aliasing={{1}: (9, {}), {2}: (10, {}), {3}: (11, {}), {4}: (12, {}), ... | custom-call | flops 6000000000 | bytes 1 | tf_op jit(solution)/shard_map/hidden_units/pallas_call | solution.py:771
  206.3 11.1 %hidden_units.7 = (bf16[256,128]{1,0:T(8,128)(2,1)S(1)}, bf16[1024,1408]{1,0:T(8,128)(2,1)}, bf16[1024,768]{1,0:T(8,128)(2,1)}, bf16[1024,2816]{1,0:T(8,128)(2,1...) custom-call(s32[1]{0:T(128)} %bitcast.6.me_ref, ...), custom_call_target="tpu_custom_call", output_to_operand_aliasing={{1}: (10, {}), {2}: (11, {}), {3}: (12, {}), {4}: (13, {}),... | custom-call | flops 6000000000 | bytes 1 | tf_op jit(solution)/shard_map/hidden_units/pallas_call | solution.py:771
  217.5 11.1 %pair_dot.15 = bf16[1024,2816]{1,0:T(8,128)(2,1)} custom-call(bf16[1024,1024]{1,0:T(8,128)(2,1)} %get-tuple-element.348.refs_0_, bf16[1024,2816]{1,0:T(8,128)(2,1)} %get-tuple-element.325.refs_1_.both_hbm), custom_call_target="tpu_custom_call" | custom-call | flops 1 | bytes 1 | tf_op jit(solution)/shard_map/pair_dot/pallas_call | solution.py:933
  228.7 8.2 %units_in.4 = bf16[256,2176]{1,0:T(8,128)(2,1)S(1)} custom-call(bf16[1024,2816]{1,0:T(8,128)(2,1)} %get-tuple-element.325.refs_1_.both_hbm, bf16[1024,1408]{1,0:T(8,128)(2,1)S(1)} %copy-done, bf16[256,128]{1,0:T(8,128)(2,1)S(1)} %get-tuple-element.309.small_ref, bf16[2048,2816]{1,0:T(8,128)(2,1)} %bitcast.40, bf16[704,2048]{1,0:T(8,128)(2,1)} %bitcast.48, ...), custom_call_target="tpu_custom_call" | custom-call | flops 70000001024 | bytes 1 | tf_op jit(solution)/shard_map/units_in/pallas_call | solution.py:844
  239.0 8.1 %units_in.5 = bf16[256,2176]{1,0:T(8,128)(2,1)S(1)} custom-call(bf16[1024,2816]{1,0:T(8,128)(2,1)} %get-tuple-element.325.refs_1_.both_hbm, bf16[1024,1408]{1,0:T(8,128)(2,1)S(1)} %copy-done, bf16[256,128]{1,0:T(8,128)(2,1)S(1)} %get-tuple-element.312.small_ref, bf16[2048,2816]{1,0:T(8,128)(2,1)} %bitcast.41, bf16[704,2048]{1,0:T(8,128)(2,1)} %bitcast.49, ...), custom_call_target="tpu_custom_call" | custom-call | flops 6000000000 | bytes 1 | tf_op jit(solution)/shard_map/units_in/pallas_call | solution.py:844
  259.0 8.2 %units_in.6 = bf16[256,2176]{1,0:T(8,128)(2,1)S(1)} custom-call(bf16[1024,2816]{1,0:T(8,128)(2,1)} %get-tuple-element.325.refs_1_.both_hbm, bf16[1024,1408]{1,0:T(8,128)(2,1)S(1)} %copy-done, bf16[256,128]{1,0:T(8,128)(2,1)S(1)} %get-tuple-element.280.small_ref, bf16[2048,2816]{1,0:T(8,128)(2,1)} %bitcast.42, bf16[704,2048]{1,0:T(8,128)(2,1)} %bitcast.50, ...), custom_call_target="tpu_custom_call" | custom-call | flops 6000000000 | bytes 1 | tf_op jit(solution)/shard_map/units_in/pallas_call | solution.py:844
  276.3 8.2 %units_in.7 = bf16[256,2176]{1,0:T(8,128)(2,1)S(1)} custom-call(bf16[1024,2816]{1,0:T(8,128)(2,1)} %get-tuple-element.325.refs_1_.both_hbm, bf16[1024,1408]{1,0:T(8,128)(2,1)S(1)} %copy-done, bf16[256,128]{1,0:T(8,128)(2,1)S(1)} %get-tuple-element.268.small_ref, bf16[2048,2816]{1,0:T(8,128)(2,1)} %bitcast.43, bf16[704,2048]{1,0:T(8,128)(2,1)} %bitcast.51, ...), custom_call_target="tpu_custom_call" | custom-call | flops 12000000000 | bytes 1 | tf_op jit(solution)/shard_map/units_in/pallas_call | solution.py:844
  292.7 7.6 %layer_part.2 = bf16[512,2048]{1,0:T(8,128)(2,1)S(1)} custom-call(bf16[1024,1408]{1,0:T(8,128)(2,1)} %get-tuple-element.338.refs_1_.he_hbm, bf16[1024,768]{1,0:T(8,128)(2,1)S(1)} %copy-done.1, bf16[2048,1408]{1,0:T(8,128)(2,1)} %bitcast.69, bf16[704,2048]{1,0:T(8,128)(2,1)} %bitcast.75), custom_call_target="tpu_custom_call" | custom-call | flops 12000000000 | bytes 1 | tf_op jit(solution)/shard_map/layer_part/pallas_call | solution.py:979
  309.4 7.8 %layer_part.3 = bf16[512,2048]{1,0:T(8,128)(2,1)S(1)} custom-call(bf16[1024,1408]{1,0:T(8,128)(2,1)} %get-tuple-element.338.refs_1_.he_hbm, bf16[1024,768]{1,0:T(8,128)(2,1)S(1)} %copy-done.1, bf16[2048,1408]{1,0:T(8,128)(2,1)} %bitcast.70, bf16[704,2048]{1,0:T(8,128)(2,1)} %bitcast.76), custom_call_target="tpu_custom_call" | custom-call | flops 12000000000 | bytes 1 | tf_op jit(solution)/shard_map/layer_part/pallas_call | solution.py:979
  324.6 7.3 %pair_dot.20 = f32[512,2816]{1,0:T(8,128)} custom-call(bf16[1024,512]{1,0:T(8,128)(2,1)S(1)} %copy-done.7, bf16[1024,2816]{1,0:T(8,128)(2,1)} %get-tuple-element.325.refs_1_.both_hbm, bf16[1024,2816]{1,0:T(8,128)(2,1)} %collective-permute-done.26.refs_2_, bf16[512,2816]{1,0:T(8,128)(2,1)} %collective-permute-done.40.refs_3_), custom_call_target="tpu_custom_call" | custom-call | flops 7500000256 | bytes 1 | tf_op jit(solution)/shard_map/pair_dot/pallas_call | solution.py:933
  367.8 7.7 %attend_back.1 = (bf16[1024,768]{1,0:T(8,128)(2,1)S(1)}, f32[1,768]{1,0:T(1,128)S(1)}) custom-call(s32[8]{0:T(128)S(1)} %copy-done.45, bf16[1024,256]{1,0:T(8,128)(2,1)S(1)} %copy-done.48, bf16[1024,256]{1,0:T(8,128)(2,1)S(1)} %copy-done.50, bf16[1024,256]{1,0:T(8,128)(2,1)S(1)} %copy-done.52, bf16[1024,256]{1,0:T(8,128)(2,1)S(1)} %copy-done.54, ...), custom_call_target="tpu_custom_call" | custom-call | flops 20000000000 | bytes 1 | tf_op jit(solution)/shard_map/attend_back/pallas_call | solution.py:481
  415.6 7.4 %collective-permute-done.54.refs_3_ = bf16[512,768]{1,0:T(8,128)(2,1)} collective-permute-done((bf16[512,768]{1,0:T(8,128)(2,1)}, bf16[512,768]{1,0:T(8,128)(2,1)}, u32[]{:S(2)}, u32[]{:S(2)}) %collective-permute-start.54) | collective-permute-done | bytes 786464 | tf_op jit(solution)/shard_map/ppermute | solution.py:216
  441.3 11.2 %collective-permute-done.55 = bf16[256,2048]{1,0:T(8,128)(2,1)} collective-permute-done((bf16[256,2048]{1,0:T(8,128)(2,1)}, bf16[256,2048]{1,0:T(8,128)(2,1)}, u32[]{:S(2)}, u32[]{:S(2)}) %collective-permute-start.55) | collective-permute-done | bytes 1048608 | tf_op jit(solution)/shard_map/ppermute | solution.py:97
  464.7 9.6 %collective-permute-done.66.refs_3_ = bf16[512,1408]{1,0:T(8,128)(2,1)} collective-permute-done((bf16[512,1408]{1,0:T(8,128)(2,1)}, bf16[512,1408]{1,0:T(8,128)(2,1)}, u32[]{:S(2)}, u32[]{:S(2)}) %collective-permute-start.66) | collective-permute-done | bytes 1441824 | tf_op jit(solution)/shard_map/ppermute | solution.py:216
  (409 shorter events, 280.6 us)
Async XLA Ops:
  56.7 18.5 %collective-permute-start.8 = (bf16[128,2048]{1,0:T(8,128)(2,1)S(1)}, bf16[128,2048]{1,0:T(8,128)(2,1)S(1)}, u32[]{:S(2)}, u32[]{:S(2)}) collective-permute-start(bf16[128,2048]{1,0:T(8,128)(2,1)S(1)} %copy-done.30), channel_id=1, source_target_pairs={{0,2},{2,4},{4,6},{6,7},{7,5},{5,3},{3,1},{1,0},{8,10},{10,12},{12... | collective-permute-start | bytes 1572872 | tf_op jit(solution)/shard_map/ppermute | solution.py:97
  57.7 17.6 %collective-permute-start.9 = (bf16[128,2048]{1,0:T(8,128)(2,1)S(1)}, bf16[128,2048]{1,0:T(8,128)(2,1)S(1)}, u32[]{:S(2)}, u32[]{:S(2)}) collective-permute-start(bf16[128,2048]{1,0:T(8,128)(2,1)S(1)} %copy-done.30), channel_id=1, source_target_pairs={{0,1},{2,0},{4,2},{6,4},{7,6},{5,7},{3,5},{1,3},{8,9},{10,8},{12,1... | collective-permute-start | bytes 1572872 | tf_op jit(solution)/shard_map/ppermute | solution.py:98
  93.8 20.6 %collective-permute-start.13 = (bf16[256,2048]{1,0:T(8,128)(2,1)S(1)}, bf16[256,2048]{1,0:T(8,128)(2,1)S(1)}, u32[]{:S(2)}, u32[]{:S(2)}) collective-permute-start(bf16[256,2048]{1,0:T(8,128)(2,1)S(1)} %pad_maximum_fusion.1), channel_id=1, source_target_pairs={{0,1},{2,0},{4,2},{6,4},{7,6},{5,7},{3,5},{1,3},{8,9},{10,8},{12,1... | collective-permute-start | bytes 3145736 | tf_op jit(solution)/shard_map/ppermute | solution.py:98
  94.5 21.5 %collective-permute-start.12 = (bf16[256,2048]{1,0:T(8,128)(2,1)S(1)}, bf16[256,2048]{1,0:T(8,128)(2,1)S(1)}, u32[]{:S(2)}, u32[]{:S(2)}) collective-permute-start(bf16[256,2048]{1,0:T(8,128)(2,1)S(1)} %pad_maximum_fusion), channel_id=1, source_target_pairs={{0,2},{2,4},{4,6},{6,7},{7,5},{5,3},{3,1},{1,0},{8,10},{10,12},{12... | collective-permute-start | bytes 3145736 | tf_op jit(solution)/shard_map/ppermute | solution.py:97
  117.8 17.6 %collective-permute-start.14 = (bf16[192,2048]{1,0:T(8,128)(2,1)S(1)}, bf16[192,2048]{1,0:T(8,128)(2,1)S(1)}, u32[]{:S(2)}, u32[]{:S(2)}) collective-permute-start(bf16[192,2048]{1,0:T(8,128)(2,1)S(1)} %pad_maximum_fusion.8), channel_id=1, source_target_pairs={{0,2},{2,4},{4,6},{6,7},{7,5},{5,3},{3,1},{1,0},{8,10},{10,12},{12... | collective-permute-start | bytes 2359304 | tf_op jit(solution)/shard_map/ppermute | solution.py:97
  119.9 17.6 %collective-permute-start.15 = (bf16[192,2048]{1,0:T(8,128)(2,1)S(1)}, bf16[192,2048]{1,0:T(8,128)(2,1)S(1)}, u32[]{:S(2)}, u32[]{:S(2)}) collective-permute-start(bf16[192,2048]{1,0:T(8,128)(2,1)S(1)} %pad_maximum_fusion.9), channel_id=1, source_target_pairs={{0,1},{2,0},{4,2},{6,4},{7,6},{5,7},{3,5},{1,3},{8,9},{10,8},{12,1... | collective-permute-start | bytes 2359304 | tf_op jit(solution)/shard_map/ppermute | solution.py:98
  228.6 18.9 %collective-permute-start.26 = (bf16[1024,2816]{1,0:T(8,128)(2,1)}, bf16[1024,2816]{1,0:T(8,128)(2,1)}, u32[]{:S(2)}, u32[]{:S(2)}) collective-permute-start(bf16[1024,2816]{1,0:T(8,128)(2,1)} %pair_dot.15), channel_id=1, source_target_pairs={{0,8},{8,0},{16,24},{24,16},{1,9},{9,1},{17,25},{25,17},{2,10},{10... | collective-permute-start | bytes 17301512 | tf_op jit(solution)/shard_map/ppermute | solution.py:204
  255.4 69.3 %collective-permute-start.40 = (bf16[512,2816]{1,0:T(8,128)(2,1)}, bf16[512,2816]{1,0:T(8,128)(2,1)}, u32[]{:S(2)}, u32[]{:S(2)}) collective-permute-start(bf16[512,2816]{1,0:T(8,128)(2,1)} %pair_dot.16), channel_id=1, source_target_pairs={{0,16},{8,24},{16,0},{24,8},{1,17},{9,25},{17,1},{25,9},{2,18},{10... | collective-permute-start | bytes 8650760 | tf_op jit(solution)/shard_map/ppermute | solution.py:216
  257.0 17.0 %collective-permute-start.29 = (bf16[128,2176]{1,0:T(8,128)(2,1)S(1)}, bf16[128,2176]{1,0:T(8,128)(2,1)S(1)}, u32[]{:S(2)}, u32[]{:S(2)}) collective-permute-start(bf16[128,2176]{1,0:T(8,128)(2,1)S(1)} %pad_maximum_fusion.12), channel_id=1, source_target_pairs={{0,2},{2,4},{4,6},{6,7},{7,5},{5,3},{3,1},{1,0},{8,10},{10,12},{12... | collective-permute-start | bytes 1671176 | tf_op jit(solution)/shard_map/ppermute | solution.py:97
  273.9 43.3 %collective-permute-start.37 = (bf16[1024,1408]{1,0:T(8,128)(2,1)}, bf16[1024,1408]{1,0:T(8,128)(2,1)}, u32[]{:S(2)}, u32[]{:S(2)}) collective-permute-start(bf16[1024,1408]{1,0:T(8,128)(2,1)} %pair_dot.17), channel_id=1, source_target_pairs={{0,8},{8,0},{16,24},{24,16},{1,9},{9,1},{17,25},{25,17},{2,10},{10... | collective-permute-start | bytes 8650760 | tf_op jit(solution)/shard_map/ppermute | solution.py:204
  289.6 42.4 %collective-permute-start.41 = (bf16[1024,768]{1,0:T(8,128)(2,1)S(1)}, bf16[1024,768]{1,0:T(8,128)(2,1)}, u32[]{:S(2)}, u32[]{:S(2)}) collective-permute-start(bf16[1024,768]{1,0:T(8,128)(2,1)S(1)} %pair_dot.18), channel_id=1, source_target_pairs={{0,8},{8,0},{16,24},{24,16},{1,9},{9,1},{17,25},{25,17},{2,10},{10... | collective-permute-start | bytes 4718600 | tf_op jit(solution)/shard_map/ppermute | solution.py:204
  352.0 35.4 %collective-permute-start.50 = (bf16[512,1408]{1,0:T(8,128)(2,1)}, bf16[512,1408]{1,0:T(8,128)(2,1)}, u32[]{:S(2)}, u32[]{:S(2)}) collective-permute-start(bf16[512,1408]{1,0:T(8,128)(2,1)} %pair_dot.19), channel_id=1, source_target_pairs={{0,16},{8,24},{16,0},{24,8},{1,17},{9,25},{17,1},{25,9},{2,18},{10... | collective-permute-start | bytes 4325384 | tf_op jit(solution)/shard_map/ppermute | solution.py:216
  352.5 58.3 %collective-permute-start.53 = (bf16[1024,1408]{1,0:T(8,128)(2,1)}, bf16[1024,1408]{1,0:T(8,128)(2,1)}, u32[]{:S(2)}, u32[]{:S(2)}) collective-permute-start(bf16[1024,1408]{1,0:T(8,128)(2,1)} %pair_dot.22), channel_id=1, source_target_pairs={{0,8},{8,0},{16,24},{24,16},{1,9},{9,1},{17,25},{25,17},{2,10},{10... | collective-permute-start | bytes 8650760 | tf_op jit(solution)/shard_map/ppermute | solution.py:204
  356.0 19.5 %collective-permute-start.46 = (bf16[64,2048]{1,0:T(8,128)(2,1)}, bf16[64,2048]{1,0:T(8,128)(2,1)S(1)}, u32[]{:S(2)}, u32[]{:S(2)}) collective-permute-start(bf16[64,2048]{1,0:T(8,128)(2,1)} %get-tuple-element.362), channel_id=1, source_target_pairs={{0,2},{2,4},{4,6},{6,7},{7,5},{5,3},{3,1},{1,0},{8,10},{10,12},{12... | collective-permute-start | bytes 786440 | tf_op jit(solution)/shard_map/ppermute | solution.py:97
  356.5 19.0 %collective-permute-start.47 = (bf16[64,2048]{1,0:T(8,128)(2,1)}, bf16[64,2048]{1,0:T(8,128)(2,1)}, u32[]{:S(2)}, u32[]{:S(2)}) collective-permute-start(bf16[64,2048]{1,0:T(8,128)(2,1)} %get-tuple-element.363), channel_id=1, source_target_pairs={{0,1},{2,0},{4,2},{6,4},{7,6},{5,7},{3,5},{1,3},{8,9},{10,8},{12,1... | collective-permute-start | bytes 786440 | tf_op jit(solution)/shard_map/ppermute | solution.py:98
  405.5 22.1 %collective-permute-start.51 = (bf16[256,2048]{1,0:T(8,128)(2,1)}, bf16[256,2048]{1,0:T(8,128)(2,1)}, u32[]{:S(2)}, u32[]{:S(2)}) collective-permute-start(bf16[256,2048]{1,0:T(8,128)(2,1)} %pad_maximum_fusion.2), channel_id=1, source_target_pairs={{0,2},{2,4},{4,6},{6,7},{7,5},{5,3},{3,1},{1,0},{8,10},{10,12},{12... | collective-permute-start | bytes 3145736 | tf_op jit(solution)/shard_map/ppermute | solution.py:97
  405.9 21.7 %collective-permute-start.52 = (bf16[256,2048]{1,0:T(8,128)(2,1)}, bf16[256,2048]{1,0:T(8,128)(2,1)}, u32[]{:S(2)}, u32[]{:S(2)}) collective-permute-start(bf16[256,2048]{1,0:T(8,128)(2,1)} %pad_maximum_fusion.3), channel_id=1, source_target_pairs={{0,1},{2,0},{4,2},{6,4},{7,6},{5,7},{3,5},{1,3},{8,9},{10,8},{12,1... | collective-permute-start | bytes 3145736 | tf_op jit(solution)/shard_map/ppermute | solution.py:98
  410.7 47.6 %collective-permute-start.64 = (bf16[1024,1024]{1,0:T(8,128)(2,1)}, bf16[1024,1024]{1,0:T(8,128)(2,1)}, u32[]{:S(2)}, u32[]{:S(2)}) collective-permute-start(bf16[1024,1024]{1,0:T(8,128)(2,1)} %pair_dot.24), channel_id=1, source_target_pairs={{0,8},{8,0},{16,24},{24,16},{1,9},{9,1},{17,25},{25,17},{2,10},{10... | collective-permute-start | bytes 6291464 | tf_op jit(solution)/shard_map/ppermute | solution.py:204
  432.4 20.2 %collective-permute-start.55 = (bf16[256,2048]{1,0:T(8,128)(2,1)}, bf16[256,2048]{1,0:T(8,128)(2,1)}, u32[]{:S(2)}, u32[]{:S(2)}) collective-permute-start(bf16[256,2048]{1,0:T(8,128)(2,1)} %pad_maximum_fusion.4), channel_id=1, source_target_pairs={{0,2},{2,4},{4,6},{6,7},{7,5},{5,3},{3,1},{1,0},{8,10},{10,12},{12... | collective-permute-start | bytes 3145736 | tf_op jit(solution)/shard_map/ppermute | solution.py:97
  432.9 20.0 %collective-permute-start.56 = (bf16[256,2048]{1,0:T(8,128)(2,1)}, bf16[256,2048]{1,0:T(8,128)(2,1)}, u32[]{:S(2)}, u32[]{:S(2)}) collective-permute-start(bf16[256,2048]{1,0:T(8,128)(2,1)} %pad_maximum_fusion.5), channel_id=1, source_target_pairs={{0,1},{2,0},{4,2},{6,4},{7,6},{5,7},{3,5},{1,3},{8,9},{10,8},{12,1... | collective-permute-start | bytes 3145736 | tf_op jit(solution)/shard_map/ppermute | solution.py:98
  439.6 34.8 %collective-permute-start.66 = (bf16[512,1408]{1,0:T(8,128)(2,1)}, bf16[512,1408]{1,0:T(8,128)(2,1)}, u32[]{:S(2)}, u32[]{:S(2)}) collective-permute-start(bf16[512,1408]{1,0:T(8,128)(2,1)} %pair_dot.25), channel_id=1, source_target_pairs={{0,16},{8,24},{16,0},{24,8},{1,17},{9,25},{17,1},{25,9},{2,18},{10... | collective-permute-start | bytes 4325384 | tf_op jit(solution)/shard_map/ppermute | solution.py:216
  456.3 23.7 %collective-permute-start.57 = (bf16[128,2048]{1,0:T(8,128)(2,1)S(1)}, bf16[128,2048]{1,0:T(8,128)(2,1)S(1)}, u32[]{:S(2)}, u32[]{:S(2)}) collective-permute-start(bf16[128,2048]{1,0:T(8,128)(2,1)S(1)} %get-tuple-element.382), channel_id=1, source_target_pairs={{0,2},{2,4},{4,6},{6,7},{7,5},{5,3},{3,1},{1,0},{8,10},{10,12},{12... | collective-permute-start | bytes 1572872 | tf_op jit(solution)/shard_map/ppermute | solution.py:97
  457.0 22.9 %collective-permute-start.58 = (bf16[128,2048]{1,0:T(8,128)(2,1)S(1)}, bf16[128,2048]{1,0:T(8,128)(2,1)S(1)}, u32[]{:S(2)}, u32[]{:S(2)}) collective-permute-start(bf16[128,2048]{1,0:T(8,128)(2,1)S(1)} %get-tuple-element.383), channel_id=1, source_target_pairs={{0,1},{2,0},{4,2},{6,4},{7,6},{5,7},{3,5},{1,3},{8,9},{10,8},{12,1... | collective-permute-start | bytes 1572872 | tf_op jit(solution)/shard_map/ppermute | solution.py:98
  462.5 33.1 %collective-permute-start.65 = (bf16[512,1024]{1,0:T(8,128)(2,1)S(1)}, bf16[512,1024]{1,0:T(8,128)(2,1)S(1)}, u32[]{:S(2)}, u32[]{:S(2)}) collective-permute-start(bf16[512,1024]{1,0:T(8,128)(2,1)S(1)} %pair_dot.27), channel_id=1, source_target_pairs={{0,16},{8,24},{16,0},{24,8},{1,17},{9,25},{17,1},{25,9},{2,18},{10... | collective-permute-start | bytes 3145736 | tf_op jit(solution)/shard_map/ppermute | solution.py:216
  (129 other events, 2094.8 us)

commit v4 on v3

--- a/solution.py
+++ b/solution.py
@@ -1244,20 +1244,24 @@
     sum_ffn = Scatter(ring, chunks, tok_rows)
     befores = [chunks[-1], sum_ffn.step()]
     busy = chunks[-1]
-    works = [(6, in_e.chips), (6, out_e.cores), (12, out_s.cores)]
+    works = [(6, None), (6, in_e.chips), (12, out_s.cores)]
     for at, which in enumerate(range(ring.half - 2, -1, -1)):
         time, work = works[at] if at < len(works) else (6, None)
+        if at == 1:
+            busy = in_e.chips(busy, befores[-2], time=6)
+            time, work = 0, None
         chunks[which] = chunk_in(which, time, busy, befores[-2])
         busy = chunks[which]
         if work is not None:
             busy = (busy, work(busy))
         befores.append(sum_ffn.step(busy))
     layer_parts[1] = layer_rows(half_rows, 12, befores[-2], busy)
+    busy = out_e.cores(layer_parts[1])
 
     grad_residual, attention_grad, score_rows, grad_ffn_gain_part = past_units(
         experts,
         residual,
-        after(sum_ffn.own(0), layer_parts[1]),
+        after(sum_ffn.own(0), busy),
         sum_ffn.ahead,
         sum_ffn.behind,
         cotangent,
@@ -1270,14 +1274,14 @@
 
     gather_grad = Gather(ring, attention_grad)
     first = gather_grad.step()
-    layer_parts[0] = layer_rows(0, 12, attention_grad)
+    layer_parts[0] = layer_rows(0, 35, attention_grad)
     busy = out_e.chips(layer_parts[0])
     second = gather_grad.step(busy)
-    totals = in_e.total(first, busy, time=7.5)
-    busy = out_s.chips(totals)
+    busy = in_s.cores(first, busy, time=7.5)
+    busy = out_s.chips(busy)
     third = gather_grad.step(busy)
-    busy = in_s.cores(second, busy, time=7.5)
-    last = gather_grad.step(busy)
+    totals = in_e.total(second, busy, time=7.5)
+    last = gather_grad.step(totals)
     while gather_grad.at < ring.half:
         last = gather_grad.step()
     attention_grad_parts = gather_grad.rest()

time: 508 us -> 503 us (level)
  waiting for transfers between devices: 141 us -> 134 us
    unnamed x170 -> x168, local copies, waits for them, and re-layouts: 10.3 us -> 10.2 us
  transfers between devices with their start and end apart: 67 -> 67, of which waited for: 34 -> 34; matrix products, arithmetic and copies ran while one was open for 6% -> 6% of each run, Pallas kernels for 42% -> 44%
where the time goes in v4:
time: 503 us; the launch traced here: 499 us
  Pallas kernels  243 us (48%)
  waiting for transfers between devices  134 us (27%)
  starting transfers between devices  68.6 us (14%)
  other arithmetic  28.3 us (6%)
  local copies, waits for them, and re-layouts  21 us (4%)
    pallas_call x15, Pallas kernels, pair_dot(): pl.pallas_call(functools.partial(pair_kernel, pairs, [first for _, first...  89 us
    ppermute x26, waiting for transfers between devices, move(): ahead = lax.ppermute(up, 'expert', ring.forward)  71.2 us
    pallas_call x4, Pallas kernels, hidden_units(): pl.pallas_call(functools.partial(units_kernel, pieces, which, experts, le...  44.3 us
    ppermute x26, waiting for transfers between devices, move(): behind = lax.ppermute(down, 'expert', ring.backward)  34 us
    ppermute x26, starting transfers between devices, move(): ahead = lax.ppermute(up, 'expert', ring.forward)  33.2 us
    pallas_call x4, Pallas kernels, units_in(): pl.pallas_call(functools.partial(units_in_kernel, which), out_shape=jax.S...  32.8 us
    pallas_call x4, Pallas kernels, back_units(): pl.pallas_call(functools.partial(back_kernel, pieces, which, len(split)),...  24.6 us
    ppermute x26, starting transfers between devices, move(): behind = lax.ppermute(down, 'expert', ring.backward)  23 us
  transfers between devices with their start and end apart: 67, of which 34 were waited for; matrix products, arithmetic and copies ran while one was open for 6% of the time, Pallas kernels for 44%

profile of v4, /device:TPU:0, one launch (start us, length us, event | category | flops | bytes accessed | tf_op | source)
XLA Modules:
  0.0 499.1 jit_solution(2766668823234885021)
XLA Ops:
  10.8 7.9 %collective-permute-done.refs_0_ = bf16[128,2048]{1,0:T(8,128)(2,1)S(1)} collective-permute-done((bf16[128,2048]{1,0:T(8,128)(2,1)S(1)}, bf16[128,2048]{1,0:T(8,128)(2,1)S(1)}, u32[]{:S(2)}, u32[]{:S(2)}) %collective-permute-start) | collective-permute-done | bytes 524320 | tf_op jit(solution)/shard_map/ppermute | solution.py:97
  22.4 10.4 %collective-permute-done.2.refs_2_ = bf16[128,2048]{1,0:T(8,128)(2,1)S(1)} collective-permute-done((bf16[128,2048]{1,0:T(8,128)(2,1)S(1)}, bf16[128,2048]{1,0:T(8,128)(2,1)S(1)}, u32[]{:S(2)}, u32[]{:S(2)}) %collective-permute-start.2) | collective-permute-done | bytes 524320 | tf_op jit(solution)/shard_map/ppermute | solution.py:97
  37.4 8.0 %collective-permute-done.4.refs_4_ = bf16[128,2048]{1,0:T(8,128)(2,1)S(1)} collective-permute-done((bf16[128,2048]{1,0:T(8,128)(2,1)S(1)}, bf16[128,2048]{1,0:T(8,128)(2,1)S(1)}, u32[]{:S(2)}, u32[]{:S(2)}) %collective-permute-start.4) | collective-permute-done | bytes 524320 | tf_op jit(solution)/shard_map/ppermute | solution.py:97
  58.6 10.0 %project.1 = (bf16[1024,256]{1,0:T(8,128)(2,1)S(1)}, bf16[1024,256]{1,0:T(8,128)(2,1)S(1)}, bf16[1024,256]{1,0:T(8,128)(2,1)}, bf16[1024,1024]{1,0:T(8,128)(2,1)...) custom-call(s32[8]{0:T(128)S(1)} %gather_fusion, s32[2]{0:T(128)S(1)} %pad_add_fusion.place, ...), custom_call_target="tpu_custom_call" | custom-call | flops 3000000000 | bytes 1 | tf_op jit(solution)/shard_map/project/pallas_call | solution.py:346
  104.2 11.6 %collective-permute-done.13 = bf16[256,2048]{1,0:T(8,128)(2,1)S(1)} collective-permute-done((bf16[256,2048]{1,0:T(8,128)(2,1)S(1)}, bf16[256,2048]{1,0:T(8,128)(2,1)S(1)}, u32[]{:S(2)}, u32[]{:S(2)}) %collective-permute-start.13) | collective-permute-done | bytes 1048608 | tf_op jit(solution)/shard_map/ppermute | solution.py:98
  128.7 8.1 %collective-permute-done.14 = bf16[192,2048]{1,0:T(8,128)(2,1)S(1)} collective-permute-done((bf16[192,2048]{1,0:T(8,128)(2,1)S(1)}, bf16[192,2048]{1,0:T(8,128)(2,1)S(1)}, u32[]{:S(2)}, u32[]{:S(2)}) %collective-permute-start.14) | collective-permute-done | bytes 786464 | tf_op jit(solution)/shard_map/ppermute | solution.py:97
  156.7 9.8 %collective-permute-done.18.refs_0_ = bf16[128,2176]{1,0:T(8,128)(2,1)S(1)} collective-permute-done((bf16[128,2176]{1,0:T(8,128)(2,1)S(1)}, bf16[128,2176]{1,0:T(8,128)(2,1)S(1)}, u32[]{:S(2)}, u32[]{:S(2)}) %collective-permute-start.18) | collective-permute-done | bytes 557088 | tf_op jit(solution)/shard_map/ppermute | solution.py:97
  170.2 11.1 %hidden_units.4 = (bf16[256,128]{1,0:T(8,128)(2,1)S(1)}, bf16[1024,1408]{1,0:T(8,128)(2,1)}, bf16[1024,768]{1,0:T(8,128)(2,1)}, bf16[1024,2816]{1,0:T(8,128)(2,1...) custom-call(s32[1]{0:T(128)} %bitcast.6.me_ref, ...), custom_call_target="tpu_custom_call" | custom-call | flops 6000000000 | bytes 1 | tf_op jit(solution)/shard_map/hidden_units/pallas_call | solution.py:771
  183.3 11.1 %hidden_units.5 = (bf16[256,128]{1,0:T(8,128)(2,1)S(1)}, bf16[1024,1408]{1,0:T(8,128)(2,1)}, bf16[1024,768]{1,0:T(8,128)(2,1)}, bf16[1024,2816]{1,0:T(8,128)(2,1...) custom-call(s32[1]{0:T(128)} %bitcast.6.me_ref, ...), custom_call_target="tpu_custom_call", output_to_operand_aliasing={{1}: (9, {}), {2}: (10, {}), {3}: (11, {}), {4}: (12, {}), ... | custom-call | flops 6000000000 | bytes 1 | tf_op jit(solution)/shard_map/hidden_units/pallas_call | solution.py:771
  196.6 11.1 %hidden_units.6 = (bf16[256,128]{1,0:T(8,128)(2,1)S(1)}, bf16[1024,1408]{1,0:T(8,128)(2,1)}, bf16[1024,768]{1,0:T(8,128)(2,1)}, bf16[1024,2816]{1,0:T(8,128)(2,1...) custom-call(s32[1]{0:T(128)} %bitcast.6.me_ref, ...), custom_call_target="tpu_custom_call", output_to_operand_aliasing={{1}: (9, {}), {2}: (10, {}), {3}: (11, {}), {4}: (12, {}), ... | custom-call | flops 6000000000 | bytes 1 | tf_op jit(solution)/shard_map/hidden_units/pallas_call | solution.py:771
  207.7 11.1 %hidden_units.7 = (bf16[256,128]{1,0:T(8,128)(2,1)S(1)}, bf16[1024,1408]{1,0:T(8,128)(2,1)}, bf16[1024,768]{1,0:T(8,128)(2,1)}, bf16[1024,2816]{1,0:T(8,128)(2,1...) custom-call(s32[1]{0:T(128)} %bitcast.6.me_ref, ...), custom_call_target="tpu_custom_call", output_to_operand_aliasing={{1}: (10, {}), {2}: (11, {}), {3}: (12, {}), {4}: (13, {}),... | custom-call | flops 6000000000 | bytes 1 | tf_op jit(solution)/shard_map/hidden_units/pallas_call | solution.py:771
  218.8 11.1 %pair_dot.15 = bf16[1024,2816]{1,0:T(8,128)(2,1)} custom-call(bf16[1024,1024]{1,0:T(8,128)(2,1)} %get-tuple-element.343.refs_0_, bf16[1024,2816]{1,0:T(8,128)(2,1)} %get-tuple-element.323.refs_1_.both_hbm), custom_call_target="tpu_custom_call" | custom-call | flops 1 | bytes 1 | tf_op jit(solution)/shard_map/pair_dot/pallas_call | solution.py:933
  230.1 8.4 %units_in.4 = bf16[256,2176]{1,0:T(8,128)(2,1)S(1)} custom-call(bf16[1024,2816]{1,0:T(8,128)(2,1)} %get-tuple-element.323.refs_1_.both_hbm, bf16[1024,1408]{1,0:T(8,128)(2,1)S(1)} %copy-done, bf16[256,128]{1,0:T(8,128)(2,1)S(1)} %get-tuple-element.310.small_ref, bf16[2048,2816]{1,0:T(8,128)(2,1)} %bitcast.40, bf16[704,2048]{1,0:T(8,128)(2,1)} %bitcast.48, ...), custom_call_target="tpu_custom_call" | custom-call | flops 70000001024 | bytes 1 | tf_op jit(solution)/shard_map/units_in/pallas_call | solution.py:844
  240.6 8.1 %units_in.5 = bf16[256,2176]{1,0:T(8,128)(2,1)S(1)} custom-call(bf16[1024,2816]{1,0:T(8,128)(2,1)} %get-tuple-element.323.refs_1_.both_hbm, bf16[1024,1408]{1,0:T(8,128)(2,1)S(1)} %copy-done, bf16[256,128]{1,0:T(8,128)(2,1)S(1)} %get-tuple-element.313.small_ref, bf16[2048,2816]{1,0:T(8,128)(2,1)} %bitcast.41, bf16[704,2048]{1,0:T(8,128)(2,1)} %bitcast.49, ...), custom_call_target="tpu_custom_call" | custom-call | flops 6000000000 | bytes 1 | tf_op jit(solution)/shard_map/units_in/pallas_call | solution.py:844
  259.9 8.1 %units_in.6 = bf16[256,2176]{1,0:T(8,128)(2,1)S(1)} custom-call(bf16[1024,2816]{1,0:T(8,128)(2,1)} %get-tuple-element.323.refs_1_.both_hbm, bf16[1024,1408]{1,0:T(8,128)(2,1)S(1)} %copy-done, bf16[256,128]{1,0:T(8,128)(2,1)S(1)} %get-tuple-element.280.small_ref, bf16[2048,2816]{1,0:T(8,128)(2,1)} %bitcast.42, bf16[704,2048]{1,0:T(8,128)(2,1)} %bitcast.50, ...), custom_call_target="tpu_custom_call" | custom-call | flops 1 | bytes 1 | tf_op jit(solution)/shard_map/units_in/pallas_call | solution.py:844
  270.3 8.2 %units_in.7 = bf16[256,2176]{1,0:T(8,128)(2,1)S(1)} custom-call(bf16[1024,2816]{1,0:T(8,128)(2,1)} %get-tuple-element.323.refs_1_.both_hbm, bf16[1024,1408]{1,0:T(8,128)(2,1)S(1)} %copy-done, bf16[256,128]{1,0:T(8,128)(2,1)S(1)} %get-tuple-element.268.small_ref, bf16[2048,2816]{1,0:T(8,128)(2,1)} %bitcast.43, bf16[704,2048]{1,0:T(8,128)(2,1)} %bitcast.51, ...), custom_call_target="tpu_custom_call" | custom-call | flops 12000000000 | bytes 1 | tf_op jit(solution)/shard_map/units_in/pallas_call | solution.py:844
  286.1 7.7 %layer_part.2 = bf16[512,2048]{1,0:T(8,128)(2,1)S(1)} custom-call(bf16[1024,1408]{1,0:T(8,128)(2,1)} %get-tuple-element.338.he_hbm.refs_1_, bf16[1024,768]{1,0:T(8,128)(2,1)S(1)} %copy-done.1, bf16[2048,1408]{1,0:T(8,128)(2,1)} %bitcast.69, bf16[704,2048]{1,0:T(8,128)(2,1)} %bitcast.75), custom_call_target="tpu_custom_call" | custom-call | flops 12000000000 | bytes 1 | tf_op jit(solution)/shard_map/layer_part/pallas_call | solution.py:979
  293.8 7.4 %pair_dot.18 = bf16[1024,1408]{1,0:T(8,128)(2,1)} custom-call(bf16[1024,1024]{1,0:T(8,128)(2,1)} %get-tuple-element.329.refs_0_, bf16[1024,1408]{1,0:T(8,128)(2,1)} %get-tuple-element.338.he_hbm.refs_1_), custom_call_target="tpu_custom_call" | custom-call | flops 1 | bytes 1 | tf_op jit(solution)/shard_map/pair_dot/pallas_call | solution.py:933
  306.5 7.6 %layer_part.3 = bf16[512,2048]{1,0:T(8,128)(2,1)S(1)} custom-call(bf16[1024,1408]{1,0:T(8,128)(2,1)} %get-tuple-element.338.he_hbm.refs_1_, bf16[1024,768]{1,0:T(8,128)(2,1)S(1)} %copy-done.1, bf16[2048,1408]{1,0:T(8,128)(2,1)} %bitcast.70, bf16[704,2048]{1,0:T(8,128)(2,1)} %bitcast.76), custom_call_target="tpu_custom_call" | custom-call | flops 35000000512 | bytes 1 | tf_op jit(solution)/shard_map/layer_part/pallas_call | solution.py:979
  336.6 7.3 %pair_dot.22 = f32[512,2816]{1,0:T(8,128)} custom-call(bf16[1024,512]{1,0:T(8,128)(2,1)S(1)} %copy-done.5, bf16[1024,2816]{1,0:T(8,128)(2,1)} %get-tuple-element.323.refs_1_.both_hbm, bf16[1024,2816]{1,0:T(8,128)(2,1)} %collective-permute-done.28.refs_2_, bf16[512,2816]{1,0:T(8,128)(2,1)} %collective-permute-done.43.refs_3_), custom_call_target="tpu_custom_call" | custom-call | flops 7500000256 | bytes 1 | tf_op jit(solution)/shard_map/pair_dot/pallas_call | solution.py:933
  363.6 7.7 %attend_back.1 = (bf16[1024,768]{1,0:T(8,128)(2,1)S(1)}, f32[1,768]{1,0:T(1,128)S(1)}) custom-call(s32[8]{0:T(128)S(1)} %copy-done.46, bf16[1024,256]{1,0:T(8,128)(2,1)S(1)} %copy-done.49, bf16[1024,256]{1,0:T(8,128)(2,1)S(1)} %copy-done.51, bf16[1024,256]{1,0:T(8,128)(2,1)S(1)} %copy-done.53, bf16[1024,256]{1,0:T(8,128)(2,1)S(1)} %get-tuple-element.360.g_hbm, ...), custom_call_target="tpu_custom_call" | custom-call | flops 20000000000 | bytes 1 | tf_op jit(solution)/shard_map/attend_back/pallas_call | solution.py:481
  411.3 7.2 %collective-permute-done.54.refs_3_ = bf16[512,768]{1,0:T(8,128)(2,1)} collective-permute-done((bf16[512,768]{1,0:T(8,128)(2,1)S(1)}, bf16[512,768]{1,0:T(8,128)(2,1)}, u32[]{:S(2)}, u32[]{:S(2)}) %collective-permute-start.54) | collective-permute-done | bytes 786464 | tf_op jit(solution)/shard_map/ppermute | solution.py:216
  437.0 11.3 %collective-permute-done.55 = bf16[256,2048]{1,0:T(8,128)(2,1)} collective-permute-done((bf16[256,2048]{1,0:T(8,128)(2,1)}, bf16[256,2048]{1,0:T(8,128)(2,1)}, u32[]{:S(2)}, u32[]{:S(2)}) %collective-permute-start.55) | collective-permute-done | bytes 1048608 | tf_op jit(solution)/shard_map/ppermute | solution.py:97
  460.5 9.5 %collective-permute-done.66.refs_3_ = bf16[512,1408]{1,0:T(8,128)(2,1)} collective-permute-done((bf16[512,1408]{1,0:T(8,128)(2,1)}, bf16[512,1408]{1,0:T(8,128)(2,1)}, u32[]{:S(2)}, u32[]{:S(2)}) %collective-permute-start.66) | collective-permute-done | bytes 1441824 | tf_op jit(solution)/shard_map/ppermute | solution.py:216
  (407 shorter events, 276.3 us)
Async XLA Ops:
  56.4 18.5 %collective-permute-start.8 = (bf16[128,2048]{1,0:T(8,128)(2,1)S(1)}, bf16[128,2048]{1,0:T(8,128)(2,1)S(1)}, u32[]{:S(2)}, u32[]{:S(2)}) collective-permute-start(bf16[128,2048]{1,0:T(8,128)(2,1)S(1)} %copy-done.31), channel_id=1, source_target_pairs={{0,2},{2,4},{4,6},{6,7},{7,5},{5,3},{3,1},{1,0},{8,10},{10,12},{12... | collective-permute-start | bytes 1572872 | tf_op jit(solution)/shard_map/ppermute | solution.py:97
  57.3 17.6 %collective-permute-start.9 = (bf16[128,2048]{1,0:T(8,128)(2,1)S(1)}, bf16[128,2048]{1,0:T(8,128)(2,1)S(1)}, u32[]{:S(2)}, u32[]{:S(2)}) collective-permute-start(bf16[128,2048]{1,0:T(8,128)(2,1)S(1)} %copy-done.31), channel_id=1, source_target_pairs={{0,1},{2,0},{4,2},{6,4},{7,6},{5,7},{3,5},{1,3},{8,9},{10,8},{12,1... | collective-permute-start | bytes 1572872 | tf_op jit(solution)/shard_map/ppermute | solution.py:98
  95.2 20.6 %collective-permute-start.13 = (bf16[256,2048]{1,0:T(8,128)(2,1)S(1)}, bf16[256,2048]{1,0:T(8,128)(2,1)S(1)}, u32[]{:S(2)}, u32[]{:S(2)}) collective-permute-start(bf16[256,2048]{1,0:T(8,128)(2,1)S(1)} %pad_maximum_fusion.1), channel_id=1, source_target_pairs={{0,1},{2,0},{4,2},{6,4},{7,6},{5,7},{3,5},{1,3},{8,9},{10,8},{12,1... | collective-permute-start | bytes 3145736 | tf_op jit(solution)/shard_map/ppermute | solution.py:98
  95.9 21.5 %collective-permute-start.12 = (bf16[256,2048]{1,0:T(8,128)(2,1)S(1)}, bf16[256,2048]{1,0:T(8,128)(2,1)S(1)}, u32[]{:S(2)}, u32[]{:S(2)}) collective-permute-start(bf16[256,2048]{1,0:T(8,128)(2,1)S(1)} %pad_maximum_fusion), channel_id=1, source_target_pairs={{0,2},{2,4},{4,6},{6,7},{7,5},{5,3},{3,1},{1,0},{8,10},{10,12},{12... | collective-permute-start | bytes 3145736 | tf_op jit(solution)/shard_map/ppermute | solution.py:97
  119.2 17.6 %collective-permute-start.14 = (bf16[192,2048]{1,0:T(8,128)(2,1)S(1)}, bf16[192,2048]{1,0:T(8,128)(2,1)S(1)}, u32[]{:S(2)}, u32[]{:S(2)}) collective-permute-start(bf16[192,2048]{1,0:T(8,128)(2,1)S(1)} %pad_maximum_fusion.8), channel_id=1, source_target_pairs={{0,2},{2,4},{4,6},{6,7},{7,5},{5,3},{3,1},{1,0},{8,10},{10,12},{12... | collective-permute-start | bytes 2359304 | tf_op jit(solution)/shard_map/ppermute | solution.py:97
  121.3 17.6 %collective-permute-start.15 = (bf16[192,2048]{1,0:T(8,128)(2,1)S(1)}, bf16[192,2048]{1,0:T(8,128)(2,1)S(1)}, u32[]{:S(2)}, u32[]{:S(2)}) collective-permute-start(bf16[192,2048]{1,0:T(8,128)(2,1)S(1)} %pad_maximum_fusion.9), channel_id=1, source_target_pairs={{0,1},{2,0},{4,2},{6,4},{7,6},{5,7},{3,5},{1,3},{8,9},{10,8},{12,1... | collective-permute-start | bytes 2359304 | tf_op jit(solution)/shard_map/ppermute | solution.py:98
  230.0 21.2 %collective-permute-start.28 = (bf16[1024,2816]{1,0:T(8,128)(2,1)}, bf16[1024,2816]{1,0:T(8,128)(2,1)}, u32[]{:S(2)}, u32[]{:S(2)}) collective-permute-start(bf16[1024,2816]{1,0:T(8,128)(2,1)} %pair_dot.15), channel_id=1, source_target_pairs={{0,8},{8,0},{16,24},{24,16},{1,9},{9,1},{17,25},{25,17},{2,10},{10... | collective-permute-start | bytes 17301512 | tf_op jit(solution)/shard_map/ppermute | solution.py:204
  249.1 18.9 %collective-permute-start.29 = (bf16[128,2176]{1,0:T(8,128)(2,1)S(1)}, bf16[128,2176]{1,0:T(8,128)(2,1)S(1)}, u32[]{:S(2)}, u32[]{:S(2)}) collective-permute-start(bf16[128,2176]{1,0:T(8,128)(2,1)S(1)} %pad_maximum_fusion.12), channel_id=1, source_target_pairs={{0,2},{2,4},{4,6},{6,7},{7,5},{5,3},{3,1},{1,0},{8,10},{10,12},{12... | collective-permute-start | bytes 1671176 | tf_op jit(solution)/shard_map/ppermute | solution.py:97
  250.3 17.6 %collective-permute-start.30 = (bf16[128,2176]{1,0:T(8,128)(2,1)S(1)}, bf16[128,2176]{1,0:T(8,128)(2,1)S(1)}, u32[]{:S(2)}, u32[]{:S(2)}) collective-permute-start(bf16[128,2176]{1,0:T(8,128)(2,1)S(1)} %pad_maximum_fusion.13), channel_id=1, source_target_pairs={{0,1},{2,0},{4,2},{6,4},{7,6},{5,7},{3,5},{1,3},{8,9},{10,8},{12,1... | collective-permute-start | bytes 1671176 | tf_op jit(solution)/shard_map/ppermute | solution.py:98
  258.3 78.3 %collective-permute-start.43 = (bf16[512,2816]{1,0:T(8,128)(2,1)}, bf16[512,2816]{1,0:T(8,128)(2,1)}, u32[]{:S(2)}, u32[]{:S(2)}) collective-permute-start(bf16[512,2816]{1,0:T(8,128)(2,1)} %pair_dot.16), channel_id=1, source_target_pairs={{0,16},{8,24},{16,0},{24,8},{1,17},{9,25},{17,1},{25,9},{2,18},{10... | collective-permute-start | bytes 8650760 | tf_op jit(solution)/shard_map/ppermute | solution.py:216
  283.6 45.3 %collective-permute-start.40 = (bf16[1024,768]{1,0:T(8,128)(2,1)S(1)}, bf16[1024,768]{1,0:T(8,128)(2,1)}, u32[]{:S(2)}, u32[]{:S(2)}) collective-permute-start(bf16[1024,768]{1,0:T(8,128)(2,1)S(1)} %pair_dot.17), channel_id=1, source_target_pairs={{0,8},{8,0},{16,24},{24,16},{1,9},{9,1},{17,25},{25,17},{2,10},{10... | collective-permute-start | bytes 4718600 | tf_op jit(solution)/shard_map/ppermute | solution.py:204
  284.0 17.3 %collective-permute-start.33 = (bf16[128,2176]{1,0:T(8,128)(2,1)S(1)}, bf16[128,2176]{1,0:T(8,128)(2,1)S(1)}, u32[]{:S(2)}, u32[]{:S(2)}) collective-permute-start(bf16[128,2176]{1,0:T(8,128)(2,1)S(1)} %get-tuple-element.331), channel_id=1, source_target_pairs={{0,2},{2,4},{4,6},{6,7},{7,5},{5,3},{3,1},{1,0},{8,10},{10,12},{12... | collective-permute-start | bytes 1671176 | tf_op jit(solution)/shard_map/ppermute | solution.py:97
  350.5 32.6 %collective-permute-start.50 = (bf16[512,1408]{1,0:T(8,128)(2,1)}, bf16[512,1408]{1,0:T(8,128)(2,1)}, u32[]{:S(2)}, u32[]{:S(2)}) collective-permute-start(bf16[512,1408]{1,0:T(8,128)(2,1)} %pair_dot.19), channel_id=1, source_target_pairs={{0,16},{8,24},{16,0},{24,8},{1,17},{9,25},{17,1},{25,9},{2,18},{10... | collective-permute-start | bytes 4325384 | tf_op jit(solution)/shard_map/ppermute | solution.py:216
  351.0 55.5 %collective-permute-start.53 = (bf16[1024,1408]{1,0:T(8,128)(2,1)}, bf16[1024,1408]{1,0:T(8,128)(2,1)}, u32[]{:S(2)}, u32[]{:S(2)}) collective-permute-start(bf16[1024,1408]{1,0:T(8,128)(2,1)} %pair_dot.20), channel_id=1, source_target_pairs={{0,8},{8,0},{16,24},{24,16},{1,9},{9,1},{17,25},{25,17},{2,10},{10... | collective-permute-start | bytes 8650760 | tf_op jit(solution)/shard_map/ppermute | solution.py:204
  354.4 16.9 %collective-permute-start.46 = (bf16[64,2048]{1,0:T(8,128)(2,1)}, bf16[64,2048]{1,0:T(8,128)(2,1)}, u32[]{:S(2)}, u32[]{:S(2)}) collective-permute-start(bf16[64,2048]{1,0:T(8,128)(2,1)} %get-tuple-element.362), channel_id=1, source_target_pairs={{0,2},{2,4},{4,6},{6,7},{7,5},{5,3},{3,1},{1,0},{8,10},{10,12},{12... | collective-permute-start | bytes 786440 | tf_op jit(solution)/shard_map/ppermute | solution.py:97
  401.2 22.0 %collective-permute-start.51 = (bf16[256,2048]{1,0:T(8,128)(2,1)}, bf16[256,2048]{1,0:T(8,128)(2,1)}, u32[]{:S(2)}, u32[]{:S(2)}) collective-permute-start(bf16[256,2048]{1,0:T(8,128)(2,1)} %pad_maximum_fusion.2), channel_id=1, source_target_pairs={{0,2},{2,4},{4,6},{6,7},{7,5},{5,3},{3,1},{1,0},{8,10},{10,12},{12... | collective-permute-start | bytes 3145736 | tf_op jit(solution)/shard_map/ppermute | solution.py:97
  401.6 21.6 %collective-permute-start.52 = (bf16[256,2048]{1,0:T(8,128)(2,1)}, bf16[256,2048]{1,0:T(8,128)(2,1)}, u32[]{:S(2)}, u32[]{:S(2)}) collective-permute-start(bf16[256,2048]{1,0:T(8,128)(2,1)} %pad_maximum_fusion.3), channel_id=1, source_target_pairs={{0,1},{2,0},{4,2},{6,4},{7,6},{5,7},{3,5},{1,3},{8,9},{10,8},{12,1... | collective-permute-start | bytes 3145736 | tf_op jit(solution)/shard_map/ppermute | solution.py:98
  406.4 47.6 %collective-permute-start.64 = (bf16[1024,1024]{1,0:T(8,128)(2,1)}, bf16[1024,1024]{1,0:T(8,128)(2,1)}, u32[]{:S(2)}, u32[]{:S(2)}) collective-permute-start(bf16[1024,1024]{1,0:T(8,128)(2,1)} %pair_dot.24), channel_id=1, source_target_pairs={{0,8},{8,0},{16,24},{24,16},{1,9},{9,1},{17,25},{25,17},{2,10},{10... | collective-permute-start | bytes 6291464 | tf_op jit(solution)/shard_map/ppermute | solution.py:204
  428.0 20.2 %collective-permute-start.55 = (bf16[256,2048]{1,0:T(8,128)(2,1)}, bf16[256,2048]{1,0:T(8,128)(2,1)}, u32[]{:S(2)}, u32[]{:S(2)}) collective-permute-start(bf16[256,2048]{1,0:T(8,128)(2,1)} %pad_maximum_fusion.4), channel_id=1, source_target_pairs={{0,2},{2,4},{4,6},{6,7},{7,5},{5,3},{3,1},{1,0},{8,10},{10,12},{12... | collective-permute-start | bytes 3145736 | tf_op jit(solution)/shard_map/ppermute | solution.py:97
  428.5 20.2 %collective-permute-start.56 = (bf16[256,2048]{1,0:T(8,128)(2,1)}, bf16[256,2048]{1,0:T(8,128)(2,1)}, u32[]{:S(2)}, u32[]{:S(2)}) collective-permute-start(bf16[256,2048]{1,0:T(8,128)(2,1)} %pad_maximum_fusion.5), channel_id=1, source_target_pairs={{0,1},{2,0},{4,2},{6,4},{7,6},{5,7},{3,5},{1,3},{8,9},{10,8},{12,1... | collective-permute-start | bytes 3145736 | tf_op jit(solution)/shard_map/ppermute | solution.py:98
  435.2 34.8 %collective-permute-start.66 = (bf16[512,1408]{1,0:T(8,128)(2,1)}, bf16[512,1408]{1,0:T(8,128)(2,1)}, u32[]{:S(2)}, u32[]{:S(2)}) collective-permute-start(bf16[512,1408]{1,0:T(8,128)(2,1)} %pair_dot.25), channel_id=1, source_target_pairs={{0,16},{8,24},{16,0},{24,8},{1,17},{9,25},{17,1},{25,9},{2,18},{10... | collective-permute-start | bytes 4325384 | tf_op jit(solution)/shard_map/ppermute | solution.py:216
  452.0 23.6 %collective-permute-start.57 = (bf16[128,2048]{1,0:T(8,128)(2,1)S(1)}, bf16[128,2048]{1,0:T(8,128)(2,1)S(1)}, u32[]{:S(2)}, u32[]{:S(2)}) collective-permute-start(bf16[128,2048]{1,0:T(8,128)(2,1)S(1)} %get-tuple-element.382), channel_id=1, source_target_pairs={{0,2},{2,4},{4,6},{6,7},{7,5},{5,3},{3,1},{1,0},{8,10},{10,12},{12... | collective-permute-start | bytes 1572872 | tf_op jit(solution)/shard_map/ppermute | solution.py:97
  452.3 23.3 %collective-permute-start.58 = (bf16[128,2048]{1,0:T(8,128)(2,1)S(1)}, bf16[128,2048]{1,0:T(8,128)(2,1)S(1)}, u32[]{:S(2)}, u32[]{:S(2)}) collective-permute-start(bf16[128,2048]{1,0:T(8,128)(2,1)S(1)} %get-tuple-element.383), channel_id=1, source_target_pairs={{0,1},{2,0},{4,2},{6,4},{7,6},{5,7},{3,5},{1,3},{8,9},{10,8},{12,1... | collective-permute-start | bytes 1572872 | tf_op jit(solution)/shard_map/ppermute | solution.py:98
  458.2 33.0 %collective-permute-start.65 = (bf16[512,1024]{1,0:T(8,128)(2,1)S(1)}, bf16[512,1024]{1,0:T(8,128)(2,1)S(1)}, u32[]{:S(2)}, u32[]{:S(2)}) collective-permute-start(bf16[512,1024]{1,0:T(8,128)(2,1)S(1)} %pair_dot.27), channel_id=1, source_target_pairs={{0,16},{8,24},{16,0},{24,8},{1,17},{9,25},{17,1},{25,9},{2,18},{10... | collective-permute-start | bytes 3145736 | tf_op jit(solution)/shard_map/ppermute | solution.py:216
  (128 other events, 2035.9 us)
